TPU v7x, 128 devices: a whole 4x4x4 slice. The times are simulated.
128 devices in a mesh: facet: 16 (over z, x_hi, core), vis: 8 (over x_lo, y).
Axes of the slice: x: 4 (x_hi: 2, x_lo: 2; x = x_hi * 2 + x_lo), y: 4, z: 4, core: 2. Of those that a mesh axis runs over, the one named last changes fastest.
Arguments:
- sky_image: float32 [4096, 4096], P('facet', 'vis'), may hold values from -6 to 6
- observed: bfloat16 [128, 256, 256], P(('facet', 'vis')), may hold values from -6 to 6
- offsets: int32 [128, 2], replicated, may hold values from 0 to 4095
- assignments: int32 [128, 8], replicated, may hold values from 0 to 15, all different within a row
Outputs:
- residual_blocks: bfloat16 [128, 256, 256], P(('facet', 'vis'))
- residual_image: float32 [4096, 4096], P('facet', 'vis')
Inputs may be any that keep to these rules, and one draw needn't show every extreme that they name: `assignments`: each subgrid names 8 different facets, and every facet is named by some subgrid.
All inputs are finite; a program needn't handle non-finite values.
Results may differ from a plain program's by a relative error of at most 0.017.
Values may be sent and summed in bfloat16 or wider, within the bound.
No kernel may reach another device: no remote copies, remote signals or barrier semaphores. Data moves between devices by JAX's collectives and lax.ppermute only.
A program may use at most 64 MiB of HBM per device.

v0:
```python
import jax
import jax.numpy as jnp
from jax import lax
from jax.sharding import PartitionSpec as P


def cas_table(freqs, places, period, factor):
    phase = freqs[:, None] % period * places[None, :] % period
    angle = phase.astype(jnp.float32) * (2.0 * jnp.pi / period)
    return ((jnp.cos(angle) + jnp.sin(angle)) * factor).astype(jnp.bfloat16)


def on_device(sky_image, observed, offsets, assignments):
    n_facet = lax.axis_size("facet")
    n_vis = lax.axis_size("vis")
    facet_idx = lax.axis_index("facet")
    vis_idx = lax.axis_index("vis")
    face_rows = sky_image.shape[0]
    own_cols = sky_image.shape[1]
    width_cols = own_cols * n_vis
    sub_side = observed.shape[1]
    all_rows = face_rows * n_facet
    row_place = facet_idx * face_rows + jnp.arange(face_rows, dtype=jnp.int32)
    col_place = jnp.arange(width_cols, dtype=jnp.int32)
    sub_ids = jnp.arange(sub_side, dtype=jnp.int32)
    model_image = lax.all_gather(sky_image.astype(jnp.bfloat16), "vis", axis=1, tiled=True)

    def single(item_no):
        sub_index = item_no * n_vis + vis_idx
        col_pred = cas_table(
            offsets[sub_index, 0] + sub_ids, col_place, width_cols, width_cols ** (-0.5)
        )
        inner = lax.dot_general(
            model_image, col_pred, (((1,), (1,)), ((), ())), preferred_element_type=jnp.float32
        ).astype(jnp.bfloat16)
        row_pred = cas_table(
            offsets[sub_index, 1] + sub_ids, row_place, all_rows, all_rows ** (-0.5)
        )
        return jnp.dot(row_pred, inner, preferred_element_type=jnp.float32)

    predicted = lax.psum_scatter(
        lax.map(single, jnp.arange(1 * lax.axis_size("facet"), dtype=jnp.int32)),
        "facet",
        scatter_dimension=0,
        tiled=True,
    )
    own_index = facet_idx * n_vis + vis_idx
    resid = (observed.astype(jnp.float32) - predicted).astype(jnp.bfloat16)
    targets = jnp.any(
        assignments[own_index][:, None] == jnp.arange(n_facet, dtype=jnp.int32)[None, :], axis=0
    )
    outgoing = jnp.where(targets[:, None, None], resid, jnp.zeros_like(resid))
    incoming = lax.all_to_all(outgoing, "facet", split_axis=0, concat_axis=0, tiled=True)

    def is_named(sub_index):
        return jnp.any(assignments[sub_index] == facet_idx)

    def left_rows(source):
        sub_index = source * n_vis + vis_idx
        row_grid = cas_table(
            offsets[sub_index, 1] + sub_ids, row_place, all_rows, sub_side ** (-0.5)
        )
        return lax.dot_general(
            row_grid, incoming[source], (((0,), (0,)), ((), ())), preferred_element_type=jnp.float32
        ).astype(jnp.bfloat16)

    def add_slot(source, total):
        sub_index = source * n_vis + vis_idx

        def add_term(acc):
            col_grid = cas_table(
                offsets[sub_index, 0] + sub_ids, col_place, width_cols, sub_side ** (-0.5)
            )
            return acc + jnp.dot(left_rows(source), col_grid, preferred_element_type=jnp.float32)

        return lax.cond(is_named(sub_index), add_term, lambda acc: acc, total)

    partial_image = lax.fori_loop(
        0, n_facet, add_slot, jnp.zeros((face_rows, width_cols), jnp.float32)
    )
    image_out = lax.psum_scatter(
        partial_image.astype(jnp.bfloat16), "vis", scatter_dimension=1, tiled=True
    ).astype(jnp.float32)
    return (resid, image_out)


def solution(mesh):
    placed = (P("facet", "vis"), P(("facet", "vis"), None, None), P(), P())
    return jax.shard_map(
        on_device,
        mesh=mesh,
        in_specs=placed,
        out_specs=(P(("facet", "vis"), None, None), P("facet", "vis")),
        check_vma=False,
    )
```

profile of v0, /device:TPU:0, one launch (start us, length us, event | category | flops | bytes accessed | tf_op | source)
XLA Modules:
  0.0 1022.9 jit_solution(9525444430633359371)
XLA Ops:
  7.2 1.8 convert_element_type.69
  9.1 45.3 %all-gather.2.cloned.1.call-done = bf16[256,4096]{1,0:T(8,128)(2,1)} async-done(((bf16[256,512]{1,0:T(8,128)(2,1)}), bf16[256,4096]{1,0:T(8,128)(2,1)}) %all-gather.2.cloned.1.call-update) | async-done | bytes 2097168 | tf_op jit(solution)/shard_map/all_gather | solution.py:26
  54.4 399.5 %while.32 = (s32[]{:T(128)}, f32[16,256,256]{2,1,0:T(8,128)}, s32[16]{0:T(128)S(1)}, s32[]{:T(128)}, s32[128,2]{0,1:T(2,128)}, /*index=5*/bf16[256,4096]{1,0:T(8...) while((s32[]{:T(128)}, f32[16,256,256]{2,1,0:T(8,128)}, ...), condition=%wide.region_1.2_spmd.clone.clone, body=%wide.region_0.1_spmd.clone.clone.sunk | while | flops 589437184 | bytes 2628307 | solution.py:42
  55.7 1.4 constant_dynamic-slice_fusion.5
  59.7 19.7 %fusion.112 = f32[16,256,256]{2,1,0:T(8,128)} fusion(f32[16,256,256]{2,1,0:T(8,128)} %get-tuple-element.569, s32[]{:T(128)} %get-tuple-element.568, bf16[256,4096]{1,0:T(8,128)(2,1)} %get-tuple-element.584, s32[256]{0:T(256)S(1)} %get-tuple-element.547, bf16[256,256]{1,0:T(8,128)(2,1)S(1)} %multiply_convert_fusion.30), kind=kOutput, calls=%fused_computation.77.clone.3 | convolution fusion | flops 588316672 | bytes 2491904 | tf_op jit(solution)/shard_map/while/body/eval_jaxpr/dot_general | solution.py:39
  80.6 1.4 constant_dynamic-slice_fusion.5
  84.6 19.7 %fusion.112 = f32[16,256,256]{2,1,0:T(8,128)} fusion(f32[16,256,256]{2,1,0:T(8,128)} %get-tuple-element.569, s32[]{:T(128)} %get-tuple-element.568, bf16[256,4096]{1,0:T(8,128)(2,1)} %get-tuple-element.584, s32[256]{0:T(256)S(1)} %get-tuple-element.547, bf16[256,256]{1,0:T(8,128)(2,1)S(1)} %multiply_convert_fusion.30), kind=kOutput, calls=%fused_computation.77.clone.3 | convolution fusion | flops 588316672 | bytes 2491904 | tf_op jit(solution)/shard_map/while/body/eval_jaxpr/dot_general | solution.py:39
  105.6 1.4 constant_dynamic-slice_fusion.5
  109.6 19.7 %fusion.112 = f32[16,256,256]{2,1,0:T(8,128)} fusion(f32[16,256,256]{2,1,0:T(8,128)} %get-tuple-element.569, s32[]{:T(128)} %get-tuple-element.568, bf16[256,4096]{1,0:T(8,128)(2,1)} %get-tuple-element.584, s32[256]{0:T(256)S(1)} %get-tuple-element.547, bf16[256,256]{1,0:T(8,128)(2,1)S(1)} %multiply_convert_fusion.30), kind=kOutput, calls=%fused_computation.77.clone.3 | convolution fusion | flops 588316672 | bytes 2491904 | tf_op jit(solution)/shard_map/while/body/eval_jaxpr/dot_general | solution.py:39
  130.6 1.4 constant_dynamic-slice_fusion.5
  134.6 19.7 %fusion.112 = f32[16,256,256]{2,1,0:T(8,128)} fusion(f32[16,256,256]{2,1,0:T(8,128)} %get-tuple-element.569, s32[]{:T(128)} %get-tuple-element.568, bf16[256,4096]{1,0:T(8,128)(2,1)} %get-tuple-element.584, s32[256]{0:T(256)S(1)} %get-tuple-element.547, bf16[256,256]{1,0:T(8,128)(2,1)S(1)} %multiply_convert_fusion.30), kind=kOutput, calls=%fused_computation.77.clone.3 | convolution fusion | flops 588316672 | bytes 2491904 | tf_op jit(solution)/shard_map/while/body/eval_jaxpr/dot_general | solution.py:39
  155.6 1.4 constant_dynamic-slice_fusion.5
  159.6 19.7 %fusion.112 = f32[16,256,256]{2,1,0:T(8,128)} fusion(f32[16,256,256]{2,1,0:T(8,128)} %get-tuple-element.569, s32[]{:T(128)} %get-tuple-element.568, bf16[256,4096]{1,0:T(8,128)(2,1)} %get-tuple-element.584, s32[256]{0:T(256)S(1)} %get-tuple-element.547, bf16[256,256]{1,0:T(8,128)(2,1)S(1)} %multiply_convert_fusion.30), kind=kOutput, calls=%fused_computation.77.clone.3 | convolution fusion | flops 588316672 | bytes 2491904 | tf_op jit(solution)/shard_map/while/body/eval_jaxpr/dot_general | solution.py:39
  180.5 1.4 constant_dynamic-slice_fusion.5
  184.5 19.7 %fusion.112 = f32[16,256,256]{2,1,0:T(8,128)} fusion(f32[16,256,256]{2,1,0:T(8,128)} %get-tuple-element.569, s32[]{:T(128)} %get-tuple-element.568, bf16[256,4096]{1,0:T(8,128)(2,1)} %get-tuple-element.584, s32[256]{0:T(256)S(1)} %get-tuple-element.547, bf16[256,256]{1,0:T(8,128)(2,1)S(1)} %multiply_convert_fusion.30), kind=kOutput, calls=%fused_computation.77.clone.3 | convolution fusion | flops 588316672 | bytes 2491904 | tf_op jit(solution)/shard_map/while/body/eval_jaxpr/dot_general | solution.py:39
  205.5 1.4 constant_dynamic-slice_fusion.5
  209.5 19.7 %fusion.112 = f32[16,256,256]{2,1,0:T(8,128)} fusion(f32[16,256,256]{2,1,0:T(8,128)} %get-tuple-element.569, s32[]{:T(128)} %get-tuple-element.568, bf16[256,4096]{1,0:T(8,128)(2,1)} %get-tuple-element.584, s32[256]{0:T(256)S(1)} %get-tuple-element.547, bf16[256,256]{1,0:T(8,128)(2,1)S(1)} %multiply_convert_fusion.30), kind=kOutput, calls=%fused_computation.77.clone.3 | convolution fusion | flops 588316672 | bytes 2491904 | tf_op jit(solution)/shard_map/while/body/eval_jaxpr/dot_general | solution.py:39
  230.5 1.4 constant_dynamic-slice_fusion.5
  234.5 19.7 %fusion.112 = f32[16,256,256]{2,1,0:T(8,128)} fusion(f32[16,256,256]{2,1,0:T(8,128)} %get-tuple-element.569, s32[]{:T(128)} %get-tuple-element.568, bf16[256,4096]{1,0:T(8,128)(2,1)} %get-tuple-element.584, s32[256]{0:T(256)S(1)} %get-tuple-element.547, bf16[256,256]{1,0:T(8,128)(2,1)S(1)} %multiply_convert_fusion.30), kind=kOutput, calls=%fused_computation.77.clone.3 | convolution fusion | flops 588316672 | bytes 2491904 | tf_op jit(solution)/shard_map/while/body/eval_jaxpr/dot_general | solution.py:39
  255.4 1.4 constant_dynamic-slice_fusion.5
  259.4 19.7 %fusion.112 = f32[16,256,256]{2,1,0:T(8,128)} fusion(f32[16,256,256]{2,1,0:T(8,128)} %get-tuple-element.569, s32[]{:T(128)} %get-tuple-element.568, bf16[256,4096]{1,0:T(8,128)(2,1)} %get-tuple-element.584, s32[256]{0:T(256)S(1)} %get-tuple-element.547, bf16[256,256]{1,0:T(8,128)(2,1)S(1)} %multiply_convert_fusion.30), kind=kOutput, calls=%fused_computation.77.clone.3 | convolution fusion | flops 588316672 | bytes 2491904 | tf_op jit(solution)/shard_map/while/body/eval_jaxpr/dot_general | solution.py:39
  280.4 1.4 constant_dynamic-slice_fusion.5
  284.4 19.7 %fusion.112 = f32[16,256,256]{2,1,0:T(8,128)} fusion(f32[16,256,256]{2,1,0:T(8,128)} %get-tuple-element.569, s32[]{:T(128)} %get-tuple-element.568, bf16[256,4096]{1,0:T(8,128)(2,1)} %get-tuple-element.584, s32[256]{0:T(256)S(1)} %get-tuple-element.547, bf16[256,256]{1,0:T(8,128)(2,1)S(1)} %multiply_convert_fusion.30), kind=kOutput, calls=%fused_computation.77.clone.3 | convolution fusion | flops 588316672 | bytes 2491904 | tf_op jit(solution)/shard_map/while/body/eval_jaxpr/dot_general | solution.py:39
  305.4 1.4 constant_dynamic-slice_fusion.5
  309.4 19.7 %fusion.112 = f32[16,256,256]{2,1,0:T(8,128)} fusion(f32[16,256,256]{2,1,0:T(8,128)} %get-tuple-element.569, s32[]{:T(128)} %get-tuple-element.568, bf16[256,4096]{1,0:T(8,128)(2,1)} %get-tuple-element.584, s32[256]{0:T(256)S(1)} %get-tuple-element.547, bf16[256,256]{1,0:T(8,128)(2,1)S(1)} %multiply_convert_fusion.30), kind=kOutput, calls=%fused_computation.77.clone.3 | convolution fusion | flops 588316672 | bytes 2491904 | tf_op jit(solution)/shard_map/while/body/eval_jaxpr/dot_general | solution.py:39
  330.3 1.4 constant_dynamic-slice_fusion.5
  334.3 19.7 %fusion.112 = f32[16,256,256]{2,1,0:T(8,128)} fusion(f32[16,256,256]{2,1,0:T(8,128)} %get-tuple-element.569, s32[]{:T(128)} %get-tuple-element.568, bf16[256,4096]{1,0:T(8,128)(2,1)} %get-tuple-element.584, s32[256]{0:T(256)S(1)} %get-tuple-element.547, bf16[256,256]{1,0:T(8,128)(2,1)S(1)} %multiply_convert_fusion.30), kind=kOutput, calls=%fused_computation.77.clone.3 | convolution fusion | flops 588316672 | bytes 2491904 | tf_op jit(solution)/shard_map/while/body/eval_jaxpr/dot_general | solution.py:39
  355.3 1.4 constant_dynamic-slice_fusion.5
  359.3 19.7 %fusion.112 = f32[16,256,256]{2,1,0:T(8,128)} fusion(f32[16,256,256]{2,1,0:T(8,128)} %get-tuple-element.569, s32[]{:T(128)} %get-tuple-element.568, bf16[256,4096]{1,0:T(8,128)(2,1)} %get-tuple-element.584, s32[256]{0:T(256)S(1)} %get-tuple-element.547, bf16[256,256]{1,0:T(8,128)(2,1)S(1)} %multiply_convert_fusion.30), kind=kOutput, calls=%fused_computation.77.clone.3 | convolution fusion | flops 588316672 | bytes 2491904 | tf_op jit(solution)/shard_map/while/body/eval_jaxpr/dot_general | solution.py:39
  380.3 1.4 constant_dynamic-slice_fusion.5
  384.3 19.7 %fusion.112 = f32[16,256,256]{2,1,0:T(8,128)} fusion(f32[16,256,256]{2,1,0:T(8,128)} %get-tuple-element.569, s32[]{:T(128)} %get-tuple-element.568, bf16[256,4096]{1,0:T(8,128)(2,1)} %get-tuple-element.584, s32[256]{0:T(256)S(1)} %get-tuple-element.547, bf16[256,256]{1,0:T(8,128)(2,1)S(1)} %multiply_convert_fusion.30), kind=kOutput, calls=%fused_computation.77.clone.3 | convolution fusion | flops 588316672 | bytes 2491904 | tf_op jit(solution)/shard_map/while/body/eval_jaxpr/dot_general | solution.py:39
  405.3 1.4 constant_dynamic-slice_fusion.5
  409.3 19.7 %fusion.112 = f32[16,256,256]{2,1,0:T(8,128)} fusion(f32[16,256,256]{2,1,0:T(8,128)} %get-tuple-element.569, s32[]{:T(128)} %get-tuple-element.568, bf16[256,4096]{1,0:T(8,128)(2,1)} %get-tuple-element.584, s32[256]{0:T(256)S(1)} %get-tuple-element.547, bf16[256,256]{1,0:T(8,128)(2,1)S(1)} %multiply_convert_fusion.30), kind=kOutput, calls=%fused_computation.77.clone.3 | convolution fusion | flops 588316672 | bytes 2491904 | tf_op jit(solution)/shard_map/while/body/eval_jaxpr/dot_general | solution.py:39
  430.2 1.4 constant_dynamic-slice_fusion.5
  434.2 19.7 %fusion.112 = f32[16,256,256]{2,1,0:T(8,128)} fusion(f32[16,256,256]{2,1,0:T(8,128)} %get-tuple-element.569, s32[]{:T(128)} %get-tuple-element.568, bf16[256,4096]{1,0:T(8,128)(2,1)} %get-tuple-element.584, s32[256]{0:T(256)S(1)} %get-tuple-element.547, bf16[256,256]{1,0:T(8,128)(2,1)S(1)} %multiply_convert_fusion.30), kind=kOutput, calls=%fused_computation.77.clone.3 | convolution fusion | flops 588316672 | bytes 2491904 | tf_op jit(solution)/shard_map/while/body/eval_jaxpr/dot_general | solution.py:39
  454.9 79.0 %reduce-scatter.3.cloned.1.call-done = f32[1,256,256]{2,1,0:T(8,128)} async-done(((f32[16,256,256]{2,1,0:T(8,128)}), f32[1,256,256]{2,1,0:T(8,128)}) %reduce-scatter.3.cloned.1.call-update) | async-done | bytes 262160 | tf_op jit(solution)/shard_map/reduce_scatter | solution.py:41
  534.9 1.6 broadcast_select_fusion
  536.4 4.2 all-to-all-start
  540.7 29.3 %all-to-all-done = bf16[16,256,256]{2,1,0:T(8,128)(2,1)S(1)} async-done(((bf16[16,256,256]{2,1,0:T(8,128)(2,1)}), bf16[16,256,256]{2,1,0:T(8,128)(2,1)S(1)}, u32[]{:S(2)}, u32[]{:S(2)}) %all-to-all-start) | async-done | bytes 2097184 | tf_op jit(solution)/shard_map/all_to_all | solution.py:53
  570.0 2.4 broadcast_in_dim.51
  572.4 211.3 %while.33 = (s32[]{:T(128)}, f32[256,4096]{1,0:T(8,128)}, s32[]{:T(128)}, s32[128,8]{0,1:T(8,128)S(1)}, s32[]{:T(128)}, /*index=5*/s32[128,2]{0,1:T(2,128)S(1)},...) while((s32[]{:T(128)}, f32[256,4096]{1,0:T(8,128)}, ...), condition=%wide.region_8.9_spmd.clone.clone, body=%wide.region_4.8_spmd.clone.clone.sunk | while | flops 590485760 | bytes 8825315 | solution.py:78
  575.4 23.4 %conditional.4 = (f32[256,4096]{1,0:T(8,128)}) conditional(s32[]{:T(128)} %convert_element_type.181, f32[256,4096]{1,0:T(8,128)} %get-tuple-element.603, (s32[]{:T(128)}, s32[]{:T(128)}, s32[128,2]{0,1:T(2,128)S(1)}, s32[256]{0:T(256)S(1)}, s32[]{:T(128)}, /*index=5*/bf16[16,256,256]{2,1,0:T(8,128)(2,1)S(1)}, s32[]{:T(128)}, s32[256]{0:T(256)S(1)}, ...), branch_computations={%region_6.6_spmd, %region_7.7_spmd} | conditional | flops 590485760 | bytes 8807598 | solution.py:76
  577.4 1.3 convolution_convert_fusion.clone.5
  578.7 20.1 %convolution_add_fusion = f32[256,4096]{1,0:T(8,128)} fusion(f32[256,4096]{1,0:T(8,128)} %get-tuple-element.302, s32[4096]{0:T(1024)S(1)} %get-tuple-element.311, s32[256]{0:T(256)S(1)} %get-tuple-element.451, bf16[256,256]{1,0:T(8,128)(2,1)S(1)} %convolution_convert_fusion.clone.5), kind=kOutput, calls=%fused_computation.11 | convolution fusion | flops 555745280 | bytes 8537088 | tf_op jit(solution)/shard_map/while/body/eval_jaxpr/cond/branch_1_fun/dot_general | solution.py:74
  604.9 23.4 %conditional.4 = (f32[256,4096]{1,0:T(8,128)}) conditional(s32[]{:T(128)} %convert_element_type.181, f32[256,4096]{1,0:T(8,128)} %get-tuple-element.603, (s32[]{:T(128)}, s32[]{:T(128)}, s32[128,2]{0,1:T(2,128)S(1)}, s32[256]{0:T(256)S(1)}, s32[]{:T(128)}, /*index=5*/bf16[16,256,256]{2,1,0:T(8,128)(2,1)S(1)}, s32[]{:T(128)}, s32[256]{0:T(256)S(1)}, ...), branch_computations={%region_6.6_spmd, %region_7.7_spmd} | conditional | flops 590485760 | bytes 8807598 | solution.py:76
  606.8 1.3 convolution_convert_fusion.clone.5
  608.2 20.1 %convolution_add_fusion = f32[256,4096]{1,0:T(8,128)} fusion(f32[256,4096]{1,0:T(8,128)} %get-tuple-element.302, s32[4096]{0:T(1024)S(1)} %get-tuple-element.311, s32[256]{0:T(256)S(1)} %get-tuple-element.451, bf16[256,256]{1,0:T(8,128)(2,1)S(1)} %convolution_convert_fusion.clone.5), kind=kOutput, calls=%fused_computation.11 | convolution fusion | flops 555745280 | bytes 8537088 | tf_op jit(solution)/shard_map/while/body/eval_jaxpr/cond/branch_1_fun/dot_general | solution.py:74
  629.8 23.4 %conditional.4 = (f32[256,4096]{1,0:T(8,128)}) conditional(s32[]{:T(128)} %convert_element_type.181, f32[256,4096]{1,0:T(8,128)} %get-tuple-element.603, (s32[]{:T(128)}, s32[]{:T(128)}, s32[128,2]{0,1:T(2,128)S(1)}, s32[256]{0:T(256)S(1)}, s32[]{:T(128)}, /*index=5*/bf16[16,256,256]{2,1,0:T(8,128)(2,1)S(1)}, s32[]{:T(128)}, s32[256]{0:T(256)S(1)}, ...), branch_computations={%region_6.6_spmd, %region_7.7_spmd} | conditional | flops 590485760 | bytes 8807598 | solution.py:76
  631.7 1.3 convolution_convert_fusion.clone.5
  633.0 20.1 %convolution_add_fusion = f32[256,4096]{1,0:T(8,128)} fusion(f32[256,4096]{1,0:T(8,128)} %get-tuple-element.302, s32[4096]{0:T(1024)S(1)} %get-tuple-element.311, s32[256]{0:T(256)S(1)} %get-tuple-element.451, bf16[256,256]{1,0:T(8,128)(2,1)S(1)} %convolution_convert_fusion.clone.5), kind=kOutput, calls=%fused_computation.11 | convolution fusion | flops 555745280 | bytes 8537088 | tf_op jit(solution)/shard_map/while/body/eval_jaxpr/cond/branch_1_fun/dot_general | solution.py:74
  654.6 23.4 %conditional.4 = (f32[256,4096]{1,0:T(8,128)}) conditional(s32[]{:T(128)} %convert_element_type.181, f32[256,4096]{1,0:T(8,128)} %get-tuple-element.603, (s32[]{:T(128)}, s32[]{:T(128)}, s32[128,2]{0,1:T(2,128)S(1)}, s32[256]{0:T(256)S(1)}, s32[]{:T(128)}, /*index=5*/bf16[16,256,256]{2,1,0:T(8,128)(2,1)S(1)}, s32[]{:T(128)}, s32[256]{0:T(256)S(1)}, ...), branch_computations={%region_6.6_spmd, %region_7.7_spmd} | conditional | flops 590485760 | bytes 8807598 | solution.py:76
  656.6 1.3 convolution_convert_fusion.clone.5
  657.9 20.1 %convolution_add_fusion = f32[256,4096]{1,0:T(8,128)} fusion(f32[256,4096]{1,0:T(8,128)} %get-tuple-element.302, s32[4096]{0:T(1024)S(1)} %get-tuple-element.311, s32[256]{0:T(256)S(1)} %get-tuple-element.451, bf16[256,256]{1,0:T(8,128)(2,1)S(1)} %convolution_convert_fusion.clone.5), kind=kOutput, calls=%fused_computation.11 | convolution fusion | flops 555745280 | bytes 8537088 | tf_op jit(solution)/shard_map/while/body/eval_jaxpr/cond/branch_1_fun/dot_general | solution.py:74
  682.6 23.4 %conditional.4 = (f32[256,4096]{1,0:T(8,128)}) conditional(s32[]{:T(128)} %convert_element_type.181, f32[256,4096]{1,0:T(8,128)} %get-tuple-element.603, (s32[]{:T(128)}, s32[]{:T(128)}, s32[128,2]{0,1:T(2,128)S(1)}, s32[256]{0:T(256)S(1)}, s32[]{:T(128)}, /*index=5*/bf16[16,256,256]{2,1,0:T(8,128)(2,1)S(1)}, s32[]{:T(128)}, s32[256]{0:T(256)S(1)}, ...), branch_computations={%region_6.6_spmd, %region_7.7_spmd} | conditional | flops 590485760 | bytes 8807598 | solution.py:76
  685.9 20.1 %convolution_add_fusion = f32[256,4096]{1,0:T(8,128)} fusion(f32[256,4096]{1,0:T(8,128)} %get-tuple-element.302, s32[4096]{0:T(1024)S(1)} %get-tuple-element.311, s32[256]{0:T(256)S(1)} %get-tuple-element.451, bf16[256,256]{1,0:T(8,128)(2,1)S(1)} %convolution_convert_fusion.clone.5), kind=kOutput, calls=%fused_computation.11 | convolution fusion | flops 555745280 | bytes 8537088 | tf_op jit(solution)/shard_map/while/body/eval_jaxpr/cond/branch_1_fun/dot_general | solution.py:74
  709.0 23.4 %conditional.4 = (f32[256,4096]{1,0:T(8,128)}) conditional(s32[]{:T(128)} %convert_element_type.181, f32[256,4096]{1,0:T(8,128)} %get-tuple-element.603, (s32[]{:T(128)}, s32[]{:T(128)}, s32[128,2]{0,1:T(2,128)S(1)}, s32[256]{0:T(256)S(1)}, s32[]{:T(128)}, /*index=5*/bf16[16,256,256]{2,1,0:T(8,128)(2,1)S(1)}, s32[]{:T(128)}, s32[256]{0:T(256)S(1)}, ...), branch_computations={%region_6.6_spmd, %region_7.7_spmd} | conditional | flops 590485760 | bytes 8807598 | solution.py:76
  712.3 20.1 %convolution_add_fusion = f32[256,4096]{1,0:T(8,128)} fusion(f32[256,4096]{1,0:T(8,128)} %get-tuple-element.302, s32[4096]{0:T(1024)S(1)} %get-tuple-element.311, s32[256]{0:T(256)S(1)} %get-tuple-element.451, bf16[256,256]{1,0:T(8,128)(2,1)S(1)} %convolution_convert_fusion.clone.5), kind=kOutput, calls=%fused_computation.11 | convolution fusion | flops 555745280 | bytes 8537088 | tf_op jit(solution)/shard_map/while/body/eval_jaxpr/cond/branch_1_fun/dot_general | solution.py:74
  733.9 23.4 %conditional.4 = (f32[256,4096]{1,0:T(8,128)}) conditional(s32[]{:T(128)} %convert_element_type.181, f32[256,4096]{1,0:T(8,128)} %get-tuple-element.603, (s32[]{:T(128)}, s32[]{:T(128)}, s32[128,2]{0,1:T(2,128)S(1)}, s32[256]{0:T(256)S(1)}, s32[]{:T(128)}, /*index=5*/bf16[16,256,256]{2,1,0:T(8,128)(2,1)S(1)}, s32[]{:T(128)}, s32[256]{0:T(256)S(1)}, ...), branch_computations={%region_6.6_spmd, %region_7.7_spmd} | conditional | flops 590485760 | bytes 8807598 | solution.py:76
  737.2 20.1 %convolution_add_fusion = f32[256,4096]{1,0:T(8,128)} fusion(f32[256,4096]{1,0:T(8,128)} %get-tuple-element.302, s32[4096]{0:T(1024)S(1)} %get-tuple-element.311, s32[256]{0:T(256)S(1)} %get-tuple-element.451, bf16[256,256]{1,0:T(8,128)(2,1)S(1)} %convolution_convert_fusion.clone.5), kind=kOutput, calls=%fused_computation.11 | convolution fusion | flops 555745280 | bytes 8537088 | tf_op jit(solution)/shard_map/while/body/eval_jaxpr/cond/branch_1_fun/dot_general | solution.py:74
  758.8 23.4 %conditional.4 = (f32[256,4096]{1,0:T(8,128)}) conditional(s32[]{:T(128)} %convert_element_type.181, f32[256,4096]{1,0:T(8,128)} %get-tuple-element.603, (s32[]{:T(128)}, s32[]{:T(128)}, s32[128,2]{0,1:T(2,128)S(1)}, s32[256]{0:T(256)S(1)}, s32[]{:T(128)}, /*index=5*/bf16[16,256,256]{2,1,0:T(8,128)(2,1)S(1)}, s32[]{:T(128)}, s32[256]{0:T(256)S(1)}, ...), branch_computations={%region_6.6_spmd, %region_7.7_spmd} | conditional | flops 590485760 | bytes 8807598 | solution.py:76
  762.1 20.1 %convolution_add_fusion = f32[256,4096]{1,0:T(8,128)} fusion(f32[256,4096]{1,0:T(8,128)} %get-tuple-element.302, s32[4096]{0:T(1024)S(1)} %get-tuple-element.311, s32[256]{0:T(256)S(1)} %get-tuple-element.451, bf16[256,256]{1,0:T(8,128)(2,1)S(1)} %convolution_convert_fusion.clone.5), kind=kOutput, calls=%fused_computation.11 | convolution fusion | flops 555745280 | bytes 8537088 | tf_op jit(solution)/shard_map/while/body/eval_jaxpr/cond/branch_1_fun/dot_general | solution.py:74
  783.7 3.8 convert_element_type.71
  787.5 227.0 %reduce-scatter.5.cloned.1.call-done = bf16[256,512]{1,0:T(8,128)(2,1)} async-done(((bf16[256,4096]{1,0:T(8,128)(2,1)}), bf16[256,512]{1,0:T(8,128)(2,1)}) %reduce-scatter.5.cloned.1.call-update) | async-done | bytes 262160 | tf_op jit(solution)/shard_map/reduce_scatter | solution.py:81
  1014.5 1.8 convert_element_type.72
  (167 shorter events, 85.7 us)
Async XLA Ops:
  7.2 47.3 %all-gather.2.cloned.1.call-start = ((), (), s32[]{:S(2)}) async-start(), calls=%async_computation.3 | async-start | bytes 2359296 | tf_op jit(solution)/shard_map/all_gather | solution.py:26
  9.0 524.9 %reduce-scatter.3.cloned.1.call-start = ((), (), s32[]{:S(2)}) async-start(), calls=%async_computation.4 | async-start | bytes 4456448 | tf_op jit(solution)/shard_map/reduce_scatter | solution.py:41
  453.9 0.7 copy-start.1
  453.9 80.0 %copy-start.2 = (bf16[1,256,256]{2,1,0:T(8,128)(2,1)S(1)}, bf16[1,256,256]{2,1,0:T(8,128)(2,1)}, u32[]{:S(2)}) copy-start(bf16[1,256,256]{2,1,0:T(8,128)(2,1)} %param.11) | copy-start | bytes 393220
  534.9 37.5 %copy-start = (bf16[1,256,256]{2,1,0:T(8,128)(2,1)}, bf16[1,256,256]{2,1,0:T(8,128)(2,1)S(1)}, u32[]{:S(2)}) copy-start(bf16[1,256,256]{2,1,0:T(8,128)(2,1)S(1)} %subtract_convert_fusion) | copy-start | bytes 393220
  536.4 36.0 %copy-start.3 = (s32[128,2]{0,1:T(2,128)S(1)}, s32[128,2]{0,1:T(2,128)}, u32[]{:S(2)}) copy-start(s32[128,2]{0,1:T(2,128)} %get-tuple-element.639) | copy-start | bytes 3076
  536.4 33.6 %all-to-all-start = ((bf16[16,256,256]{2,1,0:T(8,128)(2,1)}), bf16[16,256,256]{2,1,0:T(8,128)(2,1)S(1)}, u32[]{:S(2)}, u32[]{:S(2)}) async-start(bf16[16,256,256]{2,1,0:T(8,128)(2,1)} %broadcast_select_fusion), calls=%async_computation.1 | async-start | bytes 4194304 | tf_op jit(solution)/shard_map/all_to_all | solution.py:53
  540.7 473.8 %reduce-scatter.5.cloned.1.call-start = ((), (), s32[]{:S(2)}) async-start(), calls=%async_computation.5 | async-start | bytes 2359296 | tf_op jit(solution)/shard_map/reduce_scatter | solution.py:81
Sparse Core Ops, SparseCore 0:
  10.2 44.1 all-gather.1
  454.1 79.7 reduce-scatter.2
  787.6 226.8 reduce-scatter.4
where the time goes:
time: 1030 us; the launch traced here: 1020 us
  matrix products  487 us (47%)
  waiting for transfers between devices  381 us (37%)
  other arithmetic  73.6 us (7%)
  local copies, waits for them, and re-layouts  40.5 us (4%)
  loops' own time  22.9 us (2%)
  between operations  13.8 us (1%)
    dot_general x16, matrix products, single(): return jnp.dot(row_pred, inner, preferred_element_type=jnp.float32)  316 us
    reduce_scatter x1, waiting for transfers between devices, on_device(): lax.psum_scatter(partial_image.astype(jnp.bfloat16), 'vis', scatter_dimen...  227 us
    dot_general x8, matrix products, add_term(): jnp.dot(left_rows(source), col_grid, preferred_element_type=jnp.float32)  161 us
    reduce_scatter x1, waiting for transfers between devices, on_device(): lax.psum_scatter(lax.map(single, jnp.arange(1 * lax.axis_size('facet'), d...  79 us
    all_gather x1, waiting for transfers between devices, on_device(): lax.all_gather(sky_image.astype(jnp.bfloat16), 'vis', axis=1, tiled=True)  45.3 us
    select_n x24, other arithmetic, cas_table(): phase = freqs[:, None] % period * places[None, :] % period  30.7 us
    all_to_all x1, waiting for transfers between devices, on_device(): lax.all_to_all(outgoing, 'facet', split_axis=0, concat_axis=0, tiled=True)  29.3 us
    dynamic_slice x16, local copies, waits for them, and re-layouts, single(): offsets[sub_index, 1] + sub_ids  22.6 us
  transfers between devices with their start and end apart: 4, of which 4 were waited for; matrix products, arithmetic and copies ran while one was open for 0% of the time, Pallas kernels for 0%

commit v1 on v0

v1 whole, which is shorter than its diff:
```python
import jax
import jax.numpy as jnp
import ml_dtypes
import numpy as np
from jax import lax
from jax.experimental import pallas as pl
from jax.experimental.pallas import tpu as pltpu
from jax.sharding import PartitionSpec as P

F32 = jnp.float32
BF16 = jnp.bfloat16
N = 4096
SUB = 256
HALF = 0.5**0.5
NT = (((1,), (1,)), ((), ()))


def turn(phase, period):
    angle = (2.0 * np.pi / period) * (phase % period)
    return np.cos(angle), np.sin(angle)


def bf(table):
    return table.astype(ml_dtypes.bfloat16)


def column_tables():
    order = np.arange(512)
    k1 = 16 * (order % 32) + order // 32
    c, s = turn(np.arange(512)[:, None] * k1[None, :], 512)
    ahead = bf(np.concatenate([c + s, c - s], axis=0) / 64.0)
    back = bf(np.concatenate([c.T, s.T], axis=1) / 16.0)
    c, s = turn(np.arange(8)[:, None] * np.arange(512)[None, :], N)
    return ahead, back, np.concatenate([c, s], axis=0).astype(np.float32)


def row_table():
    g = np.arange(N).reshape(16, 256)
    c, s = turn(g[:, :, None] * np.arange(SUB)[None, None, :], N)
    return bf(np.stack([c + s, c - s], axis=1).reshape(2 * N, SUB))


def own_index():
    return lax.axis_index("facet") * 8 + lax.axis_index("vis")


def lane_group(rows):
    return lax.broadcasted_iota(jnp.int32, (rows, 128), 1) >> 5


def swap_groups(parts, group):
    out = []
    for j in range(4):
        moved = [pltpu.roll(parts[i], (32 * (i - j)) % 128, 1) if i != j else parts[i] for i in range(4)]
        mixed = jnp.where(group < 2, jnp.where(group == 0, moved[0], moved[1]), jnp.where(group == 2, moved[2], moved[3]))
        out.append(mixed)
    return out


def block_selector(u):
    row = lax.broadcasted_iota(jnp.int32, (1024, 512), 0)
    col = lax.broadcasted_iota(jnp.int32, (1024, 512), 1)
    hit = ((row & 7) == (col >> 7)) & ((((row >> 3) - u) & 127) == (col & 127))
    return jnp.where(hit, 1.0, 0.0).astype(BF16)


def columns_ahead(rx_ref, obs_ref, off_ref, tw_ref, tab_ref, out_ref):
    x = [rx_ref[j].astype(F32) for j in range(8)]
    e = [x[i] + x[i + 4] for i in range(4)]
    o = [x[i] - x[i + 4] for i in range(4)]
    up, down = (o[1] + o[3]) * HALF, (o[1] - o[3]) * HALF
    e02, e13 = e[0] + e[2], e[1] + e[3]
    d1 = (o[0] + down, o[2] + up)
    d2 = (e[0] - e[2], e[1] - e[3])
    d3 = (o[0] - down, up - o[2])
    spec = [(e02 + e13, None), d1, d2, d3, (e02 - e13, None), (d3[0], -d3[1]), (d2[0], -d2[1]), (d1[0], -d1[1])]
    rows = []
    for k2 in range(8):
        c, s = tw_ref[k2 : k2 + 1, :], tw_ref[8 + k2 : 9 + k2, :]
        re, im = spec[k2]
        if im is None:
            zr, zi = re * c, re * s
        else:
            zr, zi = re * c - im * s, re * s + im * c
        rows.append(jnp.concatenate([zr, zi], axis=1))
    left = jnp.concatenate(rows, axis=0).astype(BF16)
    freq = jnp.dot(left, tab_ref[...], preferred_element_type=F32)

    u = off_ref[own_index(), 0]
    obs = obs_ref[0]
    quarters = jnp.concatenate([obs[:128, :128], obs[128:, :128], obs[:128, 128:], obs[128:, 128:]], axis=1)
    seen = lax.dot_general(block_selector(u), quarters, NT, preferred_element_type=F32).reshape(128, 8, 128)

    group = lane_group(64)
    for qg in range(4):
        part = freq[:, 128 * qg : 128 * qg + 128].reshape(8, 4, 8, 128)
        tiles = swap_groups([part[:, rg].reshape(64, 128) for rg in range(4)], group)
        for q4 in range(4):
            at = 8 * (4 * qg + q4)
            block = jnp.concatenate([tiles[q4].reshape(8, 8, 128), seen[at : at + 8]], axis=1)
            out_ref[at : at + 8] = block.astype(BF16)


def spin(re, im, c, s):
    return re * c - im * s, re * s + im * c


def cos_sin(phase):
    angle = (phase & (N - 1)).astype(F32) * np.float32(2.0 * np.pi / N)
    return jnp.cos(angle), jnp.sin(angle)


def rows_kernel(rx_ref, off_ref, asg_ref, tab_ref, out_ref, ybuf, ec, es, ect, est, rr):
    me = own_index()
    off = off_ref[...]
    u, v = off[:, 0:1], off[:, 1:2]
    first = (me - u) & 127
    s0 = ((u + first - me) >> 7) & 31
    lane = lax.broadcasted_iota(jnp.int32, (128, 128), 1)
    chosen0 = jnp.where((lane & 31) == s0, 1.0, 0.0)
    chosen1 = jnp.where((lane & 31) == ((s0 + 1) & 31), 1.0, 0.0)
    chosen = jnp.concatenate([chosen0, chosen1], axis=0).astype(BF16)

    v_row = jnp.transpose(jnp.broadcast_to(v.astype(F32), (128, 128)))[:16].astype(jnp.int32)
    step = lax.broadcasted_iota(jnp.int32, (16, 128), 0)
    lo_c, lo_s = cos_sin(v_row * step)
    hi_c, hi_s = cos_sin(v_row * step * 16)
    pairs = [spin(lo_c, lo_s, hi_c[i : i + 1], hi_s[i : i + 1]) for i in range(16)]
    base_c = jnp.concatenate([p[0] for p in pairs], axis=0)
    base_s = jnp.concatenate([p[1] for p in pairs], axis=0)
    ec[...], es[...] = base_c, base_s
    ect[...], est[...] = jnp.transpose(base_c), jnp.transpose(base_s)
    turn_c, turn_s = cos_sin(v_row[:8] * 256)
    turn_ct = jnp.transpose(jnp.broadcast_to(turn_c[:1], (256, 128)))
    turn_st = jnp.transpose(jnp.broadcast_to(turn_s[:1], (256, 128)))
    group = lax.broadcasted_iota(jnp.int32, (8, 8, 128), 2) >> 5

    @pl.loop(0, 16)
    def _(f):
        tile = rx_ref[pl.ds(8 * f, 8)].astype(F32)[:, 0:8]
        spread = jnp.stack([jnp.where(group == rg, tile, 0.0) for rg in range(4)], axis=1)
        right = spread.reshape(256, 128).astype(BF16)
        cols = lax.dot_general(chosen, right, NT, preferred_element_type=F32)
        c, s = ect[...], est[...]
        at = pl.multiple_of(f * 512, 512)
        for t in range(2):
            half = cols[128 * t : 128 * t + 128]
            ybuf[128 * t : 128 * t + 128, pl.ds(at, 256)] = (half * c).astype(BF16)
            ybuf[128 * t : 128 * t + 128, pl.ds(at + 256, 256)] = (half * s).astype(BF16)
        ect[...], est[...] = spin(c, s, turn_ct, turn_st)

    pred = jnp.dot(ybuf[...], tab_ref[...], preferred_element_type=F32) * (1.0 / 64.0)

    seen = rx_ref[...].astype(F32)[:, 8:16].reshape(1024, 128).astype(BF16)
    row = lax.broadcasted_iota(jnp.int32, (256, 1024), 0)
    col = lax.broadcasted_iota(jnp.int32, (256, 1024), 1)
    same = (col >> 3) == (row & 127)
    obs = []
    for ah in range(2):
        pick = jnp.where(same & ((col & 7) == 2 * (row >> 7) + ah), 1.0, 0.0).astype(BF16)
        obs.append(jnp.dot(pick, seen, preferred_element_type=F32))
    resid = (jnp.concatenate(obs, axis=1) - pred).astype(BF16)
    row = lax.broadcasted_iota(jnp.int32, (1024, 256), 0)
    col = lax.broadcasted_iota(jnp.int32, (1024, 256), 1)
    same = (row >> 3) == (col & 127)
    back = jnp.zeros((1024, 128), F32)
    for ah in range(2):
        pick = jnp.where(same & ((row & 7) == 2 * (col >> 7) + ah), 1.0, 0.0).astype(BF16)
        back = back + jnp.dot(pick, resid[:, 128 * ah : 128 * ah + 128], preferred_element_type=F32)
    rr[...] = back.reshape(128, 8, 128)

    bits = jnp.sum(lax.shift_left(jnp.ones_like(asg_ref[...]), asg_ref[...]).astype(F32), axis=1, keepdims=True)
    bits = jnp.broadcast_to(bits, (128, 128)).astype(jnp.int32)

    @pl.loop(0, 16)
    def _(f):
        at = pl.multiple_of(f * 512, 512)
        w1 = lax.dot_general(tab_ref[pl.ds(at, 256), :], resid, NT, preferred_element_type=F32)
        w2 = lax.dot_general(tab_ref[pl.ds(at + 256, 256), :], resid, NT, preferred_element_type=F32)
        c, s = ec[...], es[...]
        z = [c * w1[:, 128 * t : 128 * t + 128] + s * w2[:, 128 * t : 128 * t + 128] for t in range(2)]
        z = jnp.concatenate(z, axis=1).astype(BF16)
        named = (lax.shift_right_logical(bits, f) & 1) == 1
        keep = jnp.concatenate([jnp.where(named, chosen0, 0.0), jnp.where(named, chosen1, 0.0)], axis=0).astype(BF16)
        grid = jnp.dot(z, keep, preferred_element_type=F32).reshape(8, 4, 8, 128)
        mixed = jnp.where(
            group < 2,
            jnp.where(group == 0, grid[:, 0], grid[:, 1]),
            jnp.where(group == 2, grid[:, 2], grid[:, 3]),
        )
        block = jnp.concatenate([mixed * (1.0 / 16.0), rr[pl.ds(8 * f, 8)]], axis=1)
        out_ref[pl.ds(8 * f, 8)] = block.astype(BF16)
        nc, ns = spin(c.reshape(32, 8, 128), s.reshape(32, 8, 128), turn_c[None], turn_s[None])
        ec[...], es[...] = nc.reshape(256, 128), ns.reshape(256, 128)


def columns_back(rx_ref, off_ref, tw_ref, tab_ref, img_ref, res_ref):
    got = rx_ref[...].astype(F32)
    tiles = got[:, 0:8].reshape(16, 64, 128)
    group = lane_group(64)
    wide = [[None] * 4 for _ in range(4)]
    for qg in range(4):
        mixed = swap_groups([tiles[4 * qg + q4] for q4 in range(4)], group)
        for rg in range(4):
            wide[rg][qg] = mixed[rg].reshape(8, 8, 128)
    left = jnp.stack([jnp.concatenate(wide[rg], axis=2) for rg in range(4)], axis=1)
    left = left.reshape(256, 512).astype(BF16)
    both = jnp.dot(left, tab_ref[...], preferred_element_type=F32).reshape(8, 32, 1024)
    re, im = [], []
    for k2 in range(8):
        c, s = tw_ref[k2 : k2 + 1, :], tw_ref[8 + k2 : 9 + k2, :]
        a, b = spin(both[k2, :, :512], both[k2, :, 512:], c + s, s - c)
        re.append(a)
        im.append(b)
    a1, a2, a3 = re[1] + re[7], re[2] + re[6], re[3] + re[5]
    b1, b2, b3 = im[1] - im[7], im[2] - im[6], im[3] - im[5]
    plus, minus = re[0] + re[4], re[0] - re[4]
    even = [plus + a2, minus - b2, plus - a2, minus + b2]
    odd = [a1 + a3, HALF * (a1 - b1 - a3 - b3), b3 - b1, HALF * (a3 - a1 - b1 - b3)]
    for j in range(4):
        img_ref[j] = (even[j] + odd[j]).astype(BF16)
        img_ref[j + 4] = (even[j] - odd[j]).astype(BF16)

    u = off_ref[own_index(), 0]
    back = jnp.transpose(got[:, 8:16].reshape(1024, 128)).astype(BF16)
    quarters = jnp.dot(back, block_selector(u), preferred_element_type=F32).astype(BF16)
    for t in range(2):
        for ah in range(2):
            i = 2 * t + ah
            res_ref[0, 128 * ah : 128 * ah + 128, 128 * t : 128 * t + 128] = quarters[:, 128 * i : 128 * i + 128]


VMEM = pl.BlockSpec(memory_space=pltpu.VMEM)
SMEM = pl.BlockSpec(memory_space=pltpu.SMEM)
PARAMS = pltpu.CompilerParams(vmem_limit_bytes=56 * 2**20)


def on_device(sky_image, observed, offsets, assignments):
    ahead, back, twiddle = column_tables()
    rows = row_table()
    everyone = ("facet", "vis")
    message = jax.ShapeDtypeStruct((128, 16, 128), BF16)

    strips = sky_image.astype(BF16).reshape(8, 32, 512)
    strips = lax.all_to_all(strips, "vis", 0, 0, tiled=True)
    sent = pl.pallas_call(
        columns_ahead,
        out_shape=message,
        in_specs=[VMEM, VMEM, SMEM, VMEM, VMEM],
        out_specs=VMEM,
        compiler_params=PARAMS,
    )(strips, observed, offsets, jnp.asarray(twiddle), jnp.asarray(ahead))
    got = lax.all_to_all(sent, everyone, 0, 0, tiled=True)
    sent = pl.pallas_call(
        rows_kernel,
        out_shape=message,
        in_specs=[VMEM, VMEM, VMEM, VMEM],
        out_specs=VMEM,
        scratch_shapes=[
            pltpu.VMEM((256, 2 * N), BF16),
            pltpu.VMEM((256, 128), F32),
            pltpu.VMEM((256, 128), F32),
            pltpu.VMEM((128, 256), F32),
            pltpu.VMEM((128, 256), F32),
            pltpu.VMEM((128, 8, 128), F32),
        ],
        compiler_params=PARAMS,
    )(got, offsets, assignments, jnp.asarray(rows))
    got = lax.all_to_all(sent, everyone, 0, 0, tiled=True)
    image, resid = pl.pallas_call(
        columns_back,
        out_shape=(
            jax.ShapeDtypeStruct((8, 32, 512), BF16),
            jax.ShapeDtypeStruct((1, SUB, SUB), BF16),
        ),
        in_specs=[VMEM, SMEM, VMEM, VMEM],
        out_specs=(VMEM, VMEM),
        compiler_params=PARAMS,
    )(got, offsets, jnp.asarray(twiddle), jnp.asarray(back))
    image = lax.all_to_all(image, "vis", 0, 0, tiled=True)
    return resid, image.reshape(256, 512).astype(F32)


def solution(mesh):
    placed = (P("facet", "vis"), P(("facet", "vis"), None, None), P(), P())
    return jax.shard_map(
        on_device,
        mesh=mesh,
        in_specs=placed,
        out_specs=(P(("facet", "vis"), None, None), P("facet", "vis")),
        check_vma=False,
    )
```

time: 1030 us -> 92.5 us (0.09)
  matrix products: 487 us -> 0 us
  waiting for transfers between devices: 381 us -> 18.3 us
  other arithmetic: 73.6 us -> 2.65 us
  local copies, waits for them, and re-layouts: 40.5 us -> 3.63 us
  blocking collectives: 0 us -> 29.8 us
  Pallas kernels: 0 us -> 23 us
  loops' own time: 22.9 us -> 0 us
  between operations: 13.8 us -> 0.66 us
    dot_general x32 -> x0, matrix products: 487 us -> none  [the longest x16 316 us: single(): return jnp.dot(row_pred, inner, preferred_element_type=jnp.float32)]
    reduce_scatter x2 -> x0, waiting for transfers between devices: 306 us -> none  [the longest x1 227 us: on_device(): lax.psum_scatter(partial_image.astype(jnp.bfloat16), 'vis', scatter_dimen...]
    all_gather x1 -> x0, waiting for transfers between devices: 45.3 us -> none  [on_device(): lax.all_gather(sky_image.astype(jnp.bfloat16), 'vis', axis=1, tiled=True)]
    dynamic_slice x41 -> x0, local copies, waits for them, and re-layouts: 37.3 us -> none  [the longest x16 22.6 us: single(): offsets[sub_index, 1] + sub_ids]
    select_n x25 -> x0, other arithmetic: 32.3 us -> none  [the longest x24 30.7 us: cas_table(): phase = freqs[:, None] % period * places[None, :] % period]
    all_to_all x0 -> x2, blocking collectives: none -> 29.8 us  [the longest x1 18.8 us: on_device(): got = lax.all_to_all(sent, everyone, 0, 0, tiled=True)]
    pallas_call x0 -> x3, Pallas kernels: none -> 23 us  [the longest x1 15.9 us: on_device(): pl.pallas_call(rows_kernel, out_shape=message, in_specs=[VMEM, VMEM, VMEM...]
    another operation x18 -> x0, loops' own time: 22.9 us -> none  [the longest x1 11.3 us: on_device(): lax.fori_loop(0, n_facet, add_slot, jnp.zeros((face_rows, width_cols), jn...]
  transfers between devices with their start and end apart: 4 -> 2, of which waited for: 4 -> 2; matrix products, arithmetic and copies ran while one was open for 0% -> 2% of each run, Pallas kernels for 0% -> 0%
where the time goes in v1:
time: 92.5 us; the launch traced here: 92 us
  blocking collectives  29.8 us (32%)
  Pallas kernels  23 us (25%)
  waiting for transfers between devices  18.3 us (20%)
  starting transfers between devices  14 us (15%)
  local copies, waits for them, and re-layouts  3.63 us (4%)
  other arithmetic  2.65 us (3%)
    all_to_all x1, blocking collectives, on_device(): got = lax.all_to_all(sent, everyone, 0, 0, tiled=True)  18.8 us
    pallas_call x1, Pallas kernels, on_device(): pl.pallas_call(rows_kernel, out_shape=message, in_specs=[VMEM, VMEM, VMEM...  15.9 us
    all_to_all x1, waiting for transfers between devices, on_device(): got = lax.all_to_all(sent, everyone, 0, 0, tiled=True)  12.5 us
    all_to_all x1, blocking collectives, on_device(): image = lax.all_to_all(image, 'vis', 0, 0, tiled=True)  11 us
    all_to_all x1, starting transfers between devices, on_device(): got = lax.all_to_all(sent, everyone, 0, 0, tiled=True)  8.49 us
    all_to_all x1, waiting for transfers between devices, on_device(): strips = lax.all_to_all(strips, 'vis', 0, 0, tiled=True)  5.82 us
    all_to_all x1, starting transfers between devices, on_device(): strips = lax.all_to_all(strips, 'vis', 0, 0, tiled=True)  5.48 us
    unnamed x8, local copies, waits for them, and re-layouts  3.63 us
  transfers between devices with their start and end apart: 2, of which 2 were waited for; matrix products, arithmetic and copies ran while one was open for 2% of the time, Pallas kernels for 0%

profile of v1, /device:TPU:0, one launch (start us, length us, event | category | flops | bytes accessed | tf_op | source)
XLA Modules:
  0.0 92.0 jit_solution(11950786889683051095)
XLA Ops:
  0.6 0.0 copy-start.2
  0.6 1.8 %convert_element_type.9 = bf16[256,512]{1,0:T(8,128)(2,1)} convert(f32[256,512]{1,0:T(8,128)} %param.8) | non-fusion elementwise | flops 131072 | bytes 786432 | tf_op jit(solution)/shard_map/convert_element_type | solution.py:244
  2.4 5.5 %all-to-all-start = ((bf16[8,32,512]{2,1,0:T(8,128)(2,1)}), bf16[8,32,512]{2,1,0:T(8,128)(2,1)S(1)}, u32[]{:S(2)}, u32[]{:S(2)}) async-start(bf16[8,32,512]{2,1,0:T(8,128)(2,1)} %bitcast), calls=%async_computation | async-start | bytes 524288 | tf_op jit(solution)/shard_map/all_to_all | solution.py:245
  7.9 1.4 %copy.10.off_ref = s32[128,2]{1,0:T(8,128)} copy(s32[128,2]{0,1:T(2,128)} %param.10) | data formatting | bytes 2048 | tf_op args[2]
  9.3 5.8 %all-to-all-done.rx_ref = bf16[8,32,512]{2,1,0:T(8,128)(2,1)S(1)} async-done(((bf16[8,32,512]{2,1,0:T(8,128)(2,1)}), bf16[8,32,512]{2,1,0:T(8,128)(2,1)S(1)}, u32[]{:S(2)}, u32[]{:S(2)}) %all-to-all-start) | async-done | bytes 262176 | tf_op jit(solution)/shard_map/all_to_all | solution.py:245
  15.1 0.0 copy-start.1
  15.1 0.7 copy-done.1
  15.8 3.5 %shard_map.95 = bf16[128,16,128]{2,1,0:T(8,128)(2,1)} custom-call(bf16[8,32,512]{2,1,0:T(8,128)(2,1)} %copy-done.1, bf16[1,256,256]{2,1,0:T(8,128)(2,1)} %obs_ref.1, s32[128,2]{1,0:T(8,128)} %copy.10.off_ref, f32[16,512]{1,0:T(8,128)} %constant.8.clone.tw_ref, bf16[1024,512]{1,0:T(8,128)(2,1)} %constant.9.clone.tab_ref), custom_call_target="tpu_custom_call" | custom-call | tf_op jit(solution)/shard_map/pallas_call | solution.py:246
  19.4 8.5 %all-to-all-start.1 = ((bf16[128,16,128]{2,1,0:T(8,128)(2,1)}), bf16[128,16,128]{2,1,0:T(8,128)(2,1)S(1)}, u32[]{:S(2)}, u32[]{:S(2)}) async-start(bf16[128,16,128]{2,1,0:T(8,128)(2,1)} %shard_map.95), calls=%async_computation.1 | async-start | bytes 1048576 | tf_op jit(solution)/shard_map/all_to_all | solution.py:253
  27.8 0.0 copy-done.2
  27.9 0.7 copy.12.asg_ref
  28.6 12.5 %all-to-all-done.1.rx_ref = bf16[128,16,128]{2,1,0:T(8,128)(2,1)S(1)} async-done(((bf16[128,16,128]{2,1,0:T(8,128)(2,1)}), bf16[128,16,128]{2,1,0:T(8,128)(2,1)S(1)}, u32[]{:S(2)}, u32[]{:S(2)}) %all-to-all-start.1) | async-done | bytes 524320 | tf_op jit(solution)/shard_map/all_to_all | solution.py:253
  41.1 0.0 copy-start
  41.1 0.8 copy-done
  41.9 15.9 %shard_map.96 = bf16[128,16,128]{2,1,0:T(8,128)(2,1)} custom-call(bf16[128,16,128]{2,1,0:T(8,128)(2,1)} %copy-done, s32[128,2]{1,0:T(8,128)} %copy.10.off_ref, s32[128,8]{1,0:T(8,128)} %copy.12.asg_ref, bf16[8192,256]{1,0:T(8,128)(2,1)} %constant.10.clone.tab_ref), custom_call_target="tpu_custom_call" | custom-call | tf_op jit(solution)/shard_map/pallas_call | solution.py:254
  57.8 18.8 %all_to_all.20.rx_ref = bf16[128,16,128]{2,1,0:T(8,128)(2,1)} all-to-all(bf16[128,16,128]{2,1,0:T(8,128)(2,1)} %shard_map.96), channel_id=1, replica_groups=mesh['facet'=16,'vis'=8] {'facet','vis'}, dimensions={0} | all-to-all | bytes 1048576 | tf_op jit(solution)/shard_map/all_to_all | solution.py:269
  76.5 3.6 %shard_map.97 = (bf16[8,32,512]{2,1,0:T(8,128)(2,1)}, bf16[1,256,256]{2,1,0:T(8,128)(2,1)}) custom-call(bf16[128,16,128]{2,1,0:T(8,128)(2,1)} %all_to_all.20.rx_ref, s32[128,2]{1,0:T(8,128)} %copy.10.off_ref, f32[16,512]{1,0:T(8,128)} %constant.8.clone.tw_ref, bf16[512,1024]{1,0:T(8,128)(2,1)} %constant.11.clone.tab_ref), custom_call_target="tpu_custom_call" | custom-call | tf_op jit(solution)/shard_map/pallas_call | solution.py:270
  80.1 11.0 %all_to_all.21 = bf16[8,32,512]{2,1,0:T(8,128)(2,1)S(1)} all-to-all(bf16[8,32,512]{2,1,0:T(8,128)(2,1)} %get-tuple-element.5), channel_id=1, replica_groups=mesh['facet'=16,'vis'=8] {'vis'}, dimensions={0} | all-to-all | bytes 524288 | tf_op jit(solution)/shard_map/all_to_all | solution.py:280
  91.1 0.9 bitcast_convert_fusion
Async XLA Ops:
  0.6 27.2 %copy-start.2 = (s32[128,8]{0,1:T(8,128)S(1)}, s32[128,8]{0,1:T(8,128)}, u32[]{:S(2)}) copy-start(s32[128,8]{0,1:T(8,128)} %param.11) | copy-start | bytes 12292
  2.4 12.7 %all-to-all-start = ((bf16[8,32,512]{2,1,0:T(8,128)(2,1)}), bf16[8,32,512]{2,1,0:T(8,128)(2,1)S(1)}, u32[]{:S(2)}, u32[]{:S(2)}) async-start(bf16[8,32,512]{2,1,0:T(8,128)(2,1)} %bitcast), calls=%async_computation | async-start | bytes 524288 | tf_op jit(solution)/shard_map/all_to_all | solution.py:245
  15.1 0.7 copy-start.1
  19.4 21.7 %all-to-all-start.1 = ((bf16[128,16,128]{2,1,0:T(8,128)(2,1)}), bf16[128,16,128]{2,1,0:T(8,128)(2,1)S(1)}, u32[]{:S(2)}, u32[]{:S(2)}) async-start(bf16[128,16,128]{2,1,0:T(8,128)(2,1)} %shard_map.95), calls=%async_computation.1 | async-start | bytes 1048576 | tf_op jit(solution)/shard_map/all_to_all | solution.py:253
  41.1 0.8 copy-start

commit v2 on v1

v2 whole, which is shorter than its diff:
```python
import jax
import jax.numpy as jnp
import ml_dtypes
import numpy as np
from jax import lax
from jax.experimental import pallas as pl
from jax.experimental.pallas import tpu as pltpu
from jax.sharding import PartitionSpec as P

F32 = jnp.float32
BF16 = jnp.bfloat16
N = 4096
SUB = 256
HALF = 0.5**0.5
NT = (((1,), (1,)), ((), ()))


def turn(phase, period):
    angle = (2.0 * np.pi / period) * (phase % period)
    return np.cos(angle), np.sin(angle)


def bf(table):
    return table.astype(ml_dtypes.bfloat16)


def column_tables():
    order = np.arange(512)
    k1 = 16 * (order % 32) + order // 32
    c, s = turn(np.arange(512)[:, None] * k1[None, :], 512)
    ahead = bf(np.concatenate([c + s, c - s], axis=0) / 64.0)
    back = bf(np.concatenate([c.T, s.T], axis=1) / 16.0)
    c, s = turn(np.arange(8)[:, None] * np.arange(512)[None, :], N)
    return ahead, back, np.concatenate([c, s], axis=0).astype(np.float32)


def row_table():
    g = np.arange(N).reshape(16, 256)
    c, s = turn(g[:, :, None] * np.arange(SUB)[None, None, :], N)
    return bf(np.stack([c + s, c - s], axis=1).reshape(2 * N, SUB))


def own_index():
    return lax.axis_index("facet") * 8 + lax.axis_index("vis")


def lane_group(rows):
    return lax.broadcasted_iota(jnp.int32, (rows, 128), 1) >> 5


def swap_groups(parts, group):
    out = []
    for j in range(4):
        moved = [pltpu.roll(parts[i], (32 * (i - j)) % 128, 1) if i != j else parts[i] for i in range(4)]
        mixed = jnp.where(group < 2, jnp.where(group == 0, moved[0], moved[1]), jnp.where(group == 2, moved[2], moved[3]))
        out.append(mixed)
    return out


def block_selector(u):
    row = lax.broadcasted_iota(jnp.int32, (1024, 512), 0)
    col = lax.broadcasted_iota(jnp.int32, (1024, 512), 1)
    hit = ((row & 7) == (col >> 7)) & ((((row >> 3) - u) & 127) == (col & 127))
    return jnp.where(hit, 1.0, 0.0).astype(BF16)


def spin(re, im, c, s):
    return re * c - im * s, re * s + im * c


def cos_sin(phase):
    angle = (phase & (N - 1)).astype(F32) * np.float32(2.0 * np.pi / N)
    return jnp.cos(angle), jnp.sin(angle)


def tables(off_ref, asg_ref, ct_ref, st_ref, cg_ref, sg_ref, tc_ref, ts_ref, chosen_ref, bits_ref):
    me = own_index()
    v_row = jnp.broadcast_to(off_ref[1:2, :], (16, 128))
    step = lax.broadcasted_iota(jnp.int32, (16, 128), 0)
    lo_c, lo_s = cos_sin(v_row * step)
    hi_c, hi_s = cos_sin(v_row * step * 16)
    top_c, top_s = cos_sin(v_row * 256)
    pairs = [spin(lo_c, lo_s, hi_c[i : i + 1], hi_s[i : i + 1]) for i in range(16)]
    c = jnp.concatenate([p[0] for p in pairs], axis=0)
    s = jnp.concatenate([p[1] for p in pairs], axis=0)
    cg_ref[...], sg_ref[...] = c, s
    ct_ref[...], st_ref[...] = jnp.transpose(c), jnp.transpose(s)
    tc_ref[...], ts_ref[...] = top_c, top_s

    u = off_ref[0:1, :]
    first = (me - u) & 127
    s0 = ((u + first - me) >> 7) & 31
    lane = lax.broadcasted_iota(jnp.int32, (128, 128), 0) & 31
    for t in range(2):
        hit = jnp.where(lane == ((s0 + t) & 31), 1.0, 0.0)
        chosen_ref[128 * t : 128 * t + 128] = jnp.transpose(hit)
    asg = asg_ref[...]
    bits = jnp.sum(lax.shift_left(jnp.ones_like(asg), asg).astype(F32), axis=0, keepdims=True)
    bits_ref[...] = jnp.transpose(jnp.broadcast_to(bits, (128, 128))).astype(jnp.int32)


def round_image(sky_hbm, out_ref, held, sems):
    moves = [pltpu.make_async_copy(sky_hbm.at[pl.ds(64 * i, 64)], held.at[pl.ds(64 * i, 64)], sems.at[i]) for i in range(4)]
    for move in moves:
        move.start()
    for i, move in enumerate(moves):
        move.wait()
        out_ref[2 * i : 2 * i + 2] = held[64 * i : 64 * i + 64].reshape(2, 32, 512).astype(BF16)


def columns_ahead(rx_ref, obs_hbm, off_ref, big_hbm, out_ref, obs_ref, tab_ref, sems):
    moves = [pltpu.make_async_copy(obs_hbm, obs_ref, sems.at[0])]
    for i in range(2):
        half = big_hbm.at[pl.ds(2 * N + 1024 * i, 1024)]
        moves.append(pltpu.make_async_copy(half, tab_ref.at[:, pl.ds(256 * i, 256)], sems.at[1 + i]))
    for move in moves:
        move.start()
    k2 = lax.broadcasted_iota(jnp.int32, (8, 512), 0)
    twist_c, twist_s = cos_sin(k2 * lax.broadcasted_iota(jnp.int32, (8, 512), 1))
    x = [rx_ref[j].astype(F32) for j in range(8)]
    e = [x[i] + x[i + 4] for i in range(4)]
    o = [x[i] - x[i + 4] for i in range(4)]
    up, down = (o[1] + o[3]) * HALF, (o[1] - o[3]) * HALF
    e02, e13 = e[0] + e[2], e[1] + e[3]
    d1 = (o[0] + down, o[2] + up)
    d2 = (e[0] - e[2], e[1] - e[3])
    d3 = (o[0] - down, up - o[2])
    spec = [(e02 + e13, None), d1, d2, d3, (e02 - e13, None), (d3[0], -d3[1]), (d2[0], -d2[1]), (d1[0], -d1[1])]
    rows = []
    for k2 in range(8):
        c, s = twist_c[k2 : k2 + 1], twist_s[k2 : k2 + 1]
        re, im = spec[k2]
        if im is None:
            zr, zi = re * c, re * s
        else:
            zr, zi = re * c - im * s, re * s + im * c
        rows.append(jnp.concatenate([zr, zi], axis=1))
    left = jnp.concatenate(rows, axis=0).astype(BF16)
    for move in moves:
        move.wait()
    freq = jnp.dot(left, tab_ref[...], preferred_element_type=F32)

    u = off_ref[0:1, :]
    place = lax.broadcasted_iota(jnp.int32, (1, 128), 1)
    u = jnp.sum(jnp.where(place == own_index(), u, 0).astype(F32), axis=1, keepdims=True).astype(jnp.int32)
    obs = obs_ref[0]
    quarters = jnp.concatenate([obs[:128, :128], obs[128:, :128], obs[:128, 128:], obs[128:, 128:]], axis=1)
    seen = lax.dot_general(block_selector(u), quarters, NT, preferred_element_type=F32).reshape(128, 8, 128)

    group = lane_group(64)
    for qg in range(4):
        part = freq[:, 128 * qg : 128 * qg + 128].reshape(8, 4, 8, 128)
        tiles = swap_groups([part[:, rg].reshape(64, 128) for rg in range(4)], group)
        for q4 in range(4):
            at = 8 * (4 * qg + q4)
            tile = tiles[q4].reshape(8, 8, 128).astype(BF16)
            out_ref[at : at + 8, 0] = tile[:, 0:4]
            out_ref[at : at + 8, 1] = tile[:, 4:8]
            out_ref[at : at + 8, 2] = seen[at : at + 8, 0:4].astype(BF16)


def rows_kernel(
    rx_ref, off_ref, asg_ref, big_hbm,
    out_ref, ybuf, held, obs, rr, ct, st, cg, sg, tc_ref, ts_ref, chosen_ref, bits_ref, tab_ref, sem,
):
    fetch = pltpu.make_async_copy(big_hbm.at[pl.ds(0, 2 * N)], tab_ref, sem)
    fetch.start()
    tables(off_ref, asg_ref, ct, st, cg, sg, tc_ref, ts_ref, chosen_ref, bits_ref)
    group = lax.broadcasted_iota(jnp.int32, (8, 8, 128), 2) >> 5
    got = rx_ref[...].astype(F32)
    held[:, 0:4] = got[:, 0]
    held[:, 4:8] = got[:, 1]
    obs[:, 0:4] = got[:, 2]
    chosen = chosen_ref[...].astype(BF16)
    turn_ct = jnp.transpose(jnp.broadcast_to(tc_ref[:1], (256, 128)))
    turn_st = jnp.transpose(jnp.broadcast_to(ts_ref[:1], (256, 128)))

    @pl.loop(0, 16, unroll=UNROLL)
    def _(f):
        tile = held[pl.ds(8 * f, 8)]
        spread = jnp.stack([jnp.where(group == rg, tile, 0.0) for rg in range(4)], axis=1)
        right = spread.reshape(256, 128).astype(BF16)
        cols = lax.dot_general(chosen, right, NT, preferred_element_type=F32)
        at = pl.multiple_of(f * 512, 512)
        c, s = ct[...], st[...]
        for t in range(2):
            half = cols[128 * t : 128 * t + 128]
            ybuf[128 * t : 128 * t + 128, pl.ds(at, 256)] = (half * c).astype(BF16)
            ybuf[128 * t : 128 * t + 128, pl.ds(at + 256, 256)] = (half * s).astype(BF16)
        ct[...], st[...] = spin(c, s, turn_ct, turn_st)

    fetch.wait()
    pred = jnp.dot(ybuf[...], tab_ref[...], preferred_element_type=F32) * (1.0 / 64.0)
    resid = []
    seen, back = obs.reshape(1024, 128), rr.reshape(1024, 128)
    for t in range(2):
        halves = []
        for ah in range(2):
            quarter = seen[pl.ds(2 * t + ah, 128, stride=8), :] - pred[128 * t : 128 * t + 128, 128 * ah : 128 * ah + 128]
            halves.append(quarter.astype(BF16))
            back[pl.ds(2 * t + ah, 128, stride=8), :] = quarter
        resid.append(jnp.concatenate(halves, axis=1))
    resid = jnp.concatenate(resid, axis=0)
    turn_c, turn_s = tc_ref[:8][None], ts_ref[:8][None]

    @pl.loop(0, 16, unroll=UNROLL)
    def _(f):
        at = pl.multiple_of(f * 512, 512)
        both = lax.dot_general(tab_ref[pl.ds(at, 512), :], resid, NT, preferred_element_type=F32)
        w1, w2 = both[:256], both[256:]
        c, s = cg[...], sg[...]
        z = [c * w1[:, 128 * t : 128 * t + 128] + s * w2[:, 128 * t : 128 * t + 128] for t in range(2)]
        z = jnp.concatenate(z, axis=1).astype(BF16)
        named = (lax.shift_right_logical(bits_ref[...], f) & 1) == 1
        keep = [jnp.where(named, chosen_ref[128 * t : 128 * t + 128], 0.0) for t in range(2)]
        keep = jnp.concatenate(keep, axis=0).astype(BF16)
        grid = jnp.dot(z, keep, preferred_element_type=F32).reshape(8, 4, 8, 128)
        mixed = jnp.where(
            group < 2,
            jnp.where(group == 0, grid[:, 0], grid[:, 1]),
            jnp.where(group == 2, grid[:, 2], grid[:, 3]),
        )
        mixed = (mixed * (1.0 / 16.0)).astype(BF16)
        out_ref[pl.ds(8 * f, 8), 0] = mixed[:, 0:4]
        out_ref[pl.ds(8 * f, 8), 1] = mixed[:, 4:8]
        out_ref[pl.ds(8 * f, 8), 2] = rr[pl.ds(8 * f, 8)][:, 0:4].astype(BF16)
        nc, ns = spin(c.reshape(32, 8, 128), s.reshape(32, 8, 128), turn_c, turn_s)
        cg[...], sg[...] = nc.reshape(256, 128), ns.reshape(256, 128)


def columns_back(rx_ref, off_ref, tw_ref, tab_ref, img_ref, res_ref, held, sent):
    got = rx_ref[...].astype(F32)
    held[:, 0:4] = got[:, 0]
    held[:, 4:8] = got[:, 1]
    tiles = held[...].reshape(16, 64, 128)
    group = lane_group(64)
    wide = [[None] * 4 for _ in range(4)]
    for qg in range(4):
        mixed = swap_groups([tiles[4 * qg + q4] for q4 in range(4)], group)
        for rg in range(4):
            wide[rg][qg] = mixed[rg].reshape(8, 8, 128)
    left = jnp.stack([jnp.concatenate(wide[rg], axis=2) for rg in range(4)], axis=1)
    left = left.reshape(256, 512).astype(BF16)
    both = jnp.dot(left, tab_ref[...], preferred_element_type=F32).reshape(8, 32, 1024)
    re, im = [], []
    for k2 in range(8):
        c, s = tw_ref[k2 : k2 + 1, :], tw_ref[8 + k2 : 9 + k2, :]
        a, b = spin(both[k2, :, :512], both[k2, :, 512:], c + s, s - c)
        re.append(a)
        im.append(b)
    a1, a2, a3 = re[1] + re[7], re[2] + re[6], re[3] + re[5]
    b1, b2, b3 = im[1] - im[7], im[2] - im[6], im[3] - im[5]
    plus, minus = re[0] + re[4], re[0] - re[4]
    even = [plus + a2, minus - b2, plus - a2, minus + b2]
    odd = [a1 + a3, HALF * (a1 - b1 - a3 - b3), b3 - b1, HALF * (a3 - a1 - b1 - b3)]
    for j in range(4):
        img_ref[j] = (even[j] + odd[j]).astype(BF16)
        img_ref[j + 4] = (even[j] - odd[j]).astype(BF16)

    u = off_ref[0, own_index()]
    sent[...] = jnp.zeros_like(sent)
    sent[:, 0:4] = got[:, 2]
    back = jnp.transpose(sent[...].reshape(1024, 128)).astype(BF16)
    quarters = jnp.dot(back, block_selector(u), preferred_element_type=F32).astype(BF16)
    for t in range(2):
        for ah in range(2):
            i = 2 * t + ah
            res_ref[0, 128 * ah : 128 * ah + 128, 128 * t : 128 * t + 128] = quarters[:, 128 * i : 128 * i + 128]


VMEM = pl.BlockSpec(memory_space=pltpu.VMEM)
SMEM = pl.BlockSpec(memory_space=pltpu.SMEM)
HBM = pl.BlockSpec(memory_space=pltpu.HBM)
UNROLL = 4
L0, L1, L2 = 53, 53, 53


def params(mebibytes):
    return pltpu.CompilerParams(vmem_limit_bytes=mebibytes * 2**20)


def on_device(sky_image, observed, offsets, assignments):
    ahead, back, twiddle = column_tables()
    big = jnp.asarray(np.concatenate([row_table(), ahead[:, :256], ahead[:, 256:]], axis=0))
    everyone = ("facet", "vis")
    message = jax.ShapeDtypeStruct((128, 3, 4, 128), BF16)
    offsets, assignments = offsets.T, assignments.T

    strips = pl.pallas_call(
        round_image,
        out_shape=jax.ShapeDtypeStruct((8, 32, 512), BF16),
        in_specs=[HBM],
        out_specs=VMEM,
        scratch_shapes=[pltpu.VMEM((256, 512), F32), pltpu.SemaphoreType.DMA((4,))],
        compiler_params=params(L0),
    )(sky_image)
    strips = lax.all_to_all(strips, "vis", 0, 0, tiled=True)
    sent = pl.pallas_call(
        columns_ahead,
        out_shape=message,
        in_specs=[VMEM, HBM, VMEM, HBM],
        out_specs=VMEM,
        scratch_shapes=[
            pltpu.VMEM((1, SUB, SUB), BF16),
            pltpu.VMEM((1024, 512), BF16),
            pltpu.SemaphoreType.DMA((3,)),
        ],
        compiler_params=params(L1),
    )(strips, observed, offsets, big)
    got = lax.all_to_all(sent, everyone, 0, 0, tiled=True)
    sent = pl.pallas_call(
        rows_kernel,
        out_shape=message,
        in_specs=[VMEM, VMEM, VMEM, HBM],
        out_specs=VMEM,
        scratch_shapes=[
            pltpu.VMEM((256, 2 * N), BF16),
            pltpu.VMEM((128, 8, 128), F32),
            pltpu.VMEM((128, 8, 128), F32),
            pltpu.VMEM((128, 8, 128), F32),
            pltpu.VMEM((128, 256), F32),
            pltpu.VMEM((128, 256), F32),
            pltpu.VMEM((256, 128), F32),
            pltpu.VMEM((256, 128), F32),
            pltpu.VMEM((16, 128), F32),
            pltpu.VMEM((16, 128), F32),
            pltpu.VMEM((256, 128), F32),
            pltpu.VMEM((128, 128), jnp.int32),
            pltpu.VMEM((2 * N, 256), BF16),
            pltpu.SemaphoreType.DMA,
        ],
        compiler_params=params(L2),
    )(got, offsets, assignments, big)
    got = lax.all_to_all(sent, everyone, 0, 0, tiled=True)
    image, resid = pl.pallas_call(
        columns_back,
        out_shape=(
            jax.ShapeDtypeStruct((8, 32, 512), BF16),
            jax.ShapeDtypeStruct((1, SUB, SUB), BF16),
        ),
        in_specs=[VMEM, SMEM, VMEM, VMEM],
        out_specs=(VMEM, VMEM),
        scratch_shapes=[pltpu.VMEM((128, 8, 128), F32), pltpu.VMEM((128, 8, 128), F32)],
        compiler_params=params(16),
    )(got, offsets, jnp.asarray(twiddle), jnp.asarray(back))
    image = lax.all_to_all(image, "vis", 0, 0, tiled=True)
    return resid, image.reshape(256, 512).astype(F32)


def solution(mesh):
    placed = (P("facet", "vis"), P(("facet", "vis"), None, None), P(), P())
    return jax.shard_map(
        on_device,
        mesh=mesh,
        in_specs=placed,
        out_specs=(P(("facet", "vis"), None, None), P("facet", "vis")),
        check_vma=False,
    )
```

time: 92.5 us -> 77.1 us (0.83)
  blocking collectives: 29.8 us -> 59.2 us
  waiting for transfers between devices: 18.3 us -> 0 us
  starting transfers between devices: 14 us -> 0 us
  Pallas kernels: 23 us -> 13.3 us
  other arithmetic: 2.65 us -> 0.87 us
  local copies, waits for them, and re-layouts: 3.63 us -> 2.64 us
    all_to_all x2 -> x0, waiting for transfers between devices: 18.3 us -> none  [the longest x1 12.5 us: on_device(): got = lax.all_to_all(sent, everyone, 0, 0, tiled=True)]
    all_to_all x1 -> x2, blocking collectives: 18.8 us -> 36.6 us  [on_device(): got = lax.all_to_all(sent, everyone, 0, 0, tiled=True)]
    all_to_all x2 -> x0, starting transfers between devices: 14 us -> none  [the longest x1 8.49 us: on_device(): got = lax.all_to_all(sent, everyone, 0, 0, tiled=True)]
    all_to_all x0 -> x1, blocking collectives: none -> 12.5 us  [on_device(): strips = lax.all_to_all(strips, 'vis', 0, 0, tiled=True)]
    pallas_call x1, Pallas kernels: 15.9 us -> 8.01 us  [on_device(): pl.pallas_call(rows_kernel, out_shape=message, in_specs=[VMEM, VMEM, VMEM...]
    convert_element_type x1 -> x0, other arithmetic: 1.78 us -> none  [on_device(): strips = sky_image.astype(BF16).reshape(8, 32, 512)]
    pallas_call x1, Pallas kernels: 3.57 us -> 2.38 us  [on_device(): pl.pallas_call(columns_back, out_shape=(jax.ShapeDtypeStruct((8, 32, 512)...]
    unnamed x8 -> x14, local copies, waits for them, and re-layouts: 3.63 us -> 2.64 us
  transfers between devices with their start and end apart: 2 -> 0, of which waited for: 2 -> 0; matrix products, arithmetic and copies ran while one was open for 2% -> 0% of each run, Pallas kernels for 0% -> 0%
where the time goes in v2:
time: 77.1 us; the launch traced here: 76.7 us
  blocking collectives  59.2 us (77%)
  Pallas kernels  13.3 us (17%)
  local copies, waits for them, and re-layouts  2.64 us (3%)
  other arithmetic  0.87 us (1%)
    all_to_all x2, blocking collectives, on_device(): got = lax.all_to_all(sent, everyone, 0, 0, tiled=True)  36.6 us
    all_to_all x1, blocking collectives, on_device(): strips = lax.all_to_all(strips, 'vis', 0, 0, tiled=True)  12.5 us
    all_to_all x1, blocking collectives, on_device(): image = lax.all_to_all(image, 'vis', 0, 0, tiled=True)  10.1 us
    pallas_call x1, Pallas kernels, on_device(): pl.pallas_call(rows_kernel, out_shape=message, in_specs=[VMEM, VMEM, VMEM...  8.01 us
    unnamed x14, local copies, waits for them, and re-layouts  2.64 us
    pallas_call x1, Pallas kernels, on_device(): pl.pallas_call(columns_back, out_shape=(jax.ShapeDtypeStruct((8, 32, 512)...  2.38 us
    pallas_call x1, Pallas kernels, on_device(): pl.pallas_call(columns_ahead, out_shape=message, in_specs=[VMEM, HBM, VME...  2.23 us

profile of v2, /device:TPU:0, one launch (start us, length us, event | category | flops | bytes accessed | tf_op | source)
XLA Modules:
  0.0 76.7 jit_solution(15075162947713227458)
XLA Ops:
  0.6 0.0 copy-start.1
  0.6 1.0 %copy-done.1 = f32[256,512]{1,0:T(8,128)S(1)} copy-done((f32[256,512]{1,0:T(8,128)S(1)}, f32[256,512]{1,0:T(8,128)}, u32[]{:S(2)}) %copy-start.1) | copy-done | bytes 524312
  1.7 0.0 copy-start.5
  1.7 0.0 copy-start.6
  1.7 0.7 shard_map.86
  2.4 12.5 %all_to_all.20.rx_ref = bf16[8,32,512]{2,1,0:T(8,128)(2,1)S(1)} all-to-all(bf16[8,32,512]{2,1,0:T(8,128)(2,1)S(1)} %shard_map.86), channel_id=1, replica_groups=mesh['facet'=16,'vis'=8] {'vis'}, dimensions={0} | all-to-all | bytes 524288 | tf_op jit(solution)/shard_map/all_to_all | solution.py:297
  14.9 0.0 copy-start.2
  14.9 0.9 %copy-done.2 = bf16[1,256,256]{2,1,0:T(8,128)(2,1)S(1)} copy-done((bf16[1,256,256]{2,1,0:T(8,128)(2,1)S(1)}, bf16[1,256,256]{2,1,0:T(8,128)(2,1)}, u32[]{:S(2)}) %copy-start.2) | copy-done | bytes 131096
  15.8 0.0 copy-start.4
  15.8 0.7 copy-done.4
  16.5 2.2 %shard_map.87 = bf16[128,3,4,128]{3,2,1,0:T(4,128)(2,1)S(1)} custom-call(bf16[8,32,512]{2,1,0:T(8,128)(2,1)S(1)} %all_to_all.20.rx_ref, bf16[1,256,256]{2,1,0:T(8,128)(2,1)S(1)} %copy-done.2, s32[2,128]{1,0:T(2,128)S(1)} %bitcast.5, bf16[10240,256]{1,0:T(8,128)(2,1)} %constant.6.clone.big_hbm), custom_call_target="tpu_custom_call" | custom-call | tf_op jit(solution)/shard_map/pallas_call | solution.py:298
  18.7 0.0 copy-start
  18.8 0.0 copy-start.3
  18.8 20.2 %all_to_all.21.rx_ref = bf16[128,3,4,128]{3,2,1,0:T(4,128)(2,1)S(1)} all-to-all(bf16[128,3,4,128]{3,2,1,0:T(4,128)(2,1)S(1)} %shard_map.87), channel_id=1, replica_groups=mesh['facet'=16,'vis'=8] {'facet','vis'}, dimensions={0} | all-to-all | bytes 786432 | tf_op jit(solution)/shard_map/all_to_all | solution.py:310
  39.0 0.0 copy-done.5
  39.0 0.0 copy-done.6
  39.0 8.0 %shard_map.88 = bf16[128,3,4,128]{3,2,1,0:T(4,128)(2,1)S(1)} custom-call(bf16[128,3,4,128]{3,2,1,0:T(4,128)(2,1)S(1)} %all_to_all.21.rx_ref, s32[2,128]{1,0:T(2,128)S(1)} %bitcast.6, s32[8,128]{1,0:T(8,128)S(1)} %bitcast.8, bf16[10240,256]{1,0:T(8,128)(2,1)} %constant.6.clone.big_hbm), custom_call_target="tpu_custom_call" | custom-call | tf_op jit(solution)/shard_map/pallas_call | solution.py:311
  47.0 16.4 %all_to_all.22.rx_ref = bf16[128,3,4,128]{3,2,1,0:T(4,128)(2,1)S(1)} all-to-all(bf16[128,3,4,128]{3,2,1,0:T(4,128)(2,1)S(1)} %shard_map.88), channel_id=1, replica_groups=mesh['facet'=16,'vis'=8] {'facet','vis'}, dimensions={0} | all-to-all | bytes 786432 | tf_op jit(solution)/shard_map/all_to_all | solution.py:334
  63.4 0.0 copy-done
  63.4 0.0 copy-done.3
  63.4 2.4 %shard_map.89 = (bf16[8,32,512]{2,1,0:T(8,128)(2,1)S(1)}, bf16[1,256,256]{2,1,0:T(8,128)(2,1)}) custom-call(bf16[128,3,4,128]{3,2,1,0:T(4,128)(2,1)S(1)} %all_to_all.22.rx_ref, s32[2,128]{1,0:T(2,128)S(1)} %bitcast.7, f32[16,512]{1,0:T(8,128)S(1)} %copy-done.3, bf16[512,1024]{1,0:T(8,128)(2,1)S(1)} %copy-done), custom_call_target="tpu_custom_call" | custom-call | tf_op jit(solution)/shard_map/pallas_call | solution.py:335
  65.8 10.1 %all_to_all.23 = bf16[8,32,512]{2,1,0:T(8,128)(2,1)S(1)} all-to-all(bf16[8,32,512]{2,1,0:T(8,128)(2,1)S(1)} %get-tuple-element.5), channel_id=1, replica_groups=mesh['facet'=16,'vis'=8] {'vis'}, dimensions={0} | all-to-all | bytes 524288 | tf_op jit(solution)/shard_map/all_to_all | solution.py:346
  75.8 0.9 %bitcast_convert_fusion = f32[256,512]{1,0:T(8,128)} fusion(bf16[8,32,512]{2,1,0:T(8,128)(2,1)S(1)} %all_to_all.23), kind=kLoop, calls=%fused_computation | loop fusion | flops 131072 | bytes 786432 | tf_op jit(solution)/shard_map/convert_element_type | solution.py:347
Async XLA Ops:
  0.6 1.0 %copy-start.1 = (f32[256,512]{1,0:T(8,128)S(1)}, f32[256,512]{1,0:T(8,128)}, u32[]{:S(2)}) copy-start(f32[256,512]{1,0:T(8,128)} %sky_hbm.1) | copy-start | bytes 1572868
  1.7 37.3 %copy-start.5 = (s32[128,2]{0,1:T(2,128)S(1)}, s32[128,2]{0,1:T(2,128)}, u32[]{:S(2)}) copy-start(s32[128,2]{0,1:T(2,128)} %param.9) | copy-start | bytes 3076
  1.7 37.3 %copy-start.6 = (s32[128,8]{0,1:T(8,128)S(1)}, s32[128,8]{0,1:T(8,128)}, u32[]{:S(2)}) copy-start(s32[128,8]{0,1:T(8,128)} %param.10) | copy-start | bytes 12292
  14.9 0.9 %copy-start.2 = (bf16[1,256,256]{2,1,0:T(8,128)(2,1)S(1)}, bf16[1,256,256]{2,1,0:T(8,128)(2,1)}, u32[]{:S(2)}) copy-start(bf16[1,256,256]{2,1,0:T(8,128)(2,1)} %obs_hbm.1) | copy-start | bytes 393220
  15.8 0.7 copy-start.4
  18.7 44.7 %copy-start = (bf16[512,1024]{1,0:T(8,128)(2,1)S(1)}, bf16[512,1024]{1,0:T(8,128)(2,1)}, u32[]{:S(2)}) copy-start(bf16[512,1024]{1,0:T(8,128)(2,1)} %constant.8.clone.tab_ref) | copy-start | bytes 3145732
  18.8 44.6 %copy-start.3 = (f32[16,512]{1,0:T(8,128)S(1)}, f32[16,512]{1,0:T(8,128)}, u32[]{:S(2)}) copy-start(f32[16,512]{1,0:T(8,128)} %constant.7.clone.tw_ref) | copy-start | bytes 98308

commit v3 on v2

--- a/solution.py
+++ b/solution.py
@@ -57,11 +57,10 @@
     return out
 
 
-def block_selector(u):
-    row = lax.broadcasted_iota(jnp.int32, (1024, 512), 0)
-    col = lax.broadcasted_iota(jnp.int32, (1024, 512), 1)
-    hit = ((row & 7) == (col >> 7)) & ((((row >> 3) - u) & 127) == (col & 127))
-    return jnp.where(hit, 1.0, 0.0).astype(BF16)
+def selector(u):
+    row = lax.broadcasted_iota(jnp.int32, (128, 128), 0)
+    col = lax.broadcasted_iota(jnp.int32, (128, 128), 1)
+    return jnp.where(((row - u) & 127) == col, 1.0, 0.0).astype(BF16)
 
 
 def spin(re, im, c, s):
@@ -108,7 +107,7 @@
         out_ref[2 * i : 2 * i + 2] = held[64 * i : 64 * i + 64].reshape(2, 32, 512).astype(BF16)
 
 
-def columns_ahead(rx_ref, obs_hbm, off_ref, big_hbm, out_ref, obs_ref, tab_ref, sems):
+def columns_ahead(rx_ref, obs_hbm, off_ref, big_hbm, out_ref, obs_ref, tab_ref, seen, sems):
     moves = [pltpu.make_async_copy(obs_hbm, obs_ref, sems.at[0])]
     for i in range(2):
         half = big_hbm.at[pl.ds(2 * N + 1024 * i, 1024)]
@@ -143,10 +142,13 @@
     u = off_ref[0:1, :]
     place = lax.broadcasted_iota(jnp.int32, (1, 128), 1)
     u = jnp.sum(jnp.where(place == own_index(), u, 0).astype(F32), axis=1, keepdims=True).astype(jnp.int32)
-    obs = obs_ref[0]
-    quarters = jnp.concatenate([obs[:128, :128], obs[128:, :128], obs[:128, 128:], obs[128:, 128:]], axis=1)
-    seen = lax.dot_general(block_selector(u), quarters, NT, preferred_element_type=F32).reshape(128, 8, 128)
-
+    pick = selector(u)
+    rows = seen.reshape(1024, 128)
+    for t in range(2):
+        for ah in range(2):
+            quarter = obs_ref[0, 128 * ah : 128 * ah + 128, 128 * t : 128 * t + 128]
+            cols = lax.dot_general(pick, quarter, NT, preferred_element_type=F32)
+            rows[pl.ds(2 * t + ah, 128, stride=8), :] = cols
     group = lane_group(64)
     for qg in range(4):
         part = freq[:, 128 * qg : 128 * qg + 128].reshape(8, 4, 8, 128)
@@ -156,12 +158,12 @@
             tile = tiles[q4].reshape(8, 8, 128).astype(BF16)
             out_ref[at : at + 8, 0] = tile[:, 0:4]
             out_ref[at : at + 8, 1] = tile[:, 4:8]
-            out_ref[at : at + 8, 2] = seen[at : at + 8, 0:4].astype(BF16)
+            out_ref[at : at + 8, 2] = seen[at : at + 8][:, 0:4].astype(BF16)
 
 
 def rows_kernel(
     rx_ref, off_ref, asg_ref, big_hbm,
-    out_ref, ybuf, held, obs, rr, ct, st, cg, sg, tc_ref, ts_ref, chosen_ref, bits_ref, tab_ref, sem,
+    out_ref, ybuf, held, obs, rr, ct, st, cg, sg, tc_ref, ts_ref, chosen_ref, bits_ref, keep, zbuf, tab_ref, sem,
 ):
     fetch = pltpu.make_async_copy(big_hbm.at[pl.ds(0, 2 * N)], tab_ref, sem)
     fetch.start()
@@ -172,6 +174,7 @@
     held[:, 4:8] = got[:, 1]
     obs[:, 0:4] = got[:, 2]
     chosen = chosen_ref[...].astype(BF16)
+    turn_c, turn_s = tc_ref[:8][None], ts_ref[:8][None]
     turn_ct = jnp.transpose(jnp.broadcast_to(tc_ref[:1], (256, 128)))
     turn_st = jnp.transpose(jnp.broadcast_to(ts_ref[:1], (256, 128)))
 
@@ -181,40 +184,46 @@
         spread = jnp.stack([jnp.where(group == rg, tile, 0.0) for rg in range(4)], axis=1)
         right = spread.reshape(256, 128).astype(BF16)
         cols = lax.dot_general(chosen, right, NT, preferred_element_type=F32)
-        at = pl.multiple_of(f * 512, 512)
+        at = pl.multiple_of(f * 256, 256)
         c, s = ct[...], st[...]
         for t in range(2):
             half = cols[128 * t : 128 * t + 128]
-            ybuf[128 * t : 128 * t + 128, pl.ds(at, 256)] = (half * c).astype(BF16)
-            ybuf[128 * t : 128 * t + 128, pl.ds(at + 256, 256)] = (half * s).astype(BF16)
+            ybuf[128 * t : 128 * t + 128, pl.ds(2 * at, 256)] = (half * c).astype(BF16)
+            ybuf[128 * t : 128 * t + 128, pl.ds(2 * at + 256, 256)] = (half * s).astype(BF16)
         ct[...], st[...] = spin(c, s, turn_ct, turn_st)
+        named = (lax.shift_right_logical(bits_ref[...], f) & 1) == 1
+        for t in range(2):
+            kept = jnp.where(named, chosen_ref[128 * t : 128 * t + 128], 0.0)
+            keep[pl.ds(at + 128 * t, 128)] = kept.astype(BF16)
 
     fetch.wait()
     pred = jnp.dot(ybuf[...], tab_ref[...], preferred_element_type=F32) * (1.0 / 64.0)
+    seen, back = obs.reshape(1024, 128), rr.reshape(1024, 128)
     resid = []
-    seen, back = obs.reshape(1024, 128), rr.reshape(1024, 128)
     for t in range(2):
         halves = []
         for ah in range(2):
-            quarter = seen[pl.ds(2 * t + ah, 128, stride=8), :] - pred[128 * t : 128 * t + 128, 128 * ah : 128 * ah + 128]
-            halves.append(quarter.astype(BF16))
+            guess = pred[128 * t : 128 * t + 128, 128 * ah : 128 * ah + 128]
+            quarter = seen[pl.ds(2 * t + ah, 128, stride=8), :] - guess
+            halves.append(jnp.transpose(quarter))
             back[pl.ds(2 * t + ah, 128, stride=8), :] = quarter
-        resid.append(jnp.concatenate(halves, axis=1))
-    resid = jnp.concatenate(resid, axis=0)
-    turn_c, turn_s = tc_ref[:8][None], ts_ref[:8][None]
-
-    @pl.loop(0, 16, unroll=UNROLL)
+        resid.append(jnp.concatenate(halves, axis=0))
+    resid = jnp.concatenate(resid, axis=1).astype(BF16)
+
+    @pl.loop(0, 16, unroll=UNROLL1)
     def _(f):
-        at = pl.multiple_of(f * 512, 512)
-        both = lax.dot_general(tab_ref[pl.ds(at, 512), :], resid, NT, preferred_element_type=F32)
-        w1, w2 = both[:256], both[256:]
+        at = pl.multiple_of(f * 256, 256)
+        both = jnp.dot(tab_ref[pl.ds(2 * at, 512), :], resid, preferred_element_type=F32)
         c, s = cg[...], sg[...]
-        z = [c * w1[:, 128 * t : 128 * t + 128] + s * w2[:, 128 * t : 128 * t + 128] for t in range(2)]
-        z = jnp.concatenate(z, axis=1).astype(BF16)
-        named = (lax.shift_right_logical(bits_ref[...], f) & 1) == 1
-        keep = [jnp.where(named, chosen_ref[128 * t : 128 * t + 128], 0.0) for t in range(2)]
-        keep = jnp.concatenate(keep, axis=0).astype(BF16)
-        grid = jnp.dot(z, keep, preferred_element_type=F32).reshape(8, 4, 8, 128)
+        z = [c * both[:256, 128 * t : 128 * t + 128] + s * both[256:, 128 * t : 128 * t + 128] for t in range(2)]
+        zbuf[pl.ds(at, 256)] = jnp.concatenate(z, axis=1).astype(BF16)
+        nc, ns = spin(c.reshape(32, 8, 128), s.reshape(32, 8, 128), turn_c, turn_s)
+        cg[...], sg[...] = nc.reshape(256, 128), ns.reshape(256, 128)
+
+    @pl.loop(0, 16, unroll=UNROLL2)
+    def _(f):
+        at = pl.multiple_of(f * 256, 256)
+        grid = jnp.dot(zbuf[pl.ds(at, 256)], keep[pl.ds(at, 256)], preferred_element_type=F32).reshape(8, 4, 8, 128)
         mixed = jnp.where(
             group < 2,
             jnp.where(group == 0, grid[:, 0], grid[:, 1]),
@@ -224,8 +233,6 @@
         out_ref[pl.ds(8 * f, 8), 0] = mixed[:, 0:4]
         out_ref[pl.ds(8 * f, 8), 1] = mixed[:, 4:8]
         out_ref[pl.ds(8 * f, 8), 2] = rr[pl.ds(8 * f, 8)][:, 0:4].astype(BF16)
-        nc, ns = spin(c.reshape(32, 8, 128), s.reshape(32, 8, 128), turn_c, turn_s)
-        cg[...], sg[...] = nc.reshape(256, 128), ns.reshape(256, 128)
 
 
 def columns_back(rx_ref, off_ref, tw_ref, tab_ref, img_ref, res_ref, held, sent):
@@ -258,20 +265,20 @@
         img_ref[j + 4] = (even[j] - odd[j]).astype(BF16)
 
     u = off_ref[0, own_index()]
-    sent[...] = jnp.zeros_like(sent)
     sent[:, 0:4] = got[:, 2]
-    back = jnp.transpose(sent[...].reshape(1024, 128)).astype(BF16)
-    quarters = jnp.dot(back, block_selector(u), preferred_element_type=F32).astype(BF16)
+    rows = sent.reshape(1024, 128)
+    pick = selector(u)
     for t in range(2):
         for ah in range(2):
-            i = 2 * t + ah
-            res_ref[0, 128 * ah : 128 * ah + 128, 128 * t : 128 * t + 128] = quarters[:, 128 * i : 128 * i + 128]
+            quarter = jnp.transpose(rows[pl.ds(2 * t + ah, 128, stride=8), :]).astype(BF16)
+            quarter = jnp.dot(quarter, pick, preferred_element_type=F32).astype(BF16)
+            res_ref[0, 128 * ah : 128 * ah + 128, 128 * t : 128 * t + 128] = quarter
 
 
 VMEM = pl.BlockSpec(memory_space=pltpu.VMEM)
 SMEM = pl.BlockSpec(memory_space=pltpu.SMEM)
 HBM = pl.BlockSpec(memory_space=pltpu.HBM)
-UNROLL = 4
+UNROLL, UNROLL1, UNROLL2 = 8, 8, 16
 L0, L1, L2 = 53, 53, 53
 
 
@@ -303,6 +310,7 @@
         scratch_shapes=[
             pltpu.VMEM((1, SUB, SUB), BF16),
             pltpu.VMEM((1024, 512), BF16),
+            pltpu.VMEM((128, 8, 128), F32),
             pltpu.SemaphoreType.DMA((3,)),
         ],
         compiler_params=params(L1),
@@ -326,6 +334,8 @@
             pltpu.VMEM((16, 128), F32),
             pltpu.VMEM((256, 128), F32),
             pltpu.VMEM((128, 128), jnp.int32),
+            pltpu.VMEM((N, 128), BF16),
+            pltpu.VMEM((N, 256), BF16),
             pltpu.VMEM((2 * N, 256), BF16),
             pltpu.SemaphoreType.DMA,
         ],

time: 77.1 us -> 74.5 us (0.966)
  Pallas kernels: 13.3 us -> 10.7 us
    pallas_call x1, Pallas kernels: 8.01 us -> 5.96 us  [on_device(): pl.pallas_call(rows_kernel, out_shape=message, in_specs=[VMEM, VMEM, VMEM...]
where the time goes in v3:
time: 74.5 us; the launch traced here: 74.1 us
  blocking collectives  59.2 us (79%)
  Pallas kernels  10.7 us (14%)
  local copies, waits for them, and re-layouts  2.64 us (4%)
  other arithmetic  0.87 us (1%)
    all_to_all x2, blocking collectives, on_device(): got = lax.all_to_all(sent, everyone, 0, 0, tiled=True)  36.6 us
    all_to_all x1, blocking collectives, on_device(): strips = lax.all_to_all(strips, 'vis', 0, 0, tiled=True)  12.5 us
    all_to_all x1, blocking collectives, on_device(): image = lax.all_to_all(image, 'vis', 0, 0, tiled=True)  10.1 us
    pallas_call x1, Pallas kernels, on_device(): pl.pallas_call(rows_kernel, out_shape=message, in_specs=[VMEM, VMEM, VMEM...  5.96 us
    unnamed x14, local copies, waits for them, and re-layouts  2.64 us
    pallas_call x1, Pallas kernels, on_device(): pl.pallas_call(columns_ahead, out_shape=message, in_specs=[VMEM, HBM, VME...  2.09 us
    pallas_call x1, Pallas kernels, on_device(): pl.pallas_call(columns_back, out_shape=(jax.ShapeDtypeStruct((8, 32, 512)...  1.92 us

profile of v3, /device:TPU:0, one launch (start us, length us, event | category | flops | bytes accessed | tf_op | source)
XLA Modules:
  0.0 74.1 jit_solution(12195071419123087272)
XLA Ops:
  0.6 0.0 copy-start.1
  0.6 1.0 %copy-done.1 = f32[256,512]{1,0:T(8,128)S(1)} copy-done((f32[256,512]{1,0:T(8,128)S(1)}, f32[256,512]{1,0:T(8,128)}, u32[]{:S(2)}) %copy-start.1) | copy-done | bytes 524312
  1.7 0.0 copy-start.5
  1.7 0.0 copy-start.6
  1.7 0.7 shard_map.86
  2.4 12.5 %all_to_all.20.rx_ref = bf16[8,32,512]{2,1,0:T(8,128)(2,1)S(1)} all-to-all(bf16[8,32,512]{2,1,0:T(8,128)(2,1)S(1)} %shard_map.86), channel_id=1, replica_groups=mesh['facet'=16,'vis'=8] {'vis'}, dimensions={0} | all-to-all | bytes 524288 | tf_op jit(solution)/shard_map/all_to_all | solution.py:304
  14.9 0.0 copy-start.2
  14.9 0.9 %copy-done.2 = bf16[1,256,256]{2,1,0:T(8,128)(2,1)S(1)} copy-done((bf16[1,256,256]{2,1,0:T(8,128)(2,1)S(1)}, bf16[1,256,256]{2,1,0:T(8,128)(2,1)}, u32[]{:S(2)}) %copy-start.2) | copy-done | bytes 131096
  15.8 0.0 copy-start.4
  15.8 0.7 copy-done.4
  16.5 2.1 %shard_map.87 = bf16[128,3,4,128]{3,2,1,0:T(4,128)(2,1)S(1)} custom-call(bf16[8,32,512]{2,1,0:T(8,128)(2,1)S(1)} %all_to_all.20.rx_ref, bf16[1,256,256]{2,1,0:T(8,128)(2,1)S(1)} %copy-done.2, s32[2,128]{1,0:T(2,128)S(1)} %bitcast.5, bf16[10240,256]{1,0:T(8,128)(2,1)} %constant.6.clone.big_hbm), custom_call_target="tpu_custom_call" | custom-call | tf_op jit(solution)/shard_map/pallas_call | solution.py:305
  18.6 0.0 copy-start
  18.6 0.0 copy-start.3
  18.6 20.2 %all_to_all.21.rx_ref = bf16[128,3,4,128]{3,2,1,0:T(4,128)(2,1)S(1)} all-to-all(bf16[128,3,4,128]{3,2,1,0:T(4,128)(2,1)S(1)} %shard_map.87), channel_id=1, replica_groups=mesh['facet'=16,'vis'=8] {'facet','vis'}, dimensions={0} | all-to-all | bytes 786432 | tf_op jit(solution)/shard_map/all_to_all | solution.py:318
  38.8 0.0 copy-done.5
  38.8 0.0 copy-done.6
  38.9 6.0 %shard_map.88 = bf16[128,3,4,128]{3,2,1,0:T(4,128)(2,1)S(1)} custom-call(bf16[128,3,4,128]{3,2,1,0:T(4,128)(2,1)S(1)} %all_to_all.21.rx_ref, s32[2,128]{1,0:T(2,128)S(1)} %bitcast.6, s32[8,128]{1,0:T(8,128)S(1)} %bitcast.8, bf16[10240,256]{1,0:T(8,128)(2,1)} %constant.6.clone.big_hbm), custom_call_target="tpu_custom_call" | custom-call | tf_op jit(solution)/shard_map/pallas_call | solution.py:319
  44.8 16.4 %all_to_all.22.rx_ref = bf16[128,3,4,128]{3,2,1,0:T(4,128)(2,1)S(1)} all-to-all(bf16[128,3,4,128]{3,2,1,0:T(4,128)(2,1)S(1)} %shard_map.88), channel_id=1, replica_groups=mesh['facet'=16,'vis'=8] {'facet','vis'}, dimensions={0} | all-to-all | bytes 786432 | tf_op jit(solution)/shard_map/all_to_all | solution.py:344
  61.2 0.0 copy-done
  61.2 0.0 copy-done.3
  61.2 1.9 %shard_map.89 = (bf16[8,32,512]{2,1,0:T(8,128)(2,1)S(1)}, bf16[1,256,256]{2,1,0:T(8,128)(2,1)}) custom-call(bf16[128,3,4,128]{3,2,1,0:T(4,128)(2,1)S(1)} %all_to_all.22.rx_ref, s32[2,128]{1,0:T(2,128)S(1)} %bitcast.7, f32[16,512]{1,0:T(8,128)S(1)} %copy-done.3, bf16[512,1024]{1,0:T(8,128)(2,1)S(1)} %copy-done), custom_call_target="tpu_custom_call" | custom-call | tf_op jit(solution)/shard_map/pallas_call | solution.py:345
  63.1 10.1 %all_to_all.23 = bf16[8,32,512]{2,1,0:T(8,128)(2,1)S(1)} all-to-all(bf16[8,32,512]{2,1,0:T(8,128)(2,1)S(1)} %get-tuple-element.5), channel_id=1, replica_groups=mesh['facet'=16,'vis'=8] {'vis'}, dimensions={0} | all-to-all | bytes 524288 | tf_op jit(solution)/shard_map/all_to_all | solution.py:356
  73.2 0.9 %bitcast_convert_fusion = f32[256,512]{1,0:T(8,128)} fusion(bf16[8,32,512]{2,1,0:T(8,128)(2,1)S(1)} %all_to_all.23), kind=kLoop, calls=%fused_computation | loop fusion | flops 131072 | bytes 786432 | tf_op jit(solution)/shard_map/convert_element_type | solution.py:357
Async XLA Ops:
  0.6 1.0 %copy-start.1 = (f32[256,512]{1,0:T(8,128)S(1)}, f32[256,512]{1,0:T(8,128)}, u32[]{:S(2)}) copy-start(f32[256,512]{1,0:T(8,128)} %sky_hbm.1) | copy-start | bytes 1572868
  1.7 37.2 %copy-start.5 = (s32[128,2]{0,1:T(2,128)S(1)}, s32[128,2]{0,1:T(2,128)}, u32[]{:S(2)}) copy-start(s32[128,2]{0,1:T(2,128)} %param.9) | copy-start | bytes 3076
  1.7 37.2 %copy-start.6 = (s32[128,8]{0,1:T(8,128)S(1)}, s32[128,8]{0,1:T(8,128)}, u32[]{:S(2)}) copy-start(s32[128,8]{0,1:T(8,128)} %param.10) | copy-start | bytes 12292
  14.9 0.9 %copy-start.2 = (bf16[1,256,256]{2,1,0:T(8,128)(2,1)S(1)}, bf16[1,256,256]{2,1,0:T(8,128)(2,1)}, u32[]{:S(2)}) copy-start(bf16[1,256,256]{2,1,0:T(8,128)(2,1)} %obs_hbm.1) | copy-start | bytes 393220
  15.8 0.7 copy-start.4
  18.6 42.6 %copy-start = (bf16[512,1024]{1,0:T(8,128)(2,1)S(1)}, bf16[512,1024]{1,0:T(8,128)(2,1)}, u32[]{:S(2)}) copy-start(bf16[512,1024]{1,0:T(8,128)(2,1)} %constant.8.clone.tab_ref) | copy-start | bytes 3145732
  18.6 42.6 %copy-start.3 = (f32[16,512]{1,0:T(8,128)S(1)}, f32[16,512]{1,0:T(8,128)}, u32[]{:S(2)}) copy-start(f32[16,512]{1,0:T(8,128)} %constant.7.clone.tw_ref) | copy-start | bytes 98308

commit v4 on v3

--- a/solution.py
+++ b/solution.py
@@ -72,7 +72,7 @@
     return jnp.cos(angle), jnp.sin(angle)
 
 
-def tables(off_ref, asg_ref, ct_ref, st_ref, cg_ref, sg_ref, tc_ref, ts_ref, chosen_ref, bits_ref):
+def tables(off_ref, asg_ref, ct_ref, st_ref, cg_ref, sg_ref, tc_ref, ts_ref, chosen_ref, keep_ref):
     me = own_index()
     v_row = jnp.broadcast_to(off_ref[1:2, :], (16, 128))
     step = lax.broadcasted_iota(jnp.int32, (16, 128), 0)
@@ -90,30 +90,54 @@
     first = (me - u) & 127
     s0 = ((u + first - me) >> 7) & 31
     lane = lax.broadcasted_iota(jnp.int32, (128, 128), 0) & 31
-    for t in range(2):
-        hit = jnp.where(lane == ((s0 + t) & 31), 1.0, 0.0)
-        chosen_ref[128 * t : 128 * t + 128] = jnp.transpose(hit)
+    chosen = [jnp.transpose(jnp.where(lane == ((s0 + t) & 31), 1.0, 0.0)) for t in range(2)]
+    chosen_ref[...] = jnp.concatenate(chosen, axis=0).astype(BF16)
     asg = asg_ref[...]
     bits = jnp.sum(lax.shift_left(jnp.ones_like(asg), asg).astype(F32), axis=0, keepdims=True)
-    bits_ref[...] = jnp.transpose(jnp.broadcast_to(bits, (128, 128))).astype(jnp.int32)
-
-
-def round_image(sky_hbm, out_ref, held, sems):
+    bits = jnp.transpose(jnp.broadcast_to(bits, (128, 128))).astype(jnp.int32)
+    for f in range(16):
+        named = (lax.shift_right_logical(bits, f) & 1) == 1
+        for t in range(2):
+            at = 256 * f + 128 * t
+            keep_ref[at : at + 128] = jnp.where(named, chosen[t], 0.0).astype(BF16)
+
+
+def round_image(sky_hbm, out_hbm, held, done, sems):
     moves = [pltpu.make_async_copy(sky_hbm.at[pl.ds(64 * i, 64)], held.at[pl.ds(64 * i, 64)], sems.at[i]) for i in range(4)]
+    backs = [pltpu.make_async_copy(done.at[pl.ds(2 * i, 2)], out_hbm.at[pl.ds(2 * i, 2)], sems.at[4 + i]) for i in range(4)]
     for move in moves:
         move.start()
-    for i, move in enumerate(moves):
-        move.wait()
-        out_ref[2 * i : 2 * i + 2] = held[64 * i : 64 * i + 64].reshape(2, 32, 512).astype(BF16)
-
-
-def columns_ahead(rx_ref, obs_hbm, off_ref, big_hbm, out_ref, obs_ref, tab_ref, seen, sems):
-    moves = [pltpu.make_async_copy(obs_hbm, obs_ref, sems.at[0])]
+    for i in range(4):
+        moves[i].wait()
+        done[2 * i : 2 * i + 2] = held[64 * i : 64 * i + 64].reshape(2, 32, 512).astype(BF16)
+        backs[i].start()
+    for back in backs:
+        back.wait()
+
+
+def observed_columns(obs_ref, off_ref, big_hbm, out_ref, tab_ref, seen, sems):
+    moves = []
     for i in range(2):
         half = big_hbm.at[pl.ds(2 * N + 1024 * i, 1024)]
-        moves.append(pltpu.make_async_copy(half, tab_ref.at[:, pl.ds(256 * i, 256)], sems.at[1 + i]))
+        moves.append(pltpu.make_async_copy(half, tab_ref.at[:, pl.ds(256 * i, 256)], sems.at[i]))
     for move in moves:
         move.start()
+    u = off_ref[0:1, :]
+    place = lax.broadcasted_iota(jnp.int32, (1, 128), 1)
+    u = jnp.sum(jnp.where(place == own_index(), u, 0).astype(F32), axis=1, keepdims=True).astype(jnp.int32)
+    pick = selector(u)
+    rows = seen.reshape(1024, 128)
+    for t in range(2):
+        for ah in range(2):
+            quarter = obs_ref[0, 128 * ah : 128 * ah + 128, 128 * t : 128 * t + 128]
+            cols = lax.dot_general(pick, quarter, NT, preferred_element_type=F32)
+            rows[pl.ds(2 * t + ah, 128, stride=8), :] = cols
+    out_ref[...] = seen[...][:, 0:4].astype(BF16)
+    for move in moves:
+        move.wait()
+
+
+def columns_ahead(rx_ref, seen_ref, tab_ref, out_hbm, out_ref, sems):
     k2 = lax.broadcasted_iota(jnp.int32, (8, 512), 0)
     twist_c, twist_s = cos_sin(k2 * lax.broadcasted_iota(jnp.int32, (8, 512), 1))
     x = [rx_ref[j].astype(F32) for j in range(8)]
@@ -135,20 +159,10 @@
             zr, zi = re * c - im * s, re * s + im * c
         rows.append(jnp.concatenate([zr, zi], axis=1))
     left = jnp.concatenate(rows, axis=0).astype(BF16)
-    for move in moves:
-        move.wait()
     freq = jnp.dot(left, tab_ref[...], preferred_element_type=F32)
 
-    u = off_ref[0:1, :]
-    place = lax.broadcasted_iota(jnp.int32, (1, 128), 1)
-    u = jnp.sum(jnp.where(place == own_index(), u, 0).astype(F32), axis=1, keepdims=True).astype(jnp.int32)
-    pick = selector(u)
-    rows = seen.reshape(1024, 128)
-    for t in range(2):
-        for ah in range(2):
-            quarter = obs_ref[0, 128 * ah : 128 * ah + 128, 128 * t : 128 * t + 128]
-            cols = lax.dot_general(pick, quarter, NT, preferred_element_type=F32)
-            rows[pl.ds(2 * t + ah, 128, stride=8), :] = cols
+    out_ref[:, 2] = seen_ref[...]
+    leave = []
     group = lane_group(64)
     for qg in range(4):
         part = freq[:, 128 * qg : 128 * qg + 128].reshape(8, 4, 8, 128)
@@ -158,22 +172,26 @@
             tile = tiles[q4].reshape(8, 8, 128).astype(BF16)
             out_ref[at : at + 8, 0] = tile[:, 0:4]
             out_ref[at : at + 8, 1] = tile[:, 4:8]
-            out_ref[at : at + 8, 2] = seen[at : at + 8][:, 0:4].astype(BF16)
+        span = pl.ds(32 * qg, 32)
+        leave.append(pltpu.make_async_copy(out_ref.at[span], out_hbm.at[span], sems.at[qg]))
+        leave[qg].start()
+    for move in leave:
+        move.wait()
 
 
 def rows_kernel(
-    rx_ref, off_ref, asg_ref, big_hbm,
-    out_ref, ybuf, held, obs, rr, ct, st, cg, sg, tc_ref, ts_ref, chosen_ref, bits_ref, keep, zbuf, tab_ref, sem,
+    rx_ref, ct_ref, st_ref, cg_ref, sg_ref, tc_ref, ts_ref, chosen_ref, keep, big_hbm,
+    out_ref, ybuf, held, obs, rr, ct, st, cg, sg, zbuf, tab_ref, sem,
 ):
     fetch = pltpu.make_async_copy(big_hbm.at[pl.ds(0, 2 * N)], tab_ref, sem)
     fetch.start()
-    tables(off_ref, asg_ref, ct, st, cg, sg, tc_ref, ts_ref, chosen_ref, bits_ref)
+    ct[...], st[...], cg[...], sg[...] = ct_ref[...], st_ref[...], cg_ref[...], sg_ref[...]
     group = lax.broadcasted_iota(jnp.int32, (8, 8, 128), 2) >> 5
     got = rx_ref[...].astype(F32)
     held[:, 0:4] = got[:, 0]
     held[:, 4:8] = got[:, 1]
     obs[:, 0:4] = got[:, 2]
-    chosen = chosen_ref[...].astype(BF16)
+    chosen = chosen_ref[...]
     turn_c, turn_s = tc_ref[:8][None], ts_ref[:8][None]
     turn_ct = jnp.transpose(jnp.broadcast_to(tc_ref[:1], (256, 128)))
     turn_st = jnp.transpose(jnp.broadcast_to(ts_ref[:1], (256, 128)))
@@ -191,10 +209,6 @@
             ybuf[128 * t : 128 * t + 128, pl.ds(2 * at, 256)] = (half * c).astype(BF16)
             ybuf[128 * t : 128 * t + 128, pl.ds(2 * at + 256, 256)] = (half * s).astype(BF16)
         ct[...], st[...] = spin(c, s, turn_ct, turn_st)
-        named = (lax.shift_right_logical(bits_ref[...], f) & 1) == 1
-        for t in range(2):
-            kept = jnp.where(named, chosen_ref[128 * t : 128 * t + 128], 0.0)
-            keep[pl.ds(at + 128 * t, 128)] = kept.astype(BF16)
 
     fetch.wait()
     pred = jnp.dot(ybuf[...], tab_ref[...], preferred_element_type=F32) * (1.0 / 64.0)
@@ -235,7 +249,7 @@
         out_ref[pl.ds(8 * f, 8), 2] = rr[pl.ds(8 * f, 8)][:, 0:4].astype(BF16)
 
 
-def columns_back(rx_ref, off_ref, tw_ref, tab_ref, img_ref, res_ref, held, sent):
+def columns_back(rx_ref, tw_ref, tab_ref, img_hbm, held, img_ref, sems):
     got = rx_ref[...].astype(F32)
     held[:, 0:4] = got[:, 0]
     held[:, 4:8] = got[:, 1]
@@ -260,12 +274,20 @@
     plus, minus = re[0] + re[4], re[0] - re[4]
     even = [plus + a2, minus - b2, plus - a2, minus + b2]
     odd = [a1 + a3, HALF * (a1 - b1 - a3 - b3), b3 - b1, HALF * (a3 - a1 - b1 - b3)]
+    leave = []
     for j in range(4):
         img_ref[j] = (even[j] + odd[j]).astype(BF16)
         img_ref[j + 4] = (even[j] - odd[j]).astype(BF16)
-
+        for i in (j, j + 4):
+            leave.append(pltpu.make_async_copy(img_ref.at[i], img_hbm.at[i], sems.at[i]))
+            leave[-1].start()
+    for move in leave:
+        move.wait()
+
+
+def residual_block(rx_ref, off_ref, res_ref, sent):
     u = off_ref[0, own_index()]
-    sent[:, 0:4] = got[:, 2]
+    sent[:, 0:4] = rx_ref[...].astype(F32)[:, 2]
     rows = sent.reshape(1024, 128)
     pick = selector(u)
     for t in range(2):
@@ -279,7 +301,7 @@
 SMEM = pl.BlockSpec(memory_space=pltpu.SMEM)
 HBM = pl.BlockSpec(memory_space=pltpu.HBM)
 UNROLL, UNROLL1, UNROLL2 = 8, 8, 16
-L0, L1, L2 = 53, 53, 53
+L0, L1, L2 = 56, 50, 51
 
 
 def params(mebibytes):
@@ -291,35 +313,52 @@
     big = jnp.asarray(np.concatenate([row_table(), ahead[:, :256], ahead[:, 256:]], axis=0))
     everyone = ("facet", "vis")
     message = jax.ShapeDtypeStruct((128, 3, 4, 128), BF16)
+    plan_shapes = [(128, 256), (128, 256), (256, 128), (256, 128), (16, 128), (16, 128)]
     offsets, assignments = offsets.T, assignments.T
 
     strips = pl.pallas_call(
         round_image,
         out_shape=jax.ShapeDtypeStruct((8, 32, 512), BF16),
         in_specs=[HBM],
-        out_specs=VMEM,
-        scratch_shapes=[pltpu.VMEM((256, 512), F32), pltpu.SemaphoreType.DMA((4,))],
+        out_specs=HBM,
+        scratch_shapes=[pltpu.VMEM((256, 512), F32), pltpu.VMEM((8, 32, 512), BF16), pltpu.SemaphoreType.DMA((8,))],
         compiler_params=params(L0),
     )(sky_image)
     strips = lax.all_to_all(strips, "vis", 0, 0, tiled=True)
+    seen, ahead_table = pl.pallas_call(
+        observed_columns,
+        out_shape=(jax.ShapeDtypeStruct((128, 4, 128), BF16), jax.ShapeDtypeStruct((1024, 512), BF16)),
+        in_specs=[VMEM, VMEM, HBM],
+        out_specs=(VMEM, VMEM),
+        scratch_shapes=[pltpu.VMEM((128, 8, 128), F32), pltpu.SemaphoreType.DMA((2,))],
+        compiler_params=params(L1),
+        cost_estimate=pl.CostEstimate(flops=10**9, bytes_accessed=4 * 10**6, transcendentals=0),
+    )(observed, offsets, big)
     sent = pl.pallas_call(
         columns_ahead,
         out_shape=message,
-        in_specs=[VMEM, HBM, VMEM, HBM],
-        out_specs=VMEM,
-        scratch_shapes=[
-            pltpu.VMEM((1, SUB, SUB), BF16),
-            pltpu.VMEM((1024, 512), BF16),
-            pltpu.VMEM((128, 8, 128), F32),
-            pltpu.SemaphoreType.DMA((3,)),
-        ],
-        compiler_params=params(L1),
-    )(strips, observed, offsets, big)
+        in_specs=[VMEM, VMEM, VMEM],
+        out_specs=HBM,
+        scratch_shapes=[pltpu.VMEM((128, 3, 4, 128), BF16), pltpu.SemaphoreType.DMA((4,))],
+        compiler_params=params(32),
+    )(strips, seen, ahead_table)
     got = lax.all_to_all(sent, everyone, 0, 0, tiled=True)
+    plan = pl.pallas_call(
+        tables,
+        out_shape=(
+            *[jax.ShapeDtypeStruct(shape, F32) for shape in plan_shapes],
+            jax.ShapeDtypeStruct((256, 128), BF16),
+            jax.ShapeDtypeStruct((N, 128), BF16),
+        ),
+        in_specs=[VMEM, VMEM],
+        out_specs=(VMEM,) * 8,
+        compiler_params=params(32),
+        cost_estimate=pl.CostEstimate(flops=10**9, bytes_accessed=4 * 10**6, transcendentals=10**4),
+    )(offsets, assignments)
     sent = pl.pallas_call(
         rows_kernel,
         out_shape=message,
-        in_specs=[VMEM, VMEM, VMEM, HBM],
+        in_specs=[VMEM] * 9 + [HBM],
         out_specs=VMEM,
         scratch_shapes=[
             pltpu.VMEM((256, 2 * N), BF16),
@@ -330,30 +369,35 @@
             pltpu.VMEM((128, 256), F32),
             pltpu.VMEM((256, 128), F32),
             pltpu.VMEM((256, 128), F32),
-            pltpu.VMEM((16, 128), F32),
-            pltpu.VMEM((16, 128), F32),
-            pltpu.VMEM((256, 128), F32),
-            pltpu.VMEM((128, 128), jnp.int32),
-            pltpu.VMEM((N, 128), BF16),
             pltpu.VMEM((N, 256), BF16),
             pltpu.VMEM((2 * N, 256), BF16),
             pltpu.SemaphoreType.DMA,
         ],
         compiler_params=params(L2),
-    )(got, offsets, assignments, big)
+    )(got, *plan, big)
     got = lax.all_to_all(sent, everyone, 0, 0, tiled=True)
-    image, resid = pl.pallas_call(
+    image = pl.pallas_call(
         columns_back,
-        out_shape=(
-            jax.ShapeDtypeStruct((8, 32, 512), BF16),
-            jax.ShapeDtypeStruct((1, SUB, SUB), BF16),
-        ),
-        in_specs=[VMEM, SMEM, VMEM, VMEM],
-        out_specs=(VMEM, VMEM),
-        scratch_shapes=[pltpu.VMEM((128, 8, 128), F32), pltpu.VMEM((128, 8, 128), F32)],
+        out_shape=jax.ShapeDtypeStruct((8, 32, 512), BF16),
+        in_specs=[VMEM, VMEM, VMEM],
+        out_specs=HBM,
+        scratch_shapes=[
+            pltpu.VMEM((128, 8, 128), F32),
+            pltpu.VMEM((8, 32, 512), BF16),
+            pltpu.SemaphoreType.DMA((8,)),
+        ],
         compiler_params=params(16),
-    )(got, offsets, jnp.asarray(twiddle), jnp.asarray(back))
+    )(got, jnp.asarray(twiddle), jnp.asarray(back))
     image = lax.all_to_all(image, "vis", 0, 0, tiled=True)
+    resid = pl.pallas_call(
+        residual_block,
+        out_shape=jax.ShapeDtypeStruct((1, SUB, SUB), BF16),
+        in_specs=[VMEM, SMEM],
+        out_specs=VMEM,
+        scratch_shapes=[pltpu.VMEM((128, 8, 128), F32)],
+        compiler_params=params(16),
+        cost_estimate=pl.CostEstimate(flops=10**9, bytes_accessed=4 * 10**6, transcendentals=0),
+    )(got, offsets)
     return resid, image.reshape(256, 512).astype(F32)
 
 

time: 74.5 us -> 73.4 us (0.985)
  blocking collectives: 59.2 us -> 16.4 us
  waiting for transfers between devices: 0 us -> 21.9 us
  starting transfers between devices: 0 us -> 17.4 us
  Pallas kernels: 10.7 us -> 14 us
  local copies, waits for them, and re-layouts: 2.64 us -> 1.6 us
    all_to_all x2 -> x0, blocking collectives: 22.6 us -> none  [the longest x1 12.5 us: on_device(): strips = lax.all_to_all(strips, 'vis', 0, 0, tiled=True)]
    all_to_all x0 -> x3, waiting for transfers between devices: none -> 21.9 us  [the longest x1 11.4 us: on_device(): got = lax.all_to_all(sent, everyone, 0, 0, tiled=True)]
    all_to_all x2 -> x1, blocking collectives: 36.6 us -> 16.4 us  [on_device(): got = lax.all_to_all(sent, everyone, 0, 0, tiled=True)]
    all_to_all x0 -> x3, starting transfers between devices: none -> 17.4 us  [the longest x1 8.47 us: on_device(): got = lax.all_to_all(sent, everyone, 0, 0, tiled=True)]
    pallas_call x3 -> x6, Pallas kernels: 9.98 us -> 12.2 us  [the longest x1 5.98 us: on_device(): pl.pallas_call(rows_kernel, out_shape=message, in_specs=[VMEM] * 9 + [HBM...]
    pallas_call x1, Pallas kernels: 0.73 us -> 1.81 us  [on_device(): pl.pallas_call(round_image, out_shape=jax.ShapeDtypeStruct((8, 32, 512),...]
    unnamed x14 -> x12, local copies, waits for them, and re-layouts: 2.64 us -> 1.6 us
  transfers between devices with their start and end apart: 0 -> 3, of which waited for: 0 -> 3; matrix products, arithmetic and copies ran while one was open for 0% -> 0% of each run, Pallas kernels for 0% -> 4%
where the time goes in v4:
time: 73.4 us; the launch traced here: 72.9 us
  waiting for transfers between devices  21.9 us (30%)
  starting transfers between devices  17.4 us (24%)
  blocking collectives  16.4 us (22%)
  Pallas kernels  14 us (19%)
  local copies, waits for them, and re-layouts  1.6 us (2%)
  other arithmetic  0.87 us (1%)
  between operations  0.75 us (1%)
    all_to_all x1, blocking collectives, on_device(): got = lax.all_to_all(sent, everyone, 0, 0, tiled=True)  16.4 us
    all_to_all x1, waiting for transfers between devices, on_device(): got = lax.all_to_all(sent, everyone, 0, 0, tiled=True)  11.4 us
    all_to_all x1, starting transfers between devices, on_device(): got = lax.all_to_all(sent, everyone, 0, 0, tiled=True)  8.47 us
    all_to_all x1, waiting for transfers between devices, on_device(): image = lax.all_to_all(image, 'vis', 0, 0, tiled=True)  6.11 us
    pallas_call x1, Pallas kernels, on_device(): pl.pallas_call(rows_kernel, out_shape=message, in_specs=[VMEM] * 9 + [HBM...  5.98 us
    all_to_all x1, starting transfers between devices, on_device(): strips = lax.all_to_all(strips, 'vis', 0, 0, tiled=True)  5.49 us
    all_to_all x1, waiting for transfers between devices, on_device(): strips = lax.all_to_all(strips, 'vis', 0, 0, tiled=True)  4.41 us
    all_to_all x1, starting transfers between devices, on_device(): image = lax.all_to_all(image, 'vis', 0, 0, tiled=True)  3.42 us
  transfers between devices with their start and end apart: 3, of which 3 were waited for; matrix products, arithmetic and copies ran while one was open for 0% of the time, Pallas kernels for 4%

profile of v4, /device:TPU:0, one launch (start us, length us, event | category | flops | bytes accessed | tf_op | source)
XLA Modules:
  0.0 72.9 jit_solution(10454102421719681070)
XLA Ops:
  0.6 0.0 copy-start.4
  0.6 0.0 copy-start.5
  0.7 1.8 %shard_map.86 = bf16[8,32,512]{2,1,0:T(8,128)(2,1)} custom-call(f32[256,512]{1,0:T(8,128)} %sky_hbm.1), custom_call_target="tpu_custom_call" | custom-call | tf_op jit(solution)/shard_map/pallas_call | solution.py:319
  2.5 5.5 %all-to-all-start = ((bf16[8,32,512]{2,1,0:T(8,128)(2,1)}), bf16[8,32,512]{2,1,0:T(8,128)(2,1)S(1)}, u32[]{:S(2)}, u32[]{:S(2)}) async-start(bf16[8,32,512]{2,1,0:T(8,128)(2,1)} %shard_map.86), calls=%async_computation | async-start | bytes 524288 | tf_op jit(solution)/shard_map/all_to_all | solution.py:327
  8.0 0.0 copy-start.1
  8.0 0.9 %copy-done.1 = bf16[1,256,256]{2,1,0:T(8,128)(2,1)S(1)} copy-done((bf16[1,256,256]{2,1,0:T(8,128)(2,1)S(1)}, bf16[1,256,256]{2,1,0:T(8,128)(2,1)}, u32[]{:S(2)}) %copy-start.1) | copy-done | bytes 131096
  8.9 0.0 copy-start.3
  8.9 0.7 copy-done.3
  9.5 1.2 %shard_map.87 = (bf16[128,4,128]{2,1,0:T(4,128)(2,1)S(1)}, bf16[1024,512]{1,0:T(8,128)(2,1)S(1)}) custom-call(bf16[1,256,256]{2,1,0:T(8,128)(2,1)S(1)} %copy-done.1, s32[2,128]{1,0:T(2,128)S(1)} %bitcast.5, bf16[10240,256]{1,0:T(8,128)(2,1)} %constant.6.clone.big_hbm), custom_call_target="tpu_custom_call" | custom-call | flops 1000000000 | bytes 4000000 | tf_op jit(solution)/shard_map/pallas_call | solution.py:328
  10.8 4.4 %all-to-all-done.rx_ref = bf16[8,32,512]{2,1,0:T(8,128)(2,1)S(1)} async-done(((bf16[8,32,512]{2,1,0:T(8,128)(2,1)}), bf16[8,32,512]{2,1,0:T(8,128)(2,1)S(1)}, u32[]{:S(2)}, u32[]{:S(2)}) %all-to-all-start) | async-done | bytes 262176 | tf_op jit(solution)/shard_map/all_to_all | solution.py:327
  15.2 1.6 %shard_map.88 = bf16[128,3,4,128]{3,2,1,0:T(4,128)(2,1)} custom-call(bf16[8,32,512]{2,1,0:T(8,128)(2,1)S(1)} %all-to-all-done.rx_ref, bf16[128,4,128]{2,1,0:T(4,128)(2,1)S(1)} %get-tuple-element.12.seen_ref, bf16[1024,512]{1,0:T(8,128)(2,1)S(1)} %get-tuple-element.13.tab_ref), custom_call_target="tpu_custom_call" | custom-call | tf_op jit(solution)/shard_map/pallas_call | solution.py:337
  16.8 8.5 %all-to-all-start.1 = ((bf16[128,3,4,128]{3,2,1,0:T(4,128)(2,1)}), bf16[128,3,4,128]{3,2,1,0:T(4,128)(2,1)S(1)}, u32[]{:S(2)}, u32[]{:S(2)}) async-start(bf16[128,3,4,128]{3,2,1,0:T(4,128)(2,1)} %shard_map.88), calls=%async_computation.1 | async-start | bytes 786432 | tf_op jit(solution)/shard_map/all_to_all | solution.py:345
  25.3 0.0 copy-done.4
  25.3 0.0 copy-done.5
  25.3 0.0 copy-start
  25.3 0.0 copy-start.2
  25.3 0.5 shard_map.89
  25.8 11.4 %all-to-all-done.1.rx_ref = bf16[128,3,4,128]{3,2,1,0:T(4,128)(2,1)S(1)} async-done(((bf16[128,3,4,128]{3,2,1,0:T(4,128)(2,1)}), bf16[128,3,4,128]{3,2,1,0:T(4,128)(2,1)S(1)}, u32[]{:S(2)}, u32[]{:S(2)}) %all-to-all-start.1) | async-done | bytes 393248 | tf_op jit(solution)/shard_map/all_to_all | solution.py:345
  37.2 6.0 %shard_map.90 = bf16[128,3,4,128]{3,2,1,0:T(4,128)(2,1)S(1)} custom-call(bf16[128,3,4,128]{3,2,1,0:T(4,128)(2,1)S(1)} %all-to-all-done.1.rx_ref, f32[128,256]{1,0:T(8,128)S(1)} %get-tuple-element.14.ct_ref, f32[128,256]{1,0:T(8,128)S(1)} %get-tuple-element.15.st_ref, f32[256,128]{1,0:T(8,128)S(1)} %get-tuple-element.16.cg_ref, ...), custom_call_target="tpu_custom_call" | custom-call | tf_op jit(solution)/shard_map/pallas_call | solution.py:358
  43.2 16.4 %all_to_all.20.rx_ref = bf16[128,3,4,128]{3,2,1,0:T(4,128)(2,1)S(1)} all-to-all(bf16[128,3,4,128]{3,2,1,0:T(4,128)(2,1)S(1)} %shard_map.90), channel_id=1, replica_groups=mesh['facet'=16,'vis'=8] {'facet','vis'}, dimensions={0} | all-to-all | bytes 786432 | tf_op jit(solution)/shard_map/all_to_all | solution.py:378
  59.6 0.0 copy-done
  59.6 0.0 copy-done.2
  59.6 1.4 %shard_map.92 = bf16[8,32,512]{2,1,0:T(8,128)(2,1)} custom-call(bf16[128,3,4,128]{3,2,1,0:T(4,128)(2,1)S(1)} %all_to_all.20.rx_ref, f32[16,512]{1,0:T(8,128)S(1)} %copy-done.2, bf16[512,1024]{1,0:T(8,128)(2,1)S(1)} %copy-done), custom_call_target="tpu_custom_call" | custom-call | tf_op jit(solution)/shard_map/pallas_call | solution.py:379
  61.0 3.4 %all-to-all-start.3 = ((bf16[8,32,512]{2,1,0:T(8,128)(2,1)}), bf16[8,32,512]{2,1,0:T(8,128)(2,1)S(1)}, u32[]{:S(2)}, u32[]{:S(2)}) async-start(bf16[8,32,512]{2,1,0:T(8,128)(2,1)} %shard_map.92), calls=%async_computation.3 | async-start | bytes 524288 | tf_op jit(solution)/shard_map/all_to_all | solution.py:391
  64.4 1.5 %shard_map.91 = bf16[1,256,256]{2,1,0:T(8,128)(2,1)} custom-call(bf16[128,3,4,128]{3,2,1,0:T(4,128)(2,1)S(1)} %all_to_all.20.rx_ref, s32[2,128]{1,0:T(2,128)S(1)} %bitcast.7), custom_call_target="tpu_custom_call" | custom-call | flops 1000000000 | bytes 4000000 | tf_op jit(solution)/shard_map/pallas_call | solution.py:392
  65.9 6.1 %all-to-all-done.3 = bf16[8,32,512]{2,1,0:T(8,128)(2,1)S(1)} async-done(((bf16[8,32,512]{2,1,0:T(8,128)(2,1)}), bf16[8,32,512]{2,1,0:T(8,128)(2,1)S(1)}, u32[]{:S(2)}, u32[]{:S(2)}) %all-to-all-start.3) | async-done | bytes 262176 | tf_op jit(solution)/shard_map/all_to_all | solution.py:391
  72.1 0.9 %bitcast_convert_fusion = f32[256,512]{1,0:T(8,128)} fusion(bf16[8,32,512]{2,1,0:T(8,128)(2,1)S(1)} %all-to-all-done.3), kind=kLoop, calls=%fused_computation | loop fusion | flops 131072 | bytes 786432 | tf_op jit(solution)/shard_map/convert_element_type | solution.py:401
Async XLA Ops:
  0.6 24.6 %copy-start.4 = (s32[128,2]{0,1:T(2,128)S(1)}, s32[128,2]{0,1:T(2,128)}, u32[]{:S(2)}) copy-start(s32[128,2]{0,1:T(2,128)} %param.9) | copy-start | bytes 3076
  0.6 24.6 %copy-start.5 = (s32[128,8]{0,1:T(8,128)S(1)}, s32[128,8]{0,1:T(8,128)}, u32[]{:S(2)}) copy-start(s32[128,8]{0,1:T(8,128)} %param.10) | copy-start | bytes 12292
  2.5 12.7 %all-to-all-start = ((bf16[8,32,512]{2,1,0:T(8,128)(2,1)}), bf16[8,32,512]{2,1,0:T(8,128)(2,1)S(1)}, u32[]{:S(2)}, u32[]{:S(2)}) async-start(bf16[8,32,512]{2,1,0:T(8,128)(2,1)} %shard_map.86), calls=%async_computation | async-start | bytes 524288 | tf_op jit(solution)/shard_map/all_to_all | solution.py:327
  8.0 0.9 %copy-start.1 = (bf16[1,256,256]{2,1,0:T(8,128)(2,1)S(1)}, bf16[1,256,256]{2,1,0:T(8,128)(2,1)}, u32[]{:S(2)}) copy-start(bf16[1,256,256]{2,1,0:T(8,128)(2,1)} %obs_ref.1) | copy-start | bytes 393220
  8.9 0.7 copy-start.3
  16.8 20.4 %all-to-all-start.1 = ((bf16[128,3,4,128]{3,2,1,0:T(4,128)(2,1)}), bf16[128,3,4,128]{3,2,1,0:T(4,128)(2,1)S(1)}, u32[]{:S(2)}, u32[]{:S(2)}) async-start(bf16[128,3,4,128]{3,2,1,0:T(4,128)(2,1)} %shard_map.88), calls=%async_computation.1 | async-start | bytes 786432 | tf_op jit(solution)/shard_map/all_to_all | solution.py:345
  25.3 34.3 %copy-start = (bf16[512,1024]{1,0:T(8,128)(2,1)S(1)}, bf16[512,1024]{1,0:T(8,128)(2,1)}, u32[]{:S(2)}) copy-start(bf16[512,1024]{1,0:T(8,128)(2,1)} %constant.8.clone.tab_ref) | copy-start | bytes 3145732
  25.3 34.3 %copy-start.2 = (f32[16,512]{1,0:T(8,128)S(1)}, f32[16,512]{1,0:T(8,128)}, u32[]{:S(2)}) copy-start(f32[16,512]{1,0:T(8,128)} %constant.7.clone.tw_ref) | copy-start | bytes 98308
  61.0 11.0 %all-to-all-start.3 = ((bf16[8,32,512]{2,1,0:T(8,128)(2,1)}), bf16[8,32,512]{2,1,0:T(8,128)(2,1)S(1)}, u32[]{:S(2)}, u32[]{:S(2)}) async-start(bf16[8,32,512]{2,1,0:T(8,128)(2,1)} %shard_map.92), calls=%async_computation.3 | async-start | bytes 524288 | tf_op jit(solution)/shard_map/all_to_all | solution.py:391

commit v5 on v3

--- a/solution.py
+++ b/solution.py
@@ -55,6 +55,12 @@
         mixed = jnp.where(group < 2, jnp.where(group == 0, moved[0], moved[1]), jnp.where(group == 2, moved[2], moved[3]))
         out.append(mixed)
     return out
+
+
+def own_column(off_ref):
+    place = lax.broadcasted_iota(jnp.int32, (1, 128), 1)
+    own = jnp.where(place == own_index(), off_ref[0:1, :], 0).astype(F32)
+    return jnp.sum(own, axis=1, keepdims=True).astype(jnp.int32)
 
 
 def selector(u):
@@ -98,22 +104,44 @@
     bits_ref[...] = jnp.transpose(jnp.broadcast_to(bits, (128, 128))).astype(jnp.int32)
 
 
-def round_image(sky_hbm, out_ref, held, sems):
+def round_image(sky_hbm, out_hbm, held, done, sems):
     moves = [pltpu.make_async_copy(sky_hbm.at[pl.ds(64 * i, 64)], held.at[pl.ds(64 * i, 64)], sems.at[i]) for i in range(4)]
+    backs = [pltpu.make_async_copy(done.at[pl.ds(2 * i, 2)], out_hbm.at[pl.ds(2 * i, 2)], sems.at[4 + i]) for i in range(4)]
     for move in moves:
         move.start()
-    for i, move in enumerate(moves):
-        move.wait()
-        out_ref[2 * i : 2 * i + 2] = held[64 * i : 64 * i + 64].reshape(2, 32, 512).astype(BF16)
-
-
-def columns_ahead(rx_ref, obs_hbm, off_ref, big_hbm, out_ref, obs_ref, tab_ref, seen, sems):
-    moves = [pltpu.make_async_copy(obs_hbm, obs_ref, sems.at[0])]
+    for i in range(4):
+        moves[i].wait()
+        done[2 * i : 2 * i + 2] = held[64 * i : 64 * i + 64].reshape(2, 32, 512).astype(BF16)
+        backs[i].start()
+    for back in backs:
+        back.wait()
+
+
+def observed_columns(
+    obs_ref, off_ref, asg_ref, big_hbm,
+    out_ref, tab_ref, ct_ref, st_ref, cg_ref, sg_ref, tc_ref, ts_ref, chosen_ref, bits_ref, seen, sems,
+):
+    moves = []
     for i in range(2):
         half = big_hbm.at[pl.ds(2 * N + 1024 * i, 1024)]
-        moves.append(pltpu.make_async_copy(half, tab_ref.at[:, pl.ds(256 * i, 256)], sems.at[1 + i]))
+        moves.append(pltpu.make_async_copy(half, tab_ref.at[:, pl.ds(256 * i, 256)], sems.at[i]))
     for move in moves:
         move.start()
+    tables(off_ref, asg_ref, ct_ref, st_ref, cg_ref, sg_ref, tc_ref, ts_ref, chosen_ref, bits_ref)
+    u = own_column(off_ref)
+    pick = selector(u)
+    rows = seen.reshape(1024, 128)
+    for t in range(2):
+        for ah in range(2):
+            quarter = obs_ref[0, 128 * ah : 128 * ah + 128, 128 * t : 128 * t + 128]
+            cols = lax.dot_general(pick, quarter, NT, preferred_element_type=F32)
+            rows[pl.ds(2 * t + ah, 128, stride=8), :] = cols
+    out_ref[...] = seen[...][:, 0:4].astype(BF16)
+    for move in moves:
+        move.wait()
+
+
+def columns_ahead(rx_ref, seen_ref, tab_ref, out_ref):
     k2 = lax.broadcasted_iota(jnp.int32, (8, 512), 0)
     twist_c, twist_s = cos_sin(k2 * lax.broadcasted_iota(jnp.int32, (8, 512), 1))
     x = [rx_ref[j].astype(F32) for j in range(8)]
@@ -135,20 +163,9 @@
             zr, zi = re * c - im * s, re * s + im * c
         rows.append(jnp.concatenate([zr, zi], axis=1))
     left = jnp.concatenate(rows, axis=0).astype(BF16)
-    for move in moves:
-        move.wait()
     freq = jnp.dot(left, tab_ref[...], preferred_element_type=F32)
 
-    u = off_ref[0:1, :]
-    place = lax.broadcasted_iota(jnp.int32, (1, 128), 1)
-    u = jnp.sum(jnp.where(place == own_index(), u, 0).astype(F32), axis=1, keepdims=True).astype(jnp.int32)
-    pick = selector(u)
-    rows = seen.reshape(1024, 128)
-    for t in range(2):
-        for ah in range(2):
-            quarter = obs_ref[0, 128 * ah : 128 * ah + 128, 128 * t : 128 * t + 128]
-            cols = lax.dot_general(pick, quarter, NT, preferred_element_type=F32)
-            rows[pl.ds(2 * t + ah, 128, stride=8), :] = cols
+    out_ref[:, 2] = seen_ref[...]
     group = lane_group(64)
     for qg in range(4):
         part = freq[:, 128 * qg : 128 * qg + 128].reshape(8, 4, 8, 128)
@@ -158,16 +175,15 @@
             tile = tiles[q4].reshape(8, 8, 128).astype(BF16)
             out_ref[at : at + 8, 0] = tile[:, 0:4]
             out_ref[at : at + 8, 1] = tile[:, 4:8]
-            out_ref[at : at + 8, 2] = seen[at : at + 8][:, 0:4].astype(BF16)
 
 
 def rows_kernel(
-    rx_ref, off_ref, asg_ref, big_hbm,
-    out_ref, ybuf, held, obs, rr, ct, st, cg, sg, tc_ref, ts_ref, chosen_ref, bits_ref, keep, zbuf, tab_ref, sem,
+    rx_ref, ct_ref, st_ref, cg_ref, sg_ref, tc_ref, ts_ref, chosen_ref, bits_ref, big_hbm,
+    out_ref, ybuf, held, obs, rr, ct, st, cg, sg, keep, zbuf, tab_ref, sem,
 ):
     fetch = pltpu.make_async_copy(big_hbm.at[pl.ds(0, 2 * N)], tab_ref, sem)
     fetch.start()
-    tables(off_ref, asg_ref, ct, st, cg, sg, tc_ref, ts_ref, chosen_ref, bits_ref)
+    ct[...], st[...], cg[...], sg[...] = ct_ref[...], st_ref[...], cg_ref[...], sg_ref[...]
     group = lax.broadcasted_iota(jnp.int32, (8, 8, 128), 2) >> 5
     got = rx_ref[...].astype(F32)
     held[:, 0:4] = got[:, 0]
@@ -235,10 +251,21 @@
         out_ref[pl.ds(8 * f, 8), 2] = rr[pl.ds(8 * f, 8)][:, 0:4].astype(BF16)
 
 
-def columns_back(rx_ref, off_ref, tw_ref, tab_ref, img_ref, res_ref, held, sent):
+def columns_back(rx_ref, off_ref, tw_ref, tab_ref, img_ref, res_hbm, held, sent, res_ref, sem):
     got = rx_ref[...].astype(F32)
     held[:, 0:4] = got[:, 0]
     held[:, 4:8] = got[:, 1]
+    u = own_column(off_ref)
+    sent[:, 0:4] = got[:, 2]
+    rows = sent.reshape(1024, 128)
+    pick = selector(u)
+    for t in range(2):
+        for ah in range(2):
+            quarter = jnp.transpose(rows[pl.ds(2 * t + ah, 128, stride=8), :]).astype(BF16)
+            quarter = jnp.dot(quarter, pick, preferred_element_type=F32).astype(BF16)
+            res_ref[0, 128 * ah : 128 * ah + 128, 128 * t : 128 * t + 128] = quarter
+    leave = pltpu.make_async_copy(res_ref, res_hbm, sem)
+    leave.start()
     tiles = held[...].reshape(16, 64, 128)
     group = lane_group(64)
     wide = [[None] * 4 for _ in range(4)]
@@ -263,23 +290,13 @@
     for j in range(4):
         img_ref[j] = (even[j] + odd[j]).astype(BF16)
         img_ref[j + 4] = (even[j] - odd[j]).astype(BF16)
-
-    u = off_ref[0, own_index()]
-    sent[:, 0:4] = got[:, 2]
-    rows = sent.reshape(1024, 128)
-    pick = selector(u)
-    for t in range(2):
-        for ah in range(2):
-            quarter = jnp.transpose(rows[pl.ds(2 * t + ah, 128, stride=8), :]).astype(BF16)
-            quarter = jnp.dot(quarter, pick, preferred_element_type=F32).astype(BF16)
-            res_ref[0, 128 * ah : 128 * ah + 128, 128 * t : 128 * t + 128] = quarter
+    leave.wait()
 
 
 VMEM = pl.BlockSpec(memory_space=pltpu.VMEM)
-SMEM = pl.BlockSpec(memory_space=pltpu.SMEM)
 HBM = pl.BlockSpec(memory_space=pltpu.HBM)
 UNROLL, UNROLL1, UNROLL2 = 8, 8, 16
-L0, L1, L2 = 53, 53, 53
+L0, L1, L2 = 56, 50, 52
 
 
 def params(mebibytes):
@@ -297,29 +314,38 @@
         round_image,
         out_shape=jax.ShapeDtypeStruct((8, 32, 512), BF16),
         in_specs=[HBM],
-        out_specs=VMEM,
-        scratch_shapes=[pltpu.VMEM((256, 512), F32), pltpu.SemaphoreType.DMA((4,))],
+        out_specs=HBM,
+        scratch_shapes=[pltpu.VMEM((256, 512), F32), pltpu.VMEM((8, 32, 512), BF16), pltpu.SemaphoreType.DMA((8,))],
         compiler_params=params(L0),
     )(sky_image)
     strips = lax.all_to_all(strips, "vis", 0, 0, tiled=True)
+    plan_shapes = [(128, 256), (128, 256), (256, 128), (256, 128), (16, 128), (16, 128), (256, 128)]
+    seen, ahead_table, *plan = pl.pallas_call(
+        observed_columns,
+        out_shape=(
+            jax.ShapeDtypeStruct((128, 4, 128), BF16),
+            jax.ShapeDtypeStruct((1024, 512), BF16),
+            *[jax.ShapeDtypeStruct(shape, F32) for shape in plan_shapes],
+            jax.ShapeDtypeStruct((128, 128), jnp.int32),
+        ),
+        in_specs=[VMEM, VMEM, VMEM, HBM],
+        out_specs=(VMEM,) * 10,
+        scratch_shapes=[pltpu.VMEM((128, 8, 128), F32), pltpu.SemaphoreType.DMA((2,))],
+        compiler_params=params(L1),
+        cost_estimate=pl.CostEstimate(flops=10**9, bytes_accessed=4 * 10**6, transcendentals=0),
+    )(observed, offsets, assignments, big)
     sent = pl.pallas_call(
         columns_ahead,
         out_shape=message,
-        in_specs=[VMEM, HBM, VMEM, HBM],
+        in_specs=[VMEM, VMEM, VMEM],
         out_specs=VMEM,
-        scratch_shapes=[
-            pltpu.VMEM((1, SUB, SUB), BF16),
-            pltpu.VMEM((1024, 512), BF16),
-            pltpu.VMEM((128, 8, 128), F32),
-            pltpu.SemaphoreType.DMA((3,)),
-        ],
-        compiler_params=params(L1),
-    )(strips, observed, offsets, big)
+        compiler_params=params(32),
+    )(strips, seen, ahead_table)
     got = lax.all_to_all(sent, everyone, 0, 0, tiled=True)
     sent = pl.pallas_call(
         rows_kernel,
         out_shape=message,
-        in_specs=[VMEM, VMEM, VMEM, HBM],
+        in_specs=[VMEM] * 9 + [HBM],
         out_specs=VMEM,
         scratch_shapes=[
             pltpu.VMEM((256, 2 * N), BF16),
@@ -330,17 +356,13 @@
             pltpu.VMEM((128, 256), F32),
             pltpu.VMEM((256, 128), F32),
             pltpu.VMEM((256, 128), F32),
-            pltpu.VMEM((16, 128), F32),
-            pltpu.VMEM((16, 128), F32),
-            pltpu.VMEM((256, 128), F32),
-            pltpu.VMEM((128, 128), jnp.int32),
             pltpu.VMEM((N, 128), BF16),
             pltpu.VMEM((N, 256), BF16),
             pltpu.VMEM((2 * N, 256), BF16),
             pltpu.SemaphoreType.DMA,
         ],
         compiler_params=params(L2),
-    )(got, offsets, assignments, big)
+    )(got, *plan, big)
     got = lax.all_to_all(sent, everyone, 0, 0, tiled=True)
     image, resid = pl.pallas_call(
         columns_back,
@@ -348,9 +370,14 @@
             jax.ShapeDtypeStruct((8, 32, 512), BF16),
             jax.ShapeDtypeStruct((1, SUB, SUB), BF16),
         ),
-        in_specs=[VMEM, SMEM, VMEM, VMEM],
-        out_specs=(VMEM, VMEM),
-        scratch_shapes=[pltpu.VMEM((128, 8, 128), F32), pltpu.VMEM((128, 8, 128), F32)],
+        in_specs=[VMEM, VMEM, VMEM, VMEM],
+        out_specs=(VMEM, HBM),
+        scratch_shapes=[
+            pltpu.VMEM((128, 8, 128), F32),
+            pltpu.VMEM((128, 8, 128), F32),
+            pltpu.VMEM((1, SUB, SUB), BF16),
+            pltpu.SemaphoreType.DMA,
+        ],
         compiler_params=params(16),
     )(got, offsets, jnp.asarray(twiddle), jnp.asarray(back))
     image = lax.all_to_all(image, "vis", 0, 0, tiled=True)

time: 74.5 us -> 71.2 us (0.956)
  blocking collectives: 59.2 us -> 46.7 us
  starting transfers between devices: 0 us -> 5.49 us
  waiting for transfers between devices: 0 us -> 3.56 us
    all_to_all x1 -> x0, blocking collectives: 12.5 us -> none  [on_device(): strips = lax.all_to_all(strips, 'vis', 0, 0, tiled=True)]
    all_to_all x0 -> x1, starting transfers between devices: none -> 5.49 us  [on_device(): strips = lax.all_to_all(strips, 'vis', 0, 0, tiled=True)]
    all_to_all x0 -> x1, waiting for transfers between devices: none -> 3.56 us  [on_device(): strips = lax.all_to_all(strips, 'vis', 0, 0, tiled=True)]
    pallas_call x1, Pallas kernels: 0.73 us -> 1.8 us  [on_device(): pl.pallas_call(round_image, out_shape=jax.ShapeDtypeStruct((8, 32, 512),...]
    unnamed x14 -> x12, local copies, waits for them, and re-layouts: 2.64 us -> 2.29 us
    pallas_call x2 -> x3, Pallas kernels: 8.05 us -> 8.07 us  [the longest x1 5.86 us: on_device(): pl.pallas_call(rows_kernel, out_shape=message, in_specs=[VMEM] * 9 + [HBM...]
  transfers between devices with their start and end apart: 0 -> 1, of which waited for: 0 -> 1; matrix products, arithmetic and copies ran while one was open for 0% -> 0% of each run, Pallas kernels for 0% -> 2%
where the time goes in v5:
time: 71.2 us; the launch traced here: 70.8 us
  blocking collectives  46.7 us (66%)
  Pallas kernels  11.2 us (16%)
  starting transfers between devices  5.49 us (8%)
  waiting for transfers between devices  3.56 us (5%)
  local copies, waits for them, and re-layouts  2.29 us (3%)
  other arithmetic  0.87 us (1%)
    all_to_all x2, blocking collectives, on_device(): got = lax.all_to_all(sent, everyone, 0, 0, tiled=True)  36.6 us
    all_to_all x1, blocking collectives, on_device(): image = lax.all_to_all(image, 'vis', 0, 0, tiled=True)  10.1 us
    pallas_call x1, Pallas kernels, on_device(): pl.pallas_call(rows_kernel, out_shape=message, in_specs=[VMEM] * 9 + [HBM...  5.86 us
    all_to_all x1, starting transfers between devices, on_device(): strips = lax.all_to_all(strips, 'vis', 0, 0, tiled=True)  5.49 us
    all_to_all x1, waiting for transfers between devices, on_device(): strips = lax.all_to_all(strips, 'vis', 0, 0, tiled=True)  3.56 us
    unnamed x12, local copies, waits for them, and re-layouts  2.29 us
    pallas_call x1, Pallas kernels, on_device(): pl.pallas_call(round_image, out_shape=jax.ShapeDtypeStruct((8, 32, 512),...  1.8 us
  transfers between devices with their start and end apart: 1, of which 1 were waited for; matrix products, arithmetic and copies ran while one was open for 0% of the time, Pallas kernels for 2%

profile of v5, /device:TPU:0, one launch (start us, length us, event | category | flops | bytes accessed | tf_op | source)
XLA Modules:
  0.0 70.8 jit_solution(6767198242986169195)
XLA Ops:
  0.6 1.8 %shard_map.86 = bf16[8,32,512]{2,1,0:T(8,128)(2,1)} custom-call(f32[256,512]{1,0:T(8,128)} %sky_hbm.1), custom_call_target="tpu_custom_call" | custom-call | tf_op jit(solution)/shard_map/pallas_call | solution.py:313
  2.4 5.5 %all-to-all-start = ((bf16[8,32,512]{2,1,0:T(8,128)(2,1)}), bf16[8,32,512]{2,1,0:T(8,128)(2,1)S(1)}, u32[]{:S(2)}, u32[]{:S(2)}) async-start(bf16[8,32,512]{2,1,0:T(8,128)(2,1)} %shard_map.86), calls=%async_computation | async-start | bytes 524288 | tf_op jit(solution)/shard_map/all_to_all | solution.py:321
  7.9 0.0 copy-start.1
  7.9 0.9 %copy-done.1 = bf16[1,256,256]{2,1,0:T(8,128)(2,1)S(1)} copy-done((bf16[1,256,256]{2,1,0:T(8,128)(2,1)S(1)}, bf16[1,256,256]{2,1,0:T(8,128)(2,1)}, u32[]{:S(2)}) %copy-start.1) | copy-done | bytes 131096
  8.8 0.0 copy-start.3
  8.8 0.7 copy-done.3
  9.5 0.0 copy-start.4
  9.5 0.7 copy-done.4
  10.2 1.4 %shard_map.87 = (bf16[128,4,128]{2,1,0:T(4,128)(2,1)S(1)}, bf16[1024,512]{1,0:T(8,128)(2,1)S(1)}, f32[128,256]{1,0:T(8,128)S(1)}, f32[128,256]{1,0:T(8,128)S(1)}...) custom-call(bf16[1,256,256]{2,1,0:T(8,128)(2,1)S(1)} %copy-done.1, ...), custom_call_target="tpu_custom_call" | custom-call | flops 1000000000 | bytes 4000000 | tf_op jit(solution)/shard_map/pallas_call | solution.py:323
  11.6 0.0 copy-start
  11.6 0.0 copy-start.2
  11.6 0.0 copy-start.5
  11.6 3.6 %all-to-all-done.rx_ref = bf16[8,32,512]{2,1,0:T(8,128)(2,1)S(1)} async-done(((bf16[8,32,512]{2,1,0:T(8,128)(2,1)}), bf16[8,32,512]{2,1,0:T(8,128)(2,1)S(1)}, u32[]{:S(2)}, u32[]{:S(2)}) %all-to-all-start) | async-done | bytes 262176 | tf_op jit(solution)/shard_map/all_to_all | solution.py:321
  15.2 0.9 %shard_map.88 = bf16[128,3,4,128]{3,2,1,0:T(4,128)(2,1)S(1)} custom-call(bf16[8,32,512]{2,1,0:T(8,128)(2,1)S(1)} %all-to-all-done.rx_ref, bf16[128,4,128]{2,1,0:T(4,128)(2,1)S(1)} %get-tuple-element.14.seen_ref, bf16[1024,512]{1,0:T(8,128)(2,1)S(1)} %get-tuple-element.15.tab_ref), custom_call_target="tpu_custom_call" | custom-call | tf_op jit(solution)/shard_map/pallas_call | solution.py:337
  16.0 20.2 %all_to_all.20.rx_ref = bf16[128,3,4,128]{3,2,1,0:T(4,128)(2,1)S(1)} all-to-all(bf16[128,3,4,128]{3,2,1,0:T(4,128)(2,1)S(1)} %shard_map.88), channel_id=1, replica_groups=mesh['facet'=16,'vis'=8] {'facet','vis'}, dimensions={0} | all-to-all | bytes 786432 | tf_op jit(solution)/shard_map/all_to_all | solution.py:344
  36.2 5.9 %shard_map.89 = bf16[128,3,4,128]{3,2,1,0:T(4,128)(2,1)S(1)} custom-call(bf16[128,3,4,128]{3,2,1,0:T(4,128)(2,1)S(1)} %all_to_all.20.rx_ref, f32[128,256]{1,0:T(8,128)S(1)} %get-tuple-element.16.ct_ref, f32[128,256]{1,0:T(8,128)S(1)} %get-tuple-element.17.st_ref, f32[256,128]{1,0:T(8,128)S(1)} %get-tuple-element.18.cg_ref, ...), custom_call_target="tpu_custom_call" | custom-call | tf_op jit(solution)/shard_map/pallas_call | solution.py:345
  42.1 16.4 %all_to_all.21.rx_ref = bf16[128,3,4,128]{3,2,1,0:T(4,128)(2,1)S(1)} all-to-all(bf16[128,3,4,128]{3,2,1,0:T(4,128)(2,1)S(1)} %shard_map.89), channel_id=1, replica_groups=mesh['facet'=16,'vis'=8] {'facet','vis'}, dimensions={0} | all-to-all | bytes 786432 | tf_op jit(solution)/shard_map/all_to_all | solution.py:366
  58.5 0.0 copy-done
  58.5 0.0 copy-done.2
  58.5 0.0 copy-done.5
  58.5 1.3 %shard_map.90 = (bf16[8,32,512]{2,1,0:T(8,128)(2,1)S(1)}, bf16[1,256,256]{2,1,0:T(8,128)(2,1)}) custom-call(bf16[128,3,4,128]{3,2,1,0:T(4,128)(2,1)S(1)} %all_to_all.21.rx_ref, s32[2,128]{1,0:T(2,128)S(1)} %bitcast.7, f32[16,512]{1,0:T(8,128)S(1)} %copy-done.2, bf16[512,1024]{1,0:T(8,128)(2,1)S(1)} %copy-done), custom_call_target="tpu_custom_call" | custom-call | tf_op jit(solution)/shard_map/pallas_call | solution.py:367
  59.8 10.1 %all_to_all.22 = bf16[8,32,512]{2,1,0:T(8,128)(2,1)S(1)} all-to-all(bf16[8,32,512]{2,1,0:T(8,128)(2,1)S(1)} %get-tuple-element.25), channel_id=1, replica_groups=mesh['facet'=16,'vis'=8] {'vis'}, dimensions={0} | all-to-all | bytes 524288 | tf_op jit(solution)/shard_map/all_to_all | solution.py:383
  69.9 0.9 %bitcast_convert_fusion = f32[256,512]{1,0:T(8,128)} fusion(bf16[8,32,512]{2,1,0:T(8,128)(2,1)S(1)} %all_to_all.22), kind=kLoop, calls=%fused_computation | loop fusion | flops 131072 | bytes 786432 | tf_op jit(solution)/shard_map/convert_element_type | solution.py:384
Async XLA Ops:
  2.4 12.7 %all-to-all-start = ((bf16[8,32,512]{2,1,0:T(8,128)(2,1)}), bf16[8,32,512]{2,1,0:T(8,128)(2,1)S(1)}, u32[]{:S(2)}, u32[]{:S(2)}) async-start(bf16[8,32,512]{2,1,0:T(8,128)(2,1)} %shard_map.86), calls=%async_computation | async-start | bytes 524288 | tf_op jit(solution)/shard_map/all_to_all | solution.py:321
  7.9 0.9 %copy-start.1 = (bf16[1,256,256]{2,1,0:T(8,128)(2,1)S(1)}, bf16[1,256,256]{2,1,0:T(8,128)(2,1)}, u32[]{:S(2)}) copy-start(bf16[1,256,256]{2,1,0:T(8,128)(2,1)} %obs_ref.1) | copy-start | bytes 393220
  8.8 0.7 copy-start.3
  9.5 0.7 copy-start.4
  11.6 46.9 %copy-start = (bf16[512,1024]{1,0:T(8,128)(2,1)S(1)}, bf16[512,1024]{1,0:T(8,128)(2,1)}, u32[]{:S(2)}) copy-start(bf16[512,1024]{1,0:T(8,128)(2,1)} %constant.8.clone.tab_ref) | copy-start | bytes 3145732
  11.6 46.9 %copy-start.2 = (f32[16,512]{1,0:T(8,128)S(1)}, f32[16,512]{1,0:T(8,128)}, u32[]{:S(2)}) copy-start(f32[16,512]{1,0:T(8,128)} %constant.7.clone.tw_ref) | copy-start | bytes 98308
  11.6 46.9 %copy-start.5 = (s32[128,2]{0,1:T(2,128)S(1)}, s32[128,2]{0,1:T(2,128)}, u32[]{:S(2)}) copy-start(s32[128,2]{0,1:T(2,128)} %param.9) | copy-start | bytes 3076

commit v6 on v5

--- a/solution.py
+++ b/solution.py
@@ -105,16 +105,28 @@
 
 
 def round_image(sky_hbm, out_hbm, held, done, sems):
-    moves = [pltpu.make_async_copy(sky_hbm.at[pl.ds(64 * i, 64)], held.at[pl.ds(64 * i, 64)], sems.at[i]) for i in range(4)]
-    backs = [pltpu.make_async_copy(done.at[pl.ds(2 * i, 2)], out_hbm.at[pl.ds(2 * i, 2)], sems.at[4 + i]) for i in range(4)]
+    rows = [pl.ds(128 * i, 128) for i in range(2)]
+    strips = [pl.ds(4 * i, 4) for i in range(2)]
+    moves = [pltpu.make_async_copy(sky_hbm.at[rows[i]], held.at[rows[i]], sems.at[i]) for i in range(2)]
+    backs = [pltpu.make_async_copy(done.at[strips[i]], out_hbm.at[strips[i]], sems.at[2 + i]) for i in range(2)]
     for move in moves:
         move.start()
-    for i in range(4):
+    for i in range(2):
         moves[i].wait()
-        done[2 * i : 2 * i + 2] = held[64 * i : 64 * i + 64].reshape(2, 32, 512).astype(BF16)
+        done[4 * i : 4 * i + 4] = held[128 * i : 128 * i + 128].reshape(4, 32, 512).astype(BF16)
         backs[i].start()
     for back in backs:
         back.wait()
+
+
+def widen_image(img_ref, out_hbm, done, sems):
+    rows = [pl.ds(64 * i, 64) for i in range(4)]
+    leave = [pltpu.make_async_copy(done.at[rows[i]], out_hbm.at[rows[i]], sems.at[i]) for i in range(4)]
+    for i in range(4):
+        done[64 * i : 64 * i + 64] = img_ref[2 * i : 2 * i + 2].astype(F32).reshape(64, 512)
+        leave[i].start()
+    for move in leave:
+        move.wait()
 
 
 def observed_columns(
@@ -315,7 +327,7 @@
         out_shape=jax.ShapeDtypeStruct((8, 32, 512), BF16),
         in_specs=[HBM],
         out_specs=HBM,
-        scratch_shapes=[pltpu.VMEM((256, 512), F32), pltpu.VMEM((8, 32, 512), BF16), pltpu.SemaphoreType.DMA((8,))],
+        scratch_shapes=[pltpu.VMEM((256, 512), F32), pltpu.VMEM((8, 32, 512), BF16), pltpu.SemaphoreType.DMA((4,))],
         compiler_params=params(L0),
     )(sky_image)
     strips = lax.all_to_all(strips, "vis", 0, 0, tiled=True)
@@ -381,7 +393,15 @@
         compiler_params=params(16),
     )(got, offsets, jnp.asarray(twiddle), jnp.asarray(back))
     image = lax.all_to_all(image, "vis", 0, 0, tiled=True)
-    return resid, image.reshape(256, 512).astype(F32)
+    image = pl.pallas_call(
+        widen_image,
+        out_shape=jax.ShapeDtypeStruct((256, 512), F32),
+        in_specs=[VMEM],
+        out_specs=HBM,
+        scratch_shapes=[pltpu.VMEM((256, 512), F32), pltpu.SemaphoreType.DMA((4,))],
+        compiler_params=params(40),
+    )(image)
+    return resid, image
 
 
 def solution(mesh):

time: 71.2 us -> 71.1 us (level)
  other arithmetic: 0.87 us -> 0 us
    convert_element_type x1 -> x0, other arithmetic: 0.87 us -> none  [on_device(): return (resid, image.reshape(256, 512).astype(F32))]
    pallas_call x0 -> x1, Pallas kernels: none -> 0.83 us  [on_device(): pl.pallas_call(widen_image, out_shape=jax.ShapeDtypeStruct((256, 512), F3...]
where the time goes in v6:
time: 71.1 us; the launch traced here: 70.6 us
  blocking collectives  46.7 us (66%)
  Pallas kernels  11.9 us (17%)
  starting transfers between devices  5.49 us (8%)
  waiting for transfers between devices  3.56 us (5%)
  local copies, waits for them, and re-layouts  2.29 us (3%)
    all_to_all x2, blocking collectives, on_device(): got = lax.all_to_all(sent, everyone, 0, 0, tiled=True)  36.6 us
    all_to_all x1, blocking collectives, on_device(): image = lax.all_to_all(image, 'vis', 0, 0, tiled=True)  10.1 us
    pallas_call x1, Pallas kernels, on_device(): pl.pallas_call(rows_kernel, out_shape=message, in_specs=[VMEM] * 9 + [HBM...  5.86 us
    all_to_all x1, starting transfers between devices, on_device(): strips = lax.all_to_all(strips, 'vis', 0, 0, tiled=True)  5.49 us
    all_to_all x1, waiting for transfers between devices, on_device(): strips = lax.all_to_all(strips, 'vis', 0, 0, tiled=True)  3.56 us
    unnamed x12, local copies, waits for them, and re-layouts  2.29 us
    pallas_call x1, Pallas kernels, on_device(): pl.pallas_call(round_image, out_shape=jax.ShapeDtypeStruct((8, 32, 512),...  1.73 us
  transfers between devices with their start and end apart: 1, of which 1 were waited for; matrix products, arithmetic and copies ran while one was open for 0% of the time, Pallas kernels for 2%

profile of v6, /device:TPU:0, one launch (start us, length us, event | category | flops | bytes accessed | tf_op | source)
XLA Modules:
  0.0 70.6 jit_solution(13199378003989565348)
XLA Ops:
  0.6 1.7 %shard_map.86 = bf16[8,32,512]{2,1,0:T(8,128)(2,1)} custom-call(f32[256,512]{1,0:T(8,128)} %sky_hbm.1), custom_call_target="tpu_custom_call" | custom-call | tf_op jit(solution)/shard_map/pallas_call | solution.py:325
  2.4 5.5 %all-to-all-start = ((bf16[8,32,512]{2,1,0:T(8,128)(2,1)}), bf16[8,32,512]{2,1,0:T(8,128)(2,1)S(1)}, u32[]{:S(2)}, u32[]{:S(2)}) async-start(bf16[8,32,512]{2,1,0:T(8,128)(2,1)} %shard_map.86), calls=%async_computation | async-start | bytes 524288 | tf_op jit(solution)/shard_map/all_to_all | solution.py:333
  7.9 0.0 copy-start.1
  7.9 0.9 %copy-done.1 = bf16[1,256,256]{2,1,0:T(8,128)(2,1)S(1)} copy-done((bf16[1,256,256]{2,1,0:T(8,128)(2,1)S(1)}, bf16[1,256,256]{2,1,0:T(8,128)(2,1)}, u32[]{:S(2)}) %copy-start.1) | copy-done | bytes 131096
  8.8 0.0 copy-start.3
  8.8 0.7 copy-done.3
  9.5 0.0 copy-start.4
  9.5 0.7 copy-done.4
  10.1 1.4 %shard_map.87 = (bf16[128,4,128]{2,1,0:T(4,128)(2,1)S(1)}, bf16[1024,512]{1,0:T(8,128)(2,1)S(1)}, f32[128,256]{1,0:T(8,128)S(1)}, f32[128,256]{1,0:T(8,128)S(1)}...) custom-call(bf16[1,256,256]{2,1,0:T(8,128)(2,1)S(1)} %copy-done.1, ...), custom_call_target="tpu_custom_call" | custom-call | flops 1000000000 | bytes 4000000 | tf_op jit(solution)/shard_map/pallas_call | solution.py:335
  11.5 0.0 copy-start
  11.5 0.0 copy-start.2
  11.5 0.0 copy-start.5
  11.5 3.6 %all-to-all-done.rx_ref = bf16[8,32,512]{2,1,0:T(8,128)(2,1)S(1)} async-done(((bf16[8,32,512]{2,1,0:T(8,128)(2,1)}), bf16[8,32,512]{2,1,0:T(8,128)(2,1)S(1)}, u32[]{:S(2)}, u32[]{:S(2)}) %all-to-all-start) | async-done | bytes 262176 | tf_op jit(solution)/shard_map/all_to_all | solution.py:333
  15.1 0.9 %shard_map.88 = bf16[128,3,4,128]{3,2,1,0:T(4,128)(2,1)S(1)} custom-call(bf16[8,32,512]{2,1,0:T(8,128)(2,1)S(1)} %all-to-all-done.rx_ref, bf16[128,4,128]{2,1,0:T(4,128)(2,1)S(1)} %get-tuple-element.14.seen_ref, bf16[1024,512]{1,0:T(8,128)(2,1)S(1)} %get-tuple-element.15.tab_ref), custom_call_target="tpu_custom_call" | custom-call | tf_op jit(solution)/shard_map/pallas_call | solution.py:349
  16.0 20.2 %all_to_all.20.rx_ref = bf16[128,3,4,128]{3,2,1,0:T(4,128)(2,1)S(1)} all-to-all(bf16[128,3,4,128]{3,2,1,0:T(4,128)(2,1)S(1)} %shard_map.88), channel_id=1, replica_groups=mesh['facet'=16,'vis'=8] {'facet','vis'}, dimensions={0} | all-to-all | bytes 786432 | tf_op jit(solution)/shard_map/all_to_all | solution.py:356
  36.2 5.9 %shard_map.89 = bf16[128,3,4,128]{3,2,1,0:T(4,128)(2,1)S(1)} custom-call(bf16[128,3,4,128]{3,2,1,0:T(4,128)(2,1)S(1)} %all_to_all.20.rx_ref, f32[128,256]{1,0:T(8,128)S(1)} %get-tuple-element.16.ct_ref, f32[128,256]{1,0:T(8,128)S(1)} %get-tuple-element.17.st_ref, f32[256,128]{1,0:T(8,128)S(1)} %get-tuple-element.18.cg_ref, ...), custom_call_target="tpu_custom_call" | custom-call | tf_op jit(solution)/shard_map/pallas_call | solution.py:357
  42.0 16.4 %all_to_all.21.rx_ref = bf16[128,3,4,128]{3,2,1,0:T(4,128)(2,1)S(1)} all-to-all(bf16[128,3,4,128]{3,2,1,0:T(4,128)(2,1)S(1)} %shard_map.89), channel_id=1, replica_groups=mesh['facet'=16,'vis'=8] {'facet','vis'}, dimensions={0} | all-to-all | bytes 786432 | tf_op jit(solution)/shard_map/all_to_all | solution.py:378
  58.4 0.0 copy-done
  58.4 0.0 copy-done.2
  58.4 0.0 copy-done.5
  58.4 1.3 %shard_map.90 = (bf16[8,32,512]{2,1,0:T(8,128)(2,1)S(1)}, bf16[1,256,256]{2,1,0:T(8,128)(2,1)}) custom-call(bf16[128,3,4,128]{3,2,1,0:T(4,128)(2,1)S(1)} %all_to_all.21.rx_ref, s32[2,128]{1,0:T(2,128)S(1)} %bitcast.4, f32[16,512]{1,0:T(8,128)S(1)} %copy-done.2, bf16[512,1024]{1,0:T(8,128)(2,1)S(1)} %copy-done), custom_call_target="tpu_custom_call" | custom-call | tf_op jit(solution)/shard_map/pallas_call | solution.py:379
  59.7 10.1 %all_to_all.22.img_ref = bf16[8,32,512]{2,1,0:T(8,128)(2,1)S(1)} all-to-all(bf16[8,32,512]{2,1,0:T(8,128)(2,1)S(1)} %get-tuple-element.25), channel_id=1, replica_groups=mesh['facet'=16,'vis'=8] {'vis'}, dimensions={0} | all-to-all | bytes 524288 | tf_op jit(solution)/shard_map/all_to_all | solution.py:395
  69.8 0.8 %shard_map.91 = f32[256,512]{1,0:T(8,128)} custom-call(bf16[8,32,512]{2,1,0:T(8,128)(2,1)S(1)} %all_to_all.22.img_ref), custom_call_target="tpu_custom_call" | custom-call | tf_op jit(solution)/shard_map/pallas_call | solution.py:396
Async XLA Ops:
  2.4 12.7 %all-to-all-start = ((bf16[8,32,512]{2,1,0:T(8,128)(2,1)}), bf16[8,32,512]{2,1,0:T(8,128)(2,1)S(1)}, u32[]{:S(2)}, u32[]{:S(2)}) async-start(bf16[8,32,512]{2,1,0:T(8,128)(2,1)} %shard_map.86), calls=%async_computation | async-start | bytes 524288 | tf_op jit(solution)/shard_map/all_to_all | solution.py:333
  7.9 0.9 %copy-start.1 = (bf16[1,256,256]{2,1,0:T(8,128)(2,1)S(1)}, bf16[1,256,256]{2,1,0:T(8,128)(2,1)}, u32[]{:S(2)}) copy-start(bf16[1,256,256]{2,1,0:T(8,128)(2,1)} %obs_ref.1) | copy-start | bytes 393220
  8.8 0.7 copy-start.3
  9.5 0.7 copy-start.4
  11.5 46.9 %copy-start = (bf16[512,1024]{1,0:T(8,128)(2,1)S(1)}, bf16[512,1024]{1,0:T(8,128)(2,1)}, u32[]{:S(2)}) copy-start(bf16[512,1024]{1,0:T(8,128)(2,1)} %constant.8.clone.tab_ref) | copy-start | bytes 3145732
  11.5 46.9 %copy-start.2 = (f32[16,512]{1,0:T(8,128)S(1)}, f32[16,512]{1,0:T(8,128)}, u32[]{:S(2)}) copy-start(f32[16,512]{1,0:T(8,128)} %constant.7.clone.tw_ref) | copy-start | bytes 98308
  11.5 46.9 %copy-start.5 = (s32[128,2]{0,1:T(2,128)S(1)}, s32[128,2]{0,1:T(2,128)}, u32[]{:S(2)}) copy-start(s32[128,2]{0,1:T(2,128)} %param.9) | copy-start | bytes 3076

commit v7 on v5

--- a/solution.py
+++ b/solution.py
@@ -194,23 +194,27 @@
     turn_ct = jnp.transpose(jnp.broadcast_to(tc_ref[:1], (256, 128)))
     turn_st = jnp.transpose(jnp.broadcast_to(ts_ref[:1], (256, 128)))
 
-    @pl.loop(0, 16, unroll=UNROLL)
-    def _(f):
-        tile = held[pl.ds(8 * f, 8)]
-        spread = jnp.stack([jnp.where(group == rg, tile, 0.0) for rg in range(4)], axis=1)
-        right = spread.reshape(256, 128).astype(BF16)
+    group2 = lax.broadcasted_iota(jnp.int32, (16, 8, 128), 2) >> 5
+
+    @pl.loop(0, 8, unroll=UNROLL)
+    def _(pair):
+        tile = held[pl.ds(16 * pair, 16)]
+        spread = jnp.stack([jnp.where(group2 == rg, tile, 0.0) for rg in range(4)], axis=1)
+        right = spread.reshape(512, 128).astype(BF16)
         cols = lax.dot_general(chosen, right, NT, preferred_element_type=F32)
-        at = pl.multiple_of(f * 256, 256)
         c, s = ct[...], st[...]
-        for t in range(2):
-            half = cols[128 * t : 128 * t + 128]
-            ybuf[128 * t : 128 * t + 128, pl.ds(2 * at, 256)] = (half * c).astype(BF16)
-            ybuf[128 * t : 128 * t + 128, pl.ds(2 * at + 256, 256)] = (half * s).astype(BF16)
-        ct[...], st[...] = spin(c, s, turn_ct, turn_st)
-        named = (lax.shift_right_logical(bits_ref[...], f) & 1) == 1
-        for t in range(2):
-            kept = jnp.where(named, chosen_ref[128 * t : 128 * t + 128], 0.0)
-            keep[pl.ds(at + 128 * t, 128)] = kept.astype(BF16)
+        for i in range(2):
+            at = pl.multiple_of(pair * 512 + 256 * i, 256)
+            for t in range(2):
+                half = cols[128 * t : 128 * t + 128, 256 * i : 256 * i + 256]
+                ybuf[128 * t : 128 * t + 128, pl.ds(2 * at, 256)] = (half * c).astype(BF16)
+                ybuf[128 * t : 128 * t + 128, pl.ds(2 * at + 256, 256)] = (half * s).astype(BF16)
+            c, s = spin(c, s, turn_ct, turn_st)
+            named = (lax.shift_right_logical(bits_ref[...], 2 * pair + i) & 1) == 1
+            for t in range(2):
+                kept = jnp.where(named, chosen_ref[128 * t : 128 * t + 128], 0.0)
+                keep[pl.ds(at + 128 * t, 128)] = kept.astype(BF16)
+        ct[...], st[...] = c, s
 
     fetch.wait()
     pred = jnp.dot(ybuf[...], tab_ref[...], preferred_element_type=F32) * (1.0 / 64.0)
@@ -295,7 +299,7 @@
 
 VMEM = pl.BlockSpec(memory_space=pltpu.VMEM)
 HBM = pl.BlockSpec(memory_space=pltpu.HBM)
-UNROLL, UNROLL1, UNROLL2 = 8, 8, 16
+UNROLL, UNROLL1, UNROLL2 = 4, 8, 16
 L0, L1, L2 = 56, 50, 52
 
 

time: 71.2 us -> 71.2 us (level)
  no operation moved by 1% of the time
where the time goes in v7:
time: 71.2 us; the launch traced here: 70.8 us
  blocking collectives  46.7 us (66%)
  Pallas kernels  11.2 us (16%)
  starting transfers between devices  5.49 us (8%)
  waiting for transfers between devices  3.56 us (5%)
  local copies, waits for them, and re-layouts  2.29 us (3%)
  other arithmetic  0.87 us (1%)
    all_to_all x2, blocking collectives, on_device(): got = lax.all_to_all(sent, everyone, 0, 0, tiled=True)  36.6 us
    all_to_all x1, blocking collectives, on_device(): image = lax.all_to_all(image, 'vis', 0, 0, tiled=True)  10.1 us
    pallas_call x1, Pallas kernels, on_device(): pl.pallas_call(rows_kernel, out_shape=message, in_specs=[VMEM] * 9 + [HBM...  5.86 us
    all_to_all x1, starting transfers between devices, on_device(): strips = lax.all_to_all(strips, 'vis', 0, 0, tiled=True)  5.49 us
    all_to_all x1, waiting for transfers between devices, on_device(): strips = lax.all_to_all(strips, 'vis', 0, 0, tiled=True)  3.56 us
    unnamed x12, local copies, waits for them, and re-layouts  2.29 us
    pallas_call x1, Pallas kernels, on_device(): pl.pallas_call(round_image, out_shape=jax.ShapeDtypeStruct((8, 32, 512),...  1.8 us
  transfers between devices with their start and end apart: 1, of which 1 were waited for; matrix products, arithmetic and copies ran while one was open for 0% of the time, Pallas kernels for 2%

profile of v7, /device:TPU:0, one launch (start us, length us, event | category | flops | bytes accessed | tf_op | source)
XLA Modules:
  0.0 70.8 jit_solution(5100028434971616925)
XLA Ops:
  0.6 1.8 %shard_map.86 = bf16[8,32,512]{2,1,0:T(8,128)(2,1)} custom-call(f32[256,512]{1,0:T(8,128)} %sky_hbm.1), custom_call_target="tpu_custom_call" | custom-call | tf_op jit(solution)/shard_map/pallas_call | solution.py:317
  2.4 5.5 %all-to-all-start = ((bf16[8,32,512]{2,1,0:T(8,128)(2,1)}), bf16[8,32,512]{2,1,0:T(8,128)(2,1)S(1)}, u32[]{:S(2)}, u32[]{:S(2)}) async-start(bf16[8,32,512]{2,1,0:T(8,128)(2,1)} %shard_map.86), calls=%async_computation | async-start | bytes 524288 | tf_op jit(solution)/shard_map/all_to_all | solution.py:325
  7.9 0.0 copy-start.1
  7.9 0.9 %copy-done.1 = bf16[1,256,256]{2,1,0:T(8,128)(2,1)S(1)} copy-done((bf16[1,256,256]{2,1,0:T(8,128)(2,1)S(1)}, bf16[1,256,256]{2,1,0:T(8,128)(2,1)}, u32[]{:S(2)}) %copy-start.1) | copy-done | bytes 131096
  8.8 0.0 copy-start.3
  8.8 0.7 copy-done.3
  9.5 0.0 copy-start.4
  9.5 0.7 copy-done.4
  10.2 1.4 %shard_map.87 = (bf16[128,4,128]{2,1,0:T(4,128)(2,1)S(1)}, bf16[1024,512]{1,0:T(8,128)(2,1)S(1)}, f32[128,256]{1,0:T(8,128)S(1)}, f32[128,256]{1,0:T(8,128)S(1)}...) custom-call(bf16[1,256,256]{2,1,0:T(8,128)(2,1)S(1)} %copy-done.1, ...), custom_call_target="tpu_custom_call" | custom-call | flops 1000000000 | bytes 4000000 | tf_op jit(solution)/shard_map/pallas_call | solution.py:327
  11.6 0.0 copy-start
  11.6 0.0 copy-start.2
  11.6 0.0 copy-start.5
  11.6 3.6 %all-to-all-done.rx_ref = bf16[8,32,512]{2,1,0:T(8,128)(2,1)S(1)} async-done(((bf16[8,32,512]{2,1,0:T(8,128)(2,1)}), bf16[8,32,512]{2,1,0:T(8,128)(2,1)S(1)}, u32[]{:S(2)}, u32[]{:S(2)}) %all-to-all-start) | async-done | bytes 262176 | tf_op jit(solution)/shard_map/all_to_all | solution.py:325
  15.2 0.9 %shard_map.88 = bf16[128,3,4,128]{3,2,1,0:T(4,128)(2,1)S(1)} custom-call(bf16[8,32,512]{2,1,0:T(8,128)(2,1)S(1)} %all-to-all-done.rx_ref, bf16[128,4,128]{2,1,0:T(4,128)(2,1)S(1)} %get-tuple-element.14.seen_ref, bf16[1024,512]{1,0:T(8,128)(2,1)S(1)} %get-tuple-element.15.tab_ref), custom_call_target="tpu_custom_call" | custom-call | tf_op jit(solution)/shard_map/pallas_call | solution.py:341
  16.0 20.2 %all_to_all.20.rx_ref = bf16[128,3,4,128]{3,2,1,0:T(4,128)(2,1)S(1)} all-to-all(bf16[128,3,4,128]{3,2,1,0:T(4,128)(2,1)S(1)} %shard_map.88), channel_id=1, replica_groups=mesh['facet'=16,'vis'=8] {'facet','vis'}, dimensions={0} | all-to-all | bytes 786432 | tf_op jit(solution)/shard_map/all_to_all | solution.py:348
  36.2 5.9 %shard_map.89 = bf16[128,3,4,128]{3,2,1,0:T(4,128)(2,1)S(1)} custom-call(bf16[128,3,4,128]{3,2,1,0:T(4,128)(2,1)S(1)} %all_to_all.20.rx_ref, f32[128,256]{1,0:T(8,128)S(1)} %get-tuple-element.16.ct_ref, f32[128,256]{1,0:T(8,128)S(1)} %get-tuple-element.17.st_ref, f32[256,128]{1,0:T(8,128)S(1)} %get-tuple-element.18.cg_ref, ...), custom_call_target="tpu_custom_call" | custom-call | tf_op jit(solution)/shard_map/pallas_call | solution.py:349
  42.1 16.4 %all_to_all.21.rx_ref = bf16[128,3,4,128]{3,2,1,0:T(4,128)(2,1)S(1)} all-to-all(bf16[128,3,4,128]{3,2,1,0:T(4,128)(2,1)S(1)} %shard_map.89), channel_id=1, replica_groups=mesh['facet'=16,'vis'=8] {'facet','vis'}, dimensions={0} | all-to-all | bytes 786432 | tf_op jit(solution)/shard_map/all_to_all | solution.py:370
  58.5 0.0 copy-done
  58.5 0.0 copy-done.2
  58.5 0.0 copy-done.5
  58.5 1.3 %shard_map.90 = (bf16[8,32,512]{2,1,0:T(8,128)(2,1)S(1)}, bf16[1,256,256]{2,1,0:T(8,128)(2,1)}) custom-call(bf16[128,3,4,128]{3,2,1,0:T(4,128)(2,1)S(1)} %all_to_all.21.rx_ref, s32[2,128]{1,0:T(2,128)S(1)} %bitcast.7, f32[16,512]{1,0:T(8,128)S(1)} %copy-done.2, bf16[512,1024]{1,0:T(8,128)(2,1)S(1)} %copy-done), custom_call_target="tpu_custom_call" | custom-call | tf_op jit(solution)/shard_map/pallas_call | solution.py:371
  59.8 10.1 %all_to_all.22 = bf16[8,32,512]{2,1,0:T(8,128)(2,1)S(1)} all-to-all(bf16[8,32,512]{2,1,0:T(8,128)(2,1)S(1)} %get-tuple-element.25), channel_id=1, replica_groups=mesh['facet'=16,'vis'=8] {'vis'}, dimensions={0} | all-to-all | bytes 524288 | tf_op jit(solution)/shard_map/all_to_all | solution.py:387
  69.9 0.9 %bitcast_convert_fusion = f32[256,512]{1,0:T(8,128)} fusion(bf16[8,32,512]{2,1,0:T(8,128)(2,1)S(1)} %all_to_all.22), kind=kLoop, calls=%fused_computation | loop fusion | flops 131072 | bytes 786432 | tf_op jit(solution)/shard_map/convert_element_type | solution.py:388
Async XLA Ops:
  2.4 12.7 %all-to-all-start = ((bf16[8,32,512]{2,1,0:T(8,128)(2,1)}), bf16[8,32,512]{2,1,0:T(8,128)(2,1)S(1)}, u32[]{:S(2)}, u32[]{:S(2)}) async-start(bf16[8,32,512]{2,1,0:T(8,128)(2,1)} %shard_map.86), calls=%async_computation | async-start | bytes 524288 | tf_op jit(solution)/shard_map/all_to_all | solution.py:325
  7.9 0.9 %copy-start.1 = (bf16[1,256,256]{2,1,0:T(8,128)(2,1)S(1)}, bf16[1,256,256]{2,1,0:T(8,128)(2,1)}, u32[]{:S(2)}) copy-start(bf16[1,256,256]{2,1,0:T(8,128)(2,1)} %obs_ref.1) | copy-start | bytes 393220
  8.8 0.7 copy-start.3
  9.5 0.7 copy-start.4
  11.6 46.9 %copy-start = (bf16[512,1024]{1,0:T(8,128)(2,1)S(1)}, bf16[512,1024]{1,0:T(8,128)(2,1)}, u32[]{:S(2)}) copy-start(bf16[512,1024]{1,0:T(8,128)(2,1)} %constant.8.clone.tab_ref) | copy-start | bytes 3145732
  11.6 46.9 %copy-start.2 = (f32[16,512]{1,0:T(8,128)S(1)}, f32[16,512]{1,0:T(8,128)}, u32[]{:S(2)}) copy-start(f32[16,512]{1,0:T(8,128)} %constant.7.clone.tw_ref) | copy-start | bytes 98308
  11.6 46.9 %copy-start.5 = (s32[128,2]{0,1:T(2,128)S(1)}, s32[128,2]{0,1:T(2,128)}, u32[]{:S(2)}) copy-start(s32[128,2]{0,1:T(2,128)} %param.9) | copy-start | bytes 3076

commit v8 on v5

--- a/solution.py
+++ b/solution.py
@@ -203,9 +203,9 @@
         at = pl.multiple_of(f * 256, 256)
         c, s = ct[...], st[...]
         for t in range(2):
-            half = cols[128 * t : 128 * t + 128]
-            ybuf[128 * t : 128 * t + 128, pl.ds(2 * at, 256)] = (half * c).astype(BF16)
-            ybuf[128 * t : 128 * t + 128, pl.ds(2 * at + 256, 256)] = (half * s).astype(BF16)
+            half = cols[128 * t : 128 * t + 128].astype(BF16)
+            ybuf[128 * t : 128 * t + 128, pl.ds(2 * at, 256)] = half * c.astype(BF16)
+            ybuf[128 * t : 128 * t + 128, pl.ds(2 * at + 256, 256)] = half * s.astype(BF16)
         ct[...], st[...] = spin(c, s, turn_ct, turn_st)
         named = (lax.shift_right_logical(bits_ref[...], f) & 1) == 1
         for t in range(2):

time: 71.2 us -> 71.2 us (level)
  no operation moved by 1% of the time
where the time goes in v8:
time: 71.2 us; the launch traced here: 70.8 us
  blocking collectives  46.7 us (66%)
  Pallas kernels  11.2 us (16%)
  starting transfers between devices  5.49 us (8%)
  waiting for transfers between devices  3.56 us (5%)
  local copies, waits for them, and re-layouts  2.29 us (3%)
  other arithmetic  0.87 us (1%)
    all_to_all x2, blocking collectives, on_device(): got = lax.all_to_all(sent, everyone, 0, 0, tiled=True)  36.6 us
    all_to_all x1, blocking collectives, on_device(): image = lax.all_to_all(image, 'vis', 0, 0, tiled=True)  10.1 us
    pallas_call x1, Pallas kernels, on_device(): pl.pallas_call(rows_kernel, out_shape=message, in_specs=[VMEM] * 9 + [HBM...  5.86 us
    all_to_all x1, starting transfers between devices, on_device(): strips = lax.all_to_all(strips, 'vis', 0, 0, tiled=True)  5.49 us
    all_to_all x1, waiting for transfers between devices, on_device(): strips = lax.all_to_all(strips, 'vis', 0, 0, tiled=True)  3.56 us
    unnamed x12, local copies, waits for them, and re-layouts  2.29 us
    pallas_call x1, Pallas kernels, on_device(): pl.pallas_call(round_image, out_shape=jax.ShapeDtypeStruct((8, 32, 512),...  1.8 us
  transfers between devices with their start and end apart: 1, of which 1 were waited for; matrix products, arithmetic and copies ran while one was open for 0% of the time, Pallas kernels for 2%

profile of v8, /device:TPU:0, one launch (start us, length us, event | category | flops | bytes accessed | tf_op | source)
XLA Modules:
  0.0 70.8 jit_solution(14041648493278352726)
XLA Ops:
  0.6 1.8 %shard_map.86 = bf16[8,32,512]{2,1,0:T(8,128)(2,1)} custom-call(f32[256,512]{1,0:T(8,128)} %sky_hbm.1), custom_call_target="tpu_custom_call" | custom-call | tf_op jit(solution)/shard_map/pallas_call | solution.py:313
  2.4 5.5 %all-to-all-start = ((bf16[8,32,512]{2,1,0:T(8,128)(2,1)}), bf16[8,32,512]{2,1,0:T(8,128)(2,1)S(1)}, u32[]{:S(2)}, u32[]{:S(2)}) async-start(bf16[8,32,512]{2,1,0:T(8,128)(2,1)} %shard_map.86), calls=%async_computation | async-start | bytes 524288 | tf_op jit(solution)/shard_map/all_to_all | solution.py:321
  7.9 0.0 copy-start.1
  7.9 0.9 %copy-done.1 = bf16[1,256,256]{2,1,0:T(8,128)(2,1)S(1)} copy-done((bf16[1,256,256]{2,1,0:T(8,128)(2,1)S(1)}, bf16[1,256,256]{2,1,0:T(8,128)(2,1)}, u32[]{:S(2)}) %copy-start.1) | copy-done | bytes 131096
  8.8 0.0 copy-start.3
  8.8 0.7 copy-done.3
  9.5 0.0 copy-start.4
  9.5 0.7 copy-done.4
  10.2 1.4 %shard_map.87 = (bf16[128,4,128]{2,1,0:T(4,128)(2,1)S(1)}, bf16[1024,512]{1,0:T(8,128)(2,1)S(1)}, f32[128,256]{1,0:T(8,128)S(1)}, f32[128,256]{1,0:T(8,128)S(1)}...) custom-call(bf16[1,256,256]{2,1,0:T(8,128)(2,1)S(1)} %copy-done.1, ...), custom_call_target="tpu_custom_call" | custom-call | flops 1000000000 | bytes 4000000 | tf_op jit(solution)/shard_map/pallas_call | solution.py:323
  11.6 0.0 copy-start
  11.6 0.0 copy-start.2
  11.6 0.0 copy-start.5
  11.6 3.6 %all-to-all-done.rx_ref = bf16[8,32,512]{2,1,0:T(8,128)(2,1)S(1)} async-done(((bf16[8,32,512]{2,1,0:T(8,128)(2,1)}), bf16[8,32,512]{2,1,0:T(8,128)(2,1)S(1)}, u32[]{:S(2)}, u32[]{:S(2)}) %all-to-all-start) | async-done | bytes 262176 | tf_op jit(solution)/shard_map/all_to_all | solution.py:321
  15.2 0.9 %shard_map.88 = bf16[128,3,4,128]{3,2,1,0:T(4,128)(2,1)S(1)} custom-call(bf16[8,32,512]{2,1,0:T(8,128)(2,1)S(1)} %all-to-all-done.rx_ref, bf16[128,4,128]{2,1,0:T(4,128)(2,1)S(1)} %get-tuple-element.14.seen_ref, bf16[1024,512]{1,0:T(8,128)(2,1)S(1)} %get-tuple-element.15.tab_ref), custom_call_target="tpu_custom_call" | custom-call | tf_op jit(solution)/shard_map/pallas_call | solution.py:337
  16.0 20.2 %all_to_all.20.rx_ref = bf16[128,3,4,128]{3,2,1,0:T(4,128)(2,1)S(1)} all-to-all(bf16[128,3,4,128]{3,2,1,0:T(4,128)(2,1)S(1)} %shard_map.88), channel_id=1, replica_groups=mesh['facet'=16,'vis'=8] {'facet','vis'}, dimensions={0} | all-to-all | bytes 786432 | tf_op jit(solution)/shard_map/all_to_all | solution.py:344
  36.2 5.9 %shard_map.89 = bf16[128,3,4,128]{3,2,1,0:T(4,128)(2,1)S(1)} custom-call(bf16[128,3,4,128]{3,2,1,0:T(4,128)(2,1)S(1)} %all_to_all.20.rx_ref, f32[128,256]{1,0:T(8,128)S(1)} %get-tuple-element.16.ct_ref, f32[128,256]{1,0:T(8,128)S(1)} %get-tuple-element.17.st_ref, f32[256,128]{1,0:T(8,128)S(1)} %get-tuple-element.18.cg_ref, ...), custom_call_target="tpu_custom_call" | custom-call | tf_op jit(solution)/shard_map/pallas_call | solution.py:345
  42.1 16.4 %all_to_all.21.rx_ref = bf16[128,3,4,128]{3,2,1,0:T(4,128)(2,1)S(1)} all-to-all(bf16[128,3,4,128]{3,2,1,0:T(4,128)(2,1)S(1)} %shard_map.89), channel_id=1, replica_groups=mesh['facet'=16,'vis'=8] {'facet','vis'}, dimensions={0} | all-to-all | bytes 786432 | tf_op jit(solution)/shard_map/all_to_all | solution.py:366
  58.5 0.0 copy-done
  58.5 0.0 copy-done.2
  58.5 0.0 copy-done.5
  58.5 1.3 %shard_map.90 = (bf16[8,32,512]{2,1,0:T(8,128)(2,1)S(1)}, bf16[1,256,256]{2,1,0:T(8,128)(2,1)}) custom-call(bf16[128,3,4,128]{3,2,1,0:T(4,128)(2,1)S(1)} %all_to_all.21.rx_ref, s32[2,128]{1,0:T(2,128)S(1)} %bitcast.7, f32[16,512]{1,0:T(8,128)S(1)} %copy-done.2, bf16[512,1024]{1,0:T(8,128)(2,1)S(1)} %copy-done), custom_call_target="tpu_custom_call" | custom-call | tf_op jit(solution)/shard_map/pallas_call | solution.py:367
  59.8 10.1 %all_to_all.22 = bf16[8,32,512]{2,1,0:T(8,128)(2,1)S(1)} all-to-all(bf16[8,32,512]{2,1,0:T(8,128)(2,1)S(1)} %get-tuple-element.25), channel_id=1, replica_groups=mesh['facet'=16,'vis'=8] {'vis'}, dimensions={0} | all-to-all | bytes 524288 | tf_op jit(solution)/shard_map/all_to_all | solution.py:383
  69.9 0.9 %bitcast_convert_fusion = f32[256,512]{1,0:T(8,128)} fusion(bf16[8,32,512]{2,1,0:T(8,128)(2,1)S(1)} %all_to_all.22), kind=kLoop, calls=%fused_computation | loop fusion | flops 131072 | bytes 786432 | tf_op jit(solution)/shard_map/convert_element_type | solution.py:384
Async XLA Ops:
  2.4 12.7 %all-to-all-start = ((bf16[8,32,512]{2,1,0:T(8,128)(2,1)}), bf16[8,32,512]{2,1,0:T(8,128)(2,1)S(1)}, u32[]{:S(2)}, u32[]{:S(2)}) async-start(bf16[8,32,512]{2,1,0:T(8,128)(2,1)} %shard_map.86), calls=%async_computation | async-start | bytes 524288 | tf_op jit(solution)/shard_map/all_to_all | solution.py:321
  7.9 0.9 %copy-start.1 = (bf16[1,256,256]{2,1,0:T(8,128)(2,1)S(1)}, bf16[1,256,256]{2,1,0:T(8,128)(2,1)}, u32[]{:S(2)}) copy-start(bf16[1,256,256]{2,1,0:T(8,128)(2,1)} %obs_ref.1) | copy-start | bytes 393220
  8.8 0.7 copy-start.3
  9.5 0.7 copy-start.4
  11.6 46.9 %copy-start = (bf16[512,1024]{1,0:T(8,128)(2,1)S(1)}, bf16[512,1024]{1,0:T(8,128)(2,1)}, u32[]{:S(2)}) copy-start(bf16[512,1024]{1,0:T(8,128)(2,1)} %constant.8.clone.tab_ref) | copy-start | bytes 3145732
  11.6 46.9 %copy-start.2 = (f32[16,512]{1,0:T(8,128)S(1)}, f32[16,512]{1,0:T(8,128)}, u32[]{:S(2)}) copy-start(f32[16,512]{1,0:T(8,128)} %constant.7.clone.tw_ref) | copy-start | bytes 98308
  11.6 46.9 %copy-start.5 = (s32[128,2]{0,1:T(2,128)S(1)}, s32[128,2]{0,1:T(2,128)}, u32[]{:S(2)}) copy-start(s32[128,2]{0,1:T(2,128)} %param.9) | copy-start | bytes 3076
